TPU v7x, 32 devices: a whole 2x2x4 slice. The times are simulated.
32 devices in a mesh: macro: 16 (over z, x, core), vox: 2 (over y).
Axes of the slice: x: 2, y: 2, z: 4, core: 2. Of those that a mesh axis runs over, the one named last changes fastest.
Arguments:
- nodal_disp: float32 [16, 3], P('macro'), may hold values from -6 to 6
- weighted_shape_gradients: float32 [16, 3, 8], P('macro'), may hold values from -2 to 2
- rve_element: int32 [16], replicated, may hold values from 0 to 1, as said below
- connectivity: int32 [2, 8], replicated, may hold values from 0 to 15, as said below
- block_slot: int32 [2, 8, 8], replicated, may hold values from 0 to 11, as said below
- stiffness: float32 [16, 64, 4096], P('macro', 'vox'), may hold values from 0.2 to 1
- yielded_mask: int32 [16, 64, 4096], P('macro', 'vox'), may hold values 0 or 1
Outputs:
- voxel_stress: float32 [16, 6, 64, 4096], P('macro', None, 'vox')
- homogenized_stress: float32 [16, 6], P('macro')
- macro_strain: float32 [16, 6], P('macro')
- internal_node_force: float32 [16, 3], P('macro')
- tangent: float32 [16, 108], P('macro')
Inputs may be any that keep to these rules, and one draw needn't show every extreme that they name: `rve_element`: each element number is named by exactly 8 RVEs. `connectivity`: the elements form a strip of hexahedra: element e and e + 1 share four corner nodes; distinct mesh nodes have distinct numbers. `block_slot`: a node pair gets the same slot wherever it appears; the neighbours of one node get distinct slots.
All inputs are finite; a program needn't handle non-finite values. No bound on the sum of `yielded_mask` on one device may be relied on, other than what follows from the above.
Results may differ from a plain program's by a relative error of at most 0.0003.
Values sent between devices are 32-bit elements; how exact they have to be, the bound alone decides.
No kernel may reach another device: no remote copies, remote signals or barrier semaphores. Data moves between devices by JAX's collectives and lax.ppermute only.
A program may use at most 64 MiB of HBM per device.

v0:
```python
import functools

import jax
import jax.numpy as jnp
from jax import lax
from jax.experimental import pallas as pl
from jax.experimental.pallas import tpu as pltpu
from jax.sharding import PartitionSpec as P

EDGE = 64
SWEEPS = 3
NEIGHBOUR_SLOTS = 12
BLOCK = NEIGHBOUR_SLOTS * 9

lame_base = 1.5
shear_base = 1.0
yield_ratio = 0.2
precond = 1.0 / 42.0
lower_bound = 0.05
upper_bound = 2.0

ROWS = EDGE * EDGE // 128
HALO = 3


def chebyshev_terms(count):
    centre = 0.5 * (upper_bound + lower_bound)
    half_width = 0.5 * (upper_bound - lower_bound)
    ratio_bound = centre / half_width
    rho_prev = 1.0 / ratio_bound
    weights = []
    for number in range(count):
        rho_next = 1.0 / (2.0 * ratio_bound - rho_prev)
        weights.append((rho_next * rho_prev, 2.0 * rho_next / half_width))
        rho_prev = rho_next
    return (centre, weights)


centre, ((keep1, push1), (keep2, push2)) = chebyshev_terms(SWEEPS - 1)
gain1 = push1 * precond
gain2 = push2 * precond


def lanes():
    return lax.broadcasted_iota(jnp.int32, (ROWS, 128), 1)


def swap(x):
    return pltpu.roll(x, 64, 1)


def next_row(y):
    after = jnp.concatenate([y[8:], pltpu.roll(y[:8], 7, 0)], axis=0)
    return jnp.where(lanes() < 64, y, after)


def prev_row(y):
    before = jnp.concatenate([pltpu.roll(y[24:], 1, 0), y[:24]], axis=0)
    return jnp.where(lanes() < 64, before, y)


def next_lane(x, y):
    return pltpu.roll(jnp.where((lanes() & 63) == 0, y, x), 127, 1)


def prev_lane(x, y):
    return pltpu.roll(jnp.where((lanes() & 63) == 63, y, x), 1, 1)


def plane_stress(w, above, lame, shear, strain):
    w0, w1, w2 = w
    n0, n1, n2 = above
    y0, y1, y2 = swap(w0), swap(w1), swap(w2)
    e0 = (n0 - w0) + strain[0]
    e1 = (next_row(y1) - w1) + strain[1]
    e2 = (next_lane(w2, y2) - w2) + strain[2]
    g3 = (next_lane(w1, y1) + next_row(y2)) - (w1 + w2) + strain[3]
    g4 = (next_lane(w0, y0) + n2) - (w0 + w2) + strain[4]
    g5 = (next_row(y0) + n1) - (w0 + w1) + strain[5]
    bulk = lame * (e0 + e1 + e2)
    twice = shear + shear
    return (
        bulk + twice * e0,
        bulk + twice * e1,
        bulk + twice * e2,
        shear * g3,
        shear * g4,
        shear * g5,
    )


def uniform_stress(lame, shear, strain):
    bulk = lame * (strain[0] + strain[1] + strain[2])
    return (
        bulk + shear * (2.0 * strain[0]),
        bulk + shear * (2.0 * strain[1]),
        bulk + shear * (2.0 * strain[2]),
        shear * strain[3],
        shear * strain[4],
        shear * strain[5],
    )


def plane_divergence(stress, below):
    xx, yy, zz, yz, xz, xy = stress
    pxx, pxz, pxy = below
    yyz = swap(yz)
    r0 = (xx - pxx) + (xy - prev_row(swap(xy))) + (xz - prev_lane(xz, swap(xz)))
    r1 = (xy - pxy) + (yy - prev_row(swap(yy))) + (yz - prev_lane(yz, yyz))
    r2 = (xz - pxz) + (yz - prev_row(yyz)) + (zz - prev_lane(zz, swap(zz)))
    return r0, r1, r2


def slab_kernel(
    step,
    gathered,
    rve_element,
    connectivity,
    stiff_ref,
    mask_ref,
    halo_ref,
    stress_ref,
    strain_ref,
    sums_ref,
    lame_v,
    shear_v,
    w1_v,
    w2_v,
    w3_v,
    carry_v,
    out_v,
    sem,
):
    planes = stiff_ref.shape[0] // ROWS
    point = lax.axis_index("macro")
    elem = rve_element[point]

    grads = [[gathered[point, 3 + c * 8 + k] for k in range(8)] for c in range(3)]
    nodes = [connectivity[elem, k] for k in range(8)]
    moves = [[gathered[n, a] for n in nodes] for a in range(3)]

    def dot(c, a):
        total = grads[c][0] * moves[a][0]
        for k in range(1, 8):
            total = total + grads[c][k] * moves[a][k]
        return total

    strain = [
        dot(0, 0),
        dot(1, 1),
        dot(2, 2),
        dot(2, 1) + dot(1, 2),
        dot(2, 0) + dot(0, 2),
        dot(1, 0) + dot(0, 1),
    ]
    for c in range(6):
        strain_ref[0, c] = strain[c]

    def native(p8, s, q):
        return pl.ds(p8 * (8 * ROWS) + s + 8 * q, 8, stride=ROWS)

    def load_material(g, acc):
        acc_s, acc_m = acc
        for s in range(8):
            stiff = jnp.concatenate([stiff_ref[native(g, s, q), :] for q in range(4)], axis=0)
            mask = jnp.concatenate([mask_ref[native(g, s, q), :] for q in range(4)], axis=0)
            shear = stiff * jnp.where(mask == 1, shear_base * yield_ratio, shear_base)
            lame = lame_base * stiff
            lame_v[g * 8 + s + HALO] = lame
            shear_v[g * 8 + s + HALO] = shear
            acc_s = acc_s + lame
            acc_m = acc_m + shear
        return acc_s, acc_m

    zero = jnp.zeros((ROWS, 128), jnp.float32)
    lame_sum, shear_sum = lax.fori_loop(0, planes // 8, load_material, (zero, zero))
    for side in range(2):
        for h in range(HALO):
            at = h if side == 0 else HALO + planes + h
            parts = []
            for f in range(2):
                base = ((side * 2 + f) * HALO + h) * ROWS
                parts.append(
                    jnp.concatenate(
                        [halo_ref[pl.ds(base + q, 8, stride=4), :] for q in range(4)], axis=0
                    )
                )
            lame_v[at] = lame_base * parts[0]
            shear_v[at] = parts[1]

    scale1 = gain1 * gain2 * precond / centre
    strain1 = [scale1 * e for e in strain]

    def put_carry(stress):
        carry_v[0] = stress[0]
        carry_v[1] = stress[4]
        carry_v[2] = stress[5]

    def get_carry():
        return carry_v[0], carry_v[1], carry_v[2]

    def pick(stress):
        return stress[0], stress[4], stress[5]

    put_carry(uniform_stress(lame_v[0], shear_v[0], strain1))

    def sweep1(t, _):
        below = get_carry()
        for u in range(step):
            at = t * step + 1 + u
            stress = uniform_stress(lame_v[at], shear_v[at], strain1)
            r = plane_divergence(stress, below)
            for c in range(3):
                w1_v[c, at] = r[c]
            below = pick(stress)
        put_carry(stress)
        return 0

    lax.fori_loop(0, pl.cdiv(planes + 5, step), sweep1, 0)

    def load3(ref, at):
        return ref[0, at], ref[1, at], ref[2, at]

    strain2 = [gain1 * gain2 * e for e in strain]
    ratio1 = (1.0 + keep1) / gain1
    put_carry(
        plane_stress(load3(w1_v, 1), load3(w1_v, 2), lame_v[1], shear_v[1], strain2)
    )

    def sweep2(t, _):
        below = get_carry()
        w = load3(w1_v, t * step + 2)
        for u in range(step):
            at = t * step + 2 + u
            above = load3(w1_v, at + 1)
            stress = plane_stress(w, above, lame_v[at], shear_v[at], strain2)
            r = plane_divergence(stress, below)
            for c in range(3):
                w2_v[c, at] = ratio1 * w[c] + r[c]
            below = pick(stress)
            w = above
        put_carry(stress)
        return 0

    lax.fori_loop(0, pl.cdiv(planes + 3, step), sweep2, 0)

    strain3 = [gain2 * e for e in strain]
    ratio2 = (1.0 + keep2) / gain2
    ratio3 = keep2 / (gain1 * gain2)
    put_carry(
        plane_stress(load3(w2_v, 2), load3(w2_v, 3), lame_v[2], shear_v[2], strain3)
    )

    def sweep3(t, _):
        below = get_carry()
        w = load3(w2_v, t * step + 3)
        for u in range(step):
            at = t * step + 3 + u
            above = load3(w2_v, at + 1)
            stress = plane_stress(w, above, lame_v[at], shear_v[at], strain3)
            r = plane_divergence(stress, below)
            for c in range(3):
                w3_v[c, at] = ratio2 * w[c] - ratio3 * w1_v[c, at] + r[c]
            below = pick(stress)
            w = above
        put_carry(stress)
        return 0

    lax.fori_loop(0, pl.cdiv(planes + 1, step), sweep3, 0)

    def put_out(g):
        span = pl.ds(pl.multiple_of(g * (8 * ROWS), 8 * ROWS), 8 * ROWS)
        return pltpu.make_async_copy(out_v.at[:, span, :], stress_ref.at[:, span, :], sem)

    def final(g, acc):
        acc = list(acc)
        w = load3(w3_v, g * 8 + HALO)
        for s in range(8):
            at = g * 8 + s + HALO
            above = load3(w3_v, at + 1)
            stress = plane_stress(w, above, lame_v[at], shear_v[at], strain)
            for c in range(6):
                acc[c] = acc[c] + (
                    (stress[c][:8] + stress[c][8:16]) + (stress[c][16:24] + stress[c][24:])
                )
                for q in range(4):
                    out_v[c, native(g, s, q), :] = stress[c][8 * q : 8 * q + 8]
            w = above
        put_out(g).start()
        return tuple(acc)

    small = jnp.zeros((8, 128), jnp.float32)
    acc = lax.fori_loop(0, planes // 8, final, (small,) * 6)

    totals = list(acc)
    for big in (lame_sum, shear_sum):
        totals.append((big[:8] + big[8:16]) + (big[16:24] + big[24:]))
    at_lane = lax.broadcasted_iota(jnp.int32, sums_ref.shape, 1)
    row = jnp.zeros(sums_ref.shape, jnp.float32)
    for c in range(8):
        row = jnp.where(at_lane == c, jnp.sum(totals[c], axis=(0, 1), keepdims=True), row)
    sums_ref[...] = row

    def drain(g, _):
        put_out(g).wait()
        return 0

    lax.fori_loop(0, planes // 8, drain, 0)


def node_kernel(
    sums_ref,
    gathered_ref,
    elem_ref,
    connectivity,
    block_slot,
    hom_ref,
    force_ref,
    tangent_ref,
):
    points = gathered_ref.shape[0]
    elems = connectivity.shape[0]
    own = lax.axis_index("macro")
    scale = 1.0 / float(EDGE * EDGE * EDGE)
    means = sums_ref[0]
    for v in range(1, sums_ref.shape[0]):
        means = means + sums_ref[v]
    means = means * scale

    def col(x, c):
        return x[:, c : c + 1]

    place = lax.broadcasted_iota(jnp.int32, means.shape, 0)
    hom_ref[...] = jnp.sum(jnp.where(place == own, means, 0.0), axis=0, keepdims=True)[:, :6]

    grads = gathered_ref[...]
    elem = elem_ref[...]
    corner = jnp.full(elem.shape, -1, jnp.int32)
    slots = [jnp.full(elem.shape, -1, jnp.int32) for l in range(8)]
    for e in range(elems):
        at = jnp.int32(-1)
        for k in range(8):
            at = jnp.where(connectivity[e, k] == own, k, at)
        here = elem == e
        corner = jnp.where(here, at, corner)
        safe = jnp.maximum(at, 0)
        for l in range(8):
            slots[l] = jnp.where(here, block_slot[e, safe * 8 + l], slots[l])
    lane = lax.broadcasted_iota(jnp.int32, grads.shape, 1)
    mine = []
    for c in range(3):
        hit = (lane == corner + (3 + 8 * c)) & (corner >= 0)
        mine.append(jnp.sum(jnp.where(hit, grads, 0.0), axis=1, keepdims=True))
    m0, m1, m2 = mine
    sxx, syy, szz, syz, sxz, sxy, lame, shear = [col(means, c) for c in range(8)]
    pull = [
        sxx * m0 + sxy * m1 + sxz * m2,
        sxy * m0 + syy * m1 + syz * m2,
        sxz * m0 + syz * m1 + szz * m2,
    ]
    wide = lax.broadcasted_iota(jnp.int32, (points, BLOCK), 1)
    slot_of = wide // 9
    inner = wide - 9 * slot_of
    a_of = inner // 3
    b_of = inner - 3 * a_of

    def by(which, x, y, z):
        return jnp.where(which == 0, x, jnp.where(which == 1, y, z))

    tri = lax.broadcasted_iota(jnp.int32, (points, 3), 1)
    force_ref[...] = jnp.sum(by(tri, *pull), axis=0, keepdims=True)

    lame_a = lame * by(a_of, m0, m1, m2)
    shear_b = shear * by(b_of, m0, m1, m2)
    diagonal = a_of == b_of
    total = jnp.zeros((points, BLOCK), jnp.float32)
    for l in range(8):
        g0, g1, g2 = [col(grads, 3 + 8 * c + l) for c in range(3)]
        dots = shear * (m0 * g0 + m1 * g1 + m2 * g2)
        block = lame_a * by(b_of, g0, g1, g2) + shear_b * by(a_of, g0, g1, g2)
        block = block + jnp.where(diagonal, dots, 0.0)
        total = total + jnp.where(slot_of == slots[l], block, 0.0)
    tangent_ref[...] = jnp.sum(total, axis=0, keepdims=True)


def to_all(x, axes, count):
    return lax.all_to_all(x, axes, split_axis=0, concat_axis=0, tiled=True)


def on_device(
    nodal_disp,
    weighted_shape_gradients,
    rve_element,
    connectivity,
    block_slot,
    stiffness,
    yielded_mask,
):
    rve_count, planes, plane_size = stiffness.shape
    macro_size = lax.axis_size("macro")
    vox_size = lax.axis_size("vox")
    assert rve_count == 1 and nodal_disp.shape[0] == 1
    assert planes % 8 == 0 and plane_size == EDGE * EDGE

    def rim(first):
        stiff = lax.slice_in_dim(stiffness[0], first, first + HALO, axis=0)
        mask = lax.slice_in_dim(yielded_mask[0], first, first + HALO, axis=0)
        shear = shear_base * stiff * jnp.where(mask == 1, yield_ratio, 1.0)
        return jnp.stack([stiff, shear]).reshape(2 * HALO * ROWS, 128)

    upper, lower = rim(planes - HALO), rim(0)
    if vox_size == 2:
        both = jnp.concatenate([upper, lower], axis=0)
        halo = lax.ppermute(both, "vox", [(0, 1), (1, 0)])
    else:
        forward = [(i, (i + 1) % vox_size) for i in range(vox_size)]
        backward = [(t, s) for s, t in forward]
        halo = jnp.concatenate(
            [lax.ppermute(upper, "vox", forward), lax.ppermute(lower, "vox", backward)], axis=0
        )

    packet = jnp.concatenate(
        [
            nodal_disp.reshape(1, 3),
            weighted_shape_gradients.reshape(1, 24),
            jnp.zeros((1, 5), jnp.float32),
        ],
        axis=1,
    )
    gathered = to_all(jnp.broadcast_to(packet, (macro_size, 32)), "macro", macro_size)

    def flat(field):
        parted = field.reshape(planes // 8, 8, ROWS, 128)
        return parted.transpose(0, 2, 1, 3).reshape(planes * ROWS, 128)

    smem = pl.BlockSpec(memory_space=pltpu.SMEM)
    vmem = pl.BlockSpec(memory_space=pltpu.VMEM)
    everywhere = macro_size * vox_size
    step = 4
    depth = planes + 2 * HALO + step
    field = pltpu.VMEM((3, depth, ROWS, 128), jnp.float32)
    stress, strain, sums = pl.pallas_call(
        functools.partial(slab_kernel, step),
        out_shape=(
            jax.ShapeDtypeStruct((6, planes * ROWS, 128), jnp.float32),
            jax.ShapeDtypeStruct((1, 6), jnp.float32),
            jax.ShapeDtypeStruct((everywhere, 8), jnp.float32),
        ),
        in_specs=[smem, smem, smem, vmem, vmem, vmem],
        out_specs=(pl.BlockSpec(memory_space=pl.ANY), smem, vmem),
        scratch_shapes=[
            pltpu.VMEM((depth, ROWS, 128), jnp.float32),
            pltpu.VMEM((depth, ROWS, 128), jnp.float32),
            field,
            field,
            field,
            pltpu.VMEM((3, ROWS, 128), jnp.float32),
            pltpu.VMEM((6, planes * ROWS, 128), jnp.float32),
            pltpu.SemaphoreType.DMA,
        ],
        compiler_params=pltpu.CompilerParams(vmem_limit_bytes=24 * 1024 * 1024),
        cost_estimate=pl.CostEstimate(
            flops=300 * planes * plane_size,
            bytes_accessed=32 * planes * plane_size,
            transcendentals=0,
        ),
        name="slab",
    )(gathered, rve_element, connectivity, flat(stiffness), flat(yielded_mask), halo)

    voxel_stress = (
        stress.reshape(6, planes // 8, ROWS, 8, 128)
        .transpose(0, 1, 3, 2, 4)
        .reshape(1, 6, planes, plane_size)
    )

    all_sums = to_all(sums, ("vox", "macro"), everywhere).reshape(vox_size, macro_size, 8)
    homogenized, internal_node_force, tangent = pl.pallas_call(
        node_kernel,
        out_shape=(
            jax.ShapeDtypeStruct((1, 6), jnp.float32),
            jax.ShapeDtypeStruct((1, 3), jnp.float32),
            jax.ShapeDtypeStruct((1, BLOCK), jnp.float32),
        ),
        in_specs=[vmem, vmem, vmem, smem, smem],
        out_specs=(vmem, vmem, vmem),
        name="nodes",
    )(
        all_sums,
        gathered,
        rve_element.reshape(-1, 1),
        connectivity,
        block_slot.reshape(block_slot.shape[0], 64),
    )
    return (voxel_stress, homogenized, strain, internal_node_force, tangent)


def solution(mesh):
    in_specs = (
        P("macro", None),
        P("macro", None, None),
        P(),
        P(),
        P(),
        P("macro", "vox", None),
        P("macro", "vox", None),
    )
    out_specs = (
        P("macro", None, "vox", None),
        P("macro", None),
        P("macro", None),
        P("macro", None),
        P("macro", None),
    )
    return jax.shard_map(
        on_device, mesh=mesh, in_specs=in_specs, out_specs=out_specs, check_vma=False
    )
```

profile of v0, /device:TPU:0, one launch (start us, length us, event | category | flops | bytes accessed | tf_op | source)
XLA Modules:
  0.0 51.1 jit_solution(11035897475089309532)
XLA Ops:
  0.6 0.0 copy-start.5
  0.6 0.0 copy-start.7
  0.7 1.2 %select_multiply_fusion.1 = (f32[1,3,4096]{2,1,0:T(4,128)S(1)}, f32[1,3,4096]{2,1,0:T(4,128)S(1)}, f32[1,3,4096]{2,1,0:T(4,128)S(1)}, f32[1,3,4096]{2,1,0:T(4,128)S(1)}) fusion(s32[1,32,4096]{2,1,0:T(8,128)} %param.13, f32[1,32,4096]{2,1,0:T(8,128)} %param.12), kind=kLoop, calls=%fused_computation.5 | loop fusion | flops 73728 | bytes 393216 | tf_op jit(solution)/shard_map/mul | solution.py:408
  1.8 0.1 pad_maximum_fusion.1
  1.9 0.1 reshape.66
  2.0 0.1 reshape.67
  2.1 3.0 %collective-permute-start = (f32[384,128]{1,0:T(8,128)S(1)}, f32[384,128]{1,0:T(8,128)S(1)}, u32[]{:S(2)}, u32[]{:S(2)}) collective-permute-start(f32[384,128]{1,0:T(8,128)S(1)} %pad_maximum_fusion), channel_id=1, source_target_pairs={{0,1},{1,0},{2,3},{3,2},{4,5},{5,4},{6,7},{7,6},{8,9},{9,8},{10,11... | collective-permute-start | bytes 589832 | tf_op jit(solution)/shard_map/ppermute | solution.py:414
  5.1 0.7 %reduce = f32[3,8]{1,0:T(4,128)S(1)} reduce(f32[1,3,8]{2,0,1:T(1,128)} %param.8, f32[]{:T(128)} %constant.12), dimensions={0}, to_apply=%param.8.reduce_sub_computation | reduce | bytes 196 | tf_op args[1]
  5.8 0.1 reshape.61
  5.9 0.7 %fusion = f32[32]{0:T(128)S(1)} fusion(f32[5]{0:T(128)S(1)} %broadcast.16, f32[1,24]{1,0:T(1,128)S(1)} %reshape.61, f32[1,3]{1,0:T(1,128)} %param.7), kind=kLoop, calls=%fused_computation.8 | loop fusion | flops 64 | bytes 256 | tf_op jit(solution)/shard_map/concatenate | solution.py:422
  6.6 12.1 %all_to_all.17 = f32[16,1,32]{2,1,0:T(1,128)S(1)} all-to-all(f32[16,1,32]{2,1,0:T(1,128)S(1)} %broadcast_in_dim.15), channel_id=1, replica_groups=mesh['macro'=16,'vox'=2] {'macro'}, dimensions={0} | all-to-all | bytes 4096 | tf_op jit(solution)/shard_map/all_to_all | solution.py:387
  18.8 0.0 copy-start.2
  18.8 0.0 collective-permute-done.halo_ref
  18.8 0.0 copy-start
  18.8 1.0 %copy-done = f32[1,32,4096]{2,1,0:T(8,128)S(1)} copy-done((f32[1,32,4096]{2,1,0:T(8,128)S(1)}, f32[1,32,4096]{2,1,0:T(8,128)}, u32[]{:S(2)}) %copy-start) | copy-done | bytes 524312
  19.8 0.0 copy-start.1
  19.8 1.0 %copy-done.1 = s32[1,32,4096]{2,1,0:T(8,128)S(1)} copy-done((s32[1,32,4096]{2,1,0:T(8,128)S(1)}, s32[1,32,4096]{2,1,0:T(8,128)}, u32[]{:S(2)}) %copy-start.1) | copy-done | bytes 524312
  20.8 0.0 copy-start.3
  20.8 0.7 %copy-done.3 = s32[2,8]{1,0:T(2,128)S(1)} copy-done((s32[2,8]{1,0:T(2,128)S(1)}, s32[2,8]{1,0:T(2,128)}, u32[]{:S(2)}) %copy-start.3) | copy-done | bytes 88
  21.5 0.0 copy-start.4
  21.5 0.7 %copy-done.4 = s32[16]{0:T(128)S(1)} copy-done((s32[16]{0:T(128)S(1)}, s32[16]{0:T(128)}, u32[]{:S(2)}) %copy-start.4) | copy-done | bytes 88
  22.2 16.9 %slab.1 = (f32[6,1024,128]{2,1,0:T(8,128)}, f32[1,6]{1,0:T(1,128)}, f32[32,8]{1,0:T(8,128)}) custom-call(f32[16,32]{1,0:T(8,128)S(1)} %bitcast.29, s32[16]{0:T(128)S(1)} %copy-done.4, s32[2,8]{1,0:T(2,128)S(1)} %copy-done.3, f32[1024,128]{1,0:T(8,128)S(1)} %bitcast.27, s32[1024,128]{1,0:T(8,128)S(1)} %bitcast.28, f32[384,128]{1,0:T(8,128)S(1)} %collective-permute-done.halo_ref), custom_call_target="tpu_custom_call" | custom-call | flops 39321600 | bytes 4194304 | tf_op jit(solution)/shard_map/slab/pallas_call | solution.py:442
  39.1 2.5 %all-to-all-start.1 = ((f32[32,1,8]{2,1,0:T(1,128)}), f32[32,1,8]{2,1,0:T(1,128)S(1)}, u32[]{:S(2)}, u32[]{:S(2)}) async-start(f32[32,1,8]{2,1,0:T(1,128)} %bitcast.12), calls=%async_computation.1 | async-start | bytes 32768 | tf_op jit(solution)/shard_map/all_to_all | solution.py:387
  41.6 0.0 copy-done.5
  41.6 0.7 %copy.14.elem_ref = s32[16,1]{1,0:T(8,128)} copy(s32[16,1]{0,1:T(1,128)S(1)} %bitcast.31) | data formatting | bytes 128 | tf_op jit(solution)/shard_map/reshape | solution.py:490
  42.3 0.0 copy-done.7
  42.3 0.7 %reshape.72.block_slot = s32[2,64]{1,0:T(2,128)} reshape(s32[2,8,8]{2,1,0:T(8,128)S(1)} %copy-done.7) | data formatting | bytes 1024 | tf_op jit(solution)/shard_map/reshape | solution.py:492
  42.9 5.8 %all-to-all-done.1 = f32[32,1,8]{2,1,0:T(1,128)S(1)} async-done(((f32[32,1,8]{2,1,0:T(1,128)}), f32[32,1,8]{2,1,0:T(1,128)S(1)}, u32[]{:S(2)}, u32[]{:S(2)}) %all-to-all-start.1) | async-done | bytes 1056 | tf_op jit(solution)/shard_map/all_to_all | solution.py:387
  48.7 0.0 copy-start.6
  48.8 0.0 copy-done.2
  48.8 0.6 %copy-done.6 = f32[32,1,8]{2,1,0:T(1,128)} copy-done((f32[32,1,8]{2,1,0:T(1,128)}, f32[32,1,8]{2,1,0:T(1,128)S(1)}, u32[]{:S(2)}) %copy-start.6) | copy-done | bytes 1048
  49.3 1.8 %nodes.1 = (f32[1,6]{1,0:T(1,128)}, f32[1,3]{1,0:T(1,128)}, f32[1,108]{1,0:T(1,128)}) custom-call(f32[2,16,8]{2,1,0:T(8,128)} %bitcast.32, f32[16,32]{1,0:T(8,128)} %bitcast.30, s32[16,1]{1,0:T(8,128)} %copy.14.elem_ref, s32[2,8]{1,0:T(2,128)} %connectivity.3, s32[2,64]{1,0:T(2,128)} %reshape.72.block_slot), custom_call_target="tpu_custom_call" | custom-call | tf_op jit(solution)/shard_map/nodes/pallas_call | solution.py:477
  (3 shorter events, 0.0 us)
Async XLA Ops:
  0.6 41.0 %copy-start.5 = (s32[16]{0:T(128)S(1)}, s32[16]{0:T(128)}, u32[]{:S(2)}) copy-start(s32[16]{0:T(128)} %rve_element.1) | copy-start | bytes 196
  0.6 41.6 %copy-start.7 = (s32[2,8,8]{2,1,0:T(8,128)S(1)}, s32[2,8,8]{2,1,0:T(8,128)}, u32[]{:S(2)}) copy-start(s32[2,8,8]{2,1,0:T(8,128)} %param.11) | copy-start | bytes 1540
  2.1 16.7 %collective-permute-start = (f32[384,128]{1,0:T(8,128)S(1)}, f32[384,128]{1,0:T(8,128)S(1)}, u32[]{:S(2)}, u32[]{:S(2)}) collective-permute-start(f32[384,128]{1,0:T(8,128)S(1)} %pad_maximum_fusion), channel_id=1, source_target_pairs={{0,1},{1,0},{2,3},{3,2},{4,5},{5,4},{6,7},{7,6},{8,9},{9,8},{10,11... | collective-permute-start | bytes 589832 | tf_op jit(solution)/shard_map/ppermute | solution.py:414
  18.8 30.0 %copy-start.2 = (f32[16,1,32]{2,1,0:T(1,128)}, f32[16,1,32]{2,1,0:T(1,128)S(1)}, u32[]{:S(2)}) copy-start(f32[16,1,32]{2,1,0:T(1,128)S(1)} %all_to_all.17) | copy-start | bytes 6148
  18.8 1.0 %copy-start = (f32[1,32,4096]{2,1,0:T(8,128)S(1)}, f32[1,32,4096]{2,1,0:T(8,128)}, u32[]{:S(2)}) copy-start(f32[1,32,4096]{2,1,0:T(8,128)} %param.12) | copy-start | bytes 1572868
  19.8 1.0 %copy-start.1 = (s32[1,32,4096]{2,1,0:T(8,128)S(1)}, s32[1,32,4096]{2,1,0:T(8,128)}, u32[]{:S(2)}) copy-start(s32[1,32,4096]{2,1,0:T(8,128)} %param.13) | copy-start | bytes 1572868
  20.8 0.7 %copy-start.3 = (s32[2,8]{1,0:T(2,128)S(1)}, s32[2,8]{1,0:T(2,128)}, u32[]{:S(2)}) copy-start(s32[2,8]{1,0:T(2,128)} %connectivity.3) | copy-start | bytes 196
  21.5 0.7 %copy-start.4 = (s32[16]{0:T(128)S(1)}, s32[16]{0:T(128)}, u32[]{:S(2)}) copy-start(s32[16]{0:T(128)} %rve_element.1) | copy-start | bytes 196
  39.1 9.7 %all-to-all-start.1 = ((f32[32,1,8]{2,1,0:T(1,128)}), f32[32,1,8]{2,1,0:T(1,128)S(1)}, u32[]{:S(2)}, u32[]{:S(2)}) async-start(f32[32,1,8]{2,1,0:T(1,128)} %bitcast.12), calls=%async_computation.1 | async-start | bytes 32768 | tf_op jit(solution)/shard_map/all_to_all | solution.py:387
  48.7 0.6 %copy-start.6 = (f32[32,1,8]{2,1,0:T(1,128)}, f32[32,1,8]{2,1,0:T(1,128)S(1)}, u32[]{:S(2)}) copy-start(f32[32,1,8]{2,1,0:T(1,128)S(1)} %all-to-all-done.1) | copy-start | bytes 3076
where the time goes:
time: 51.5 us; the launch traced here: 51.1 us
  Pallas kernels  18.7 us (36%)
  blocking collectives  12.1 us (23%)
  waiting for transfers between devices  5.81 us (11%)
  local copies, waits for them, and re-layouts  5.6 us (11%)
  starting transfers between devices  5.55 us (11%)
  other arithmetic  2.68 us (5%)
  between operations  0.72 us (1%)
    pallas_call x1, Pallas kernels, on_device(): pl.pallas_call(functools.partial(slab_kernel, step), out_shape=(jax.Shape...  16.9 us
    all_to_all x1, blocking collectives, to_all(): return lax.all_to_all(x, axes, split_axis=0, concat_axis=0, tiled=True)  12.1 us
    all_to_all x1, waiting for transfers between devices, to_all(): return lax.all_to_all(x, axes, split_axis=0, concat_axis=0, tiled=True)  5.81 us
    unnamed x16, local copies, waits for them, and re-layouts  4.03 us
    ppermute x1, starting transfers between devices, on_device(): halo = lax.ppermute(both, 'vox', [(0, 1), (1, 0)])  3.03 us
    all_to_all x1, starting transfers between devices, to_all(): return lax.all_to_all(x, axes, split_axis=0, concat_axis=0, tiled=True)  2.52 us
    pallas_call x1, Pallas kernels, on_device(): pl.pallas_call(node_kernel, out_shape=(jax.ShapeDtypeStruct((1, 6), jnp.f...  1.79 us
    mul x1, other arithmetic, rim(): shear = shear_base * stiff * jnp.where(mask == 1, yield_ratio, 1.0)  1.17 us
  transfers between devices with their start and end apart: 2, of which 1 were waited for; matrix products, arithmetic and copies ran while one was open for 6% of the time, Pallas kernels for 0%

commit v1 on v0

v1 whole, which is shorter than its diff:
```python
import jax
import jax.numpy as jnp
from jax import lax
from jax.experimental import pallas as pl
from jax.experimental.pallas import tpu as pltpu
from jax.sharding import PartitionSpec as P

EDGE = 64
SWEEPS = 3
NEIGHBOUR_SLOTS = 12
BLOCK = NEIGHBOUR_SLOTS * 9

lame_base = 1.5
shear_base = 1.0
yield_ratio = 0.2
precond = 1.0 / 42.0
lower_bound = 0.05
upper_bound = 2.0

ROWS = EDGE * EDGE // 128
HALO = 3


def chebyshev_terms(count):
    centre = 0.5 * (upper_bound + lower_bound)
    half_width = 0.5 * (upper_bound - lower_bound)
    ratio_bound = centre / half_width
    rho_prev = 1.0 / ratio_bound
    weights = []
    for number in range(count):
        rho_next = 1.0 / (2.0 * ratio_bound - rho_prev)
        weights.append((rho_next * rho_prev, 2.0 * rho_next / half_width))
        rho_prev = rho_next
    return (centre, weights)


centre, ((keep1, push1), (keep2, push2)) = chebyshev_terms(SWEEPS - 1)
gain1 = push1 * precond
gain2 = push2 * precond

def steps_for(count, most):
    return min(range(1, most + 1), key=lambda s: (-(-count // s) * s + 2 * -(-count // s), -s))


class Ops:
    def __init__(self):
        lane = lax.broadcasted_iota(jnp.int32, (8, 128), 1)
        self.low = lane < 64
        self.first = (lane & 63) == 0
        self.last = (lane & 63) == 63

    def next_row(self, x):
        y = [pltpu.roll(v, 64, 1) for v in x]
        after = y[1:] + [pltpu.roll(y[0], 7, 0)]
        return [jnp.where(self.low, here, there) for here, there in zip(y, after)]

    def prev_row(self, x):
        y = [pltpu.roll(v, 64, 1) for v in x]
        before = [pltpu.roll(y[3], 1, 0)] + y[:3]
        return [jnp.where(self.low, there, here) for here, there in zip(y, before)]

    def next_lane(self, x):
        return [jnp.where(self.last, pltpu.roll(v, 63, 1), pltpu.roll(v, 127, 1)) for v in x]

    def prev_lane(self, x):
        return [jnp.where(self.first, pltpu.roll(v, 65, 1), pltpu.roll(v, 1, 1)) for v in x]

    def stress(self, w, above, lame, shear, strain):
        row0, row1, row2 = [self.next_row(v) for v in w]
        lane0, lane1, lane2 = [self.next_lane(v) for v in w]
        out = [[] for c in range(6)]
        for q in range(4):
            w0, w1, w2 = [v[q] for v in w]
            n0, n1, n2 = [v[q] for v in above]
            e0 = (n0 - w0) + strain[0]
            e1 = (row1[q] - w1) + strain[1]
            e2 = (lane2[q] - w2) + strain[2]
            g3 = (lane1[q] + row2[q]) - (w1 + w2) + strain[3]
            g4 = (lane0[q] + n2) - (w0 + w2) + strain[4]
            g5 = (row0[q] + n1) - (w0 + w1) + strain[5]
            bulk = lame[q] * (e0 + e1 + e2)
            twice = shear[q] + shear[q]
            out[0].append(bulk + twice * e0)
            out[1].append(bulk + twice * e1)
            out[2].append(bulk + twice * e2)
            out[3].append(shear[q] * g3)
            out[4].append(shear[q] * g4)
            out[5].append(shear[q] * g5)
        return out

    def uniform(self, lame, shear, strain):
        trace = strain[0] + strain[1] + strain[2]
        twice = [2.0 * strain[c] for c in range(3)]
        out = [[] for c in range(6)]
        for q in range(4):
            bulk = lame[q] * trace
            for c in range(3):
                out[c].append(bulk + shear[q] * twice[c])
            for c in range(3, 6):
                out[c].append(shear[q] * strain[c])
        return out

    def divergence(self, stress, below):
        xx, yy, zz, yz, xz, xy = stress
        pxx, pxz, pxy = below
        xy_row, yy_row, yz_row = [self.prev_row(v) for v in (xy, yy, yz)]
        xz_lane, yz_lane, zz_lane = [self.prev_lane(v) for v in (xz, yz, zz)]
        r0 = [
            (xx[q] - pxx[q]) + (xy[q] - xy_row[q]) + (xz[q] - xz_lane[q]) for q in range(4)
        ]
        r1 = [
            (xy[q] - pxy[q]) + (yy[q] - yy_row[q]) + (yz[q] - yz_lane[q]) for q in range(4)
        ]
        r2 = [
            (xz[q] - pxz[q]) + (yz[q] - yz_row[q]) + (zz[q] - zz_lane[q]) for q in range(4)
        ]
        return r0, r1, r2


def get(ref, *at):
    return [ref[(*at, pl.ds(8 * q, 8), slice(None))] for q in range(4)]


def put(ref, x, *at):
    for q in range(4):
        ref[(*at, pl.ds(8 * q, 8), slice(None))] = x[q]


def native(group, s, q):
    return pl.ds(group * (8 * ROWS) + s + 8 * q, 8, stride=ROWS)


def fold(x):
    return (x[0] + x[1]) + (x[2] + x[3])


def total(x):
    return jnp.sum(x, axis=(0, 1), keepdims=True)


def corner_columns(grads):
    corner = lax.broadcasted_iota(jnp.int32, (8, 128), 0)
    columns = []
    for c in range(3):
        column = jnp.full((8, 128), grads[c, 0], jnp.float32)
        for k in range(1, 8):
            column = jnp.where(corner == k, grads[c, k], column)
        columns.append(column)
    return columns


def material_kernel(
    grads,
    rve_element,
    block_slot,
    stiff_ref,
    mask_ref,
    halo_ref,
    lame_ref,
    shear_ref,
    rows_ref,
):
    planes = stiff_ref.shape[0] // ROWS
    elem = rve_element[lax.axis_index("macro")]

    def load(g, acc):
        acc_l, acc_m = acc
        for s in range(8):
            lame, shear = [], []
            for q in range(4):
                stiff = stiff_ref[native(g, s, q), :]
                mask = mask_ref[native(g, s, q), :]
                lame.append(lame_base * stiff)
                shear.append(
                    stiff * jnp.where(mask == 1, shear_base * yield_ratio, shear_base)
                )
            put(lame_ref, lame, g * 8 + s + HALO)
            put(shear_ref, shear, g * 8 + s + HALO)
            acc_l = acc_l + fold(lame)
            acc_m = acc_m + fold(shear)
        return acc_l, acc_m

    zero = jnp.zeros((8, 128), jnp.float32)
    acc_l, acc_m = lax.fori_loop(0, planes // 8, load, (zero, zero))
    for side in range(2):
        for h in range(HALO):
            at = h if side == 0 else HALO + planes + h
            parts = []
            for f in range(2):
                base = ((side * 2 + f) * HALO + h) * ROWS
                parts.append([halo_ref[pl.ds(base + q, 8, stride=4), :] for q in range(4)])
            put(lame_ref, [lame_base * v for v in parts[0]], at)
            put(shear_ref, parts[1], at)

    scale = 1.0 / float(EDGE * EDGE * EDGE)
    lame, shear = total(acc_l) * scale, total(acc_m) * scale
    mine = corner_columns(grads)
    corner = lax.broadcasted_iota(jnp.int32, (8, 128), 0)
    lane = lax.broadcasted_iota(jnp.int32, (8, 128), 1)
    slot_of = jnp.zeros((8, 128), jnp.int32)
    for s in range(1, NEIGHBOUR_SLOTS + 1):
        slot_of = slot_of + jnp.where(lane >= 9 * s, 1, 0)
    inner = lane - 9 * slot_of
    a_of = jnp.where(inner >= 3, 1, 0) + jnp.where(inner >= 6, 1, 0)
    b_of = inner - 3 * a_of

    def by(which, x, y, z):
        return jnp.where(which == 0, x, jnp.where(which == 1, y, z))

    lame_a = lame * by(a_of, *mine)
    shear_b = shear * by(b_of, *mine)
    diagonal = jnp.where(a_of == b_of, shear, 0.0)
    rows = jnp.zeros((8, 128), jnp.float32)
    for l in range(8):
        other = [grads[c, l] for c in range(3)]
        dots = mine[0] * other[0] + mine[1] * other[1] + mine[2] * other[2]
        block = lame_a * by(b_of, *other) + shear_b * by(a_of, *other) + diagonal * dots
        slot = jnp.full((8, 128), block_slot[elem, 0, l], jnp.int32)
        for k in range(1, 8):
            slot = jnp.where(corner == k, block_slot[elem, k, l], slot)
        rows = rows + jnp.where(slot_of == slot, block, 0.0)
    rows_ref[...] = rows


FORCE = BLOCK
SUMS = BLOCK + 4


def slab_kernel(
    grads,
    rve_element,
    connectivity,
    gathered,
    lame_v,
    shear_v,
    rows_ref,
    stress_ref,
    strain_ref,
    packet_ref,
    w1_v,
    w2_v,
    w3_v,
    carry_v,
    out_v,
    sem,
):
    planes = out_v.shape[1] // ROWS
    point = lax.axis_index("macro")
    elem = rve_element[point]
    ops = Ops()

    nodes = [connectivity[elem, k] for k in range(8)]
    moves = [[gathered[n ^ point, a] for n in nodes] for a in range(3)]

    def dot(c, a):
        result = grads[c, 0] * moves[a][0]
        for k in range(1, 8):
            result = result + grads[c, k] * moves[a][k]
        return result

    strain = [
        dot(0, 0),
        dot(1, 1),
        dot(2, 2),
        dot(2, 1) + dot(1, 2),
        dot(2, 0) + dot(0, 2),
        dot(1, 0) + dot(0, 1),
    ]
    for c in range(6):
        strain_ref[0, c] = strain[c]

    def material(at):
        return get(lame_v, at), get(shear_v, at)

    def load3(ref, at):
        return [get(ref, c, at) for c in range(3)]

    def pick(stress):
        return stress[0], stress[4], stress[5]

    def put_carry(stress):
        for c, x in enumerate(pick(stress)):
            put(carry_v, x, c)

    def get_carry():
        return [get(carry_v, c) for c in range(3)]

    scale1 = gain1 * gain2 * precond / centre
    strain1 = [scale1 * e for e in strain]
    put_carry(ops.uniform(*material(0), strain1))
    step1 = steps_for(planes + 5, 12)

    def sweep1(t, _):
        below = get_carry()
        for u in range(step1):
            at = t * step1 + 1 + u
            stress = ops.uniform(*material(at), strain1)
            r = ops.divergence(stress, below)
            for c in range(3):
                put(w1_v, r[c], c, at)
            below = pick(stress)
        put_carry(stress)
        return 0

    lax.fori_loop(0, pl.cdiv(planes + 5, step1), sweep1, 0)

    strain2 = [gain1 * gain2 * e for e in strain]
    ratio1 = (1.0 + keep1) / gain1
    put_carry(ops.stress(load3(w1_v, 1), load3(w1_v, 2), *material(1), strain2))
    step2 = steps_for(planes + 3, 12)

    def sweep2(t, _):
        below = get_carry()
        w = load3(w1_v, t * step2 + 2)
        for u in range(step2):
            at = t * step2 + 2 + u
            above = load3(w1_v, at + 1)
            stress = ops.stress(w, above, *material(at), strain2)
            r = ops.divergence(stress, below)
            for c in range(3):
                put(w2_v, [ratio1 * x + y for x, y in zip(w[c], r[c])], c, at)
            below = pick(stress)
            w = above
        put_carry(stress)
        return 0

    lax.fori_loop(0, pl.cdiv(planes + 3, step2), sweep2, 0)

    strain3 = [gain2 * e for e in strain]
    ratio2 = (1.0 + keep2) / gain2
    ratio3 = keep2 / (gain1 * gain2)
    put_carry(ops.stress(load3(w2_v, 2), load3(w2_v, 3), *material(2), strain3))
    step3 = steps_for(planes + 1, 12)

    def sweep3(t, _):
        below = get_carry()
        w = load3(w2_v, t * step3 + 3)
        for u in range(step3):
            at = t * step3 + 3 + u
            above = load3(w2_v, at + 1)
            stress = ops.stress(w, above, *material(at), strain3)
            r = ops.divergence(stress, below)
            old = load3(w1_v, at)
            for c in range(3):
                put(
                    w3_v,
                    [ratio2 * x - ratio3 * o + y for x, o, y in zip(w[c], old[c], r[c])],
                    c,
                    at,
                )
            below = pick(stress)
            w = above
        put_carry(stress)
        return 0

    lax.fori_loop(0, pl.cdiv(planes + 1, step3), sweep3, 0)

    def put_out(g):
        span = pl.ds(pl.multiple_of(g * (8 * ROWS), 8 * ROWS), 8 * ROWS)
        return pltpu.make_async_copy(out_v.at[:, span, :], stress_ref.at[:, span, :], sem)

    def final(g, acc):
        acc = list(acc)
        w = load3(w3_v, g * 8 + HALO)
        for s in range(8):
            at = g * 8 + s + HALO
            above = load3(w3_v, at + 1)
            stress = ops.stress(w, above, *material(at), strain)
            for c in range(6):
                acc[c] = acc[c] + fold(stress[c])
                for q in range(4):
                    out_v[c, native(g, s, q), :] = stress[c][q]
            w = above
        put_out(g).start()
        return tuple(acc)

    acc = lax.fori_loop(0, planes // 8, final, (jnp.zeros((8, 128), jnp.float32),) * 6)

    scale = 1.0 / float(EDGE * EDGE * EDGE)
    xx, yy, zz, yz, xz, xy = means = [total(x) * scale for x in acc]
    g0, g1, g2 = corner_columns(grads)
    lane = lax.broadcasted_iota(jnp.int32, (8, 128), 1)
    rows = rows_ref[...]
    rows = jnp.where(lane == FORCE, xx * g0 + xy * g1 + xz * g2, rows)
    rows = jnp.where(lane == FORCE + 1, xy * g0 + yy * g1 + yz * g2, rows)
    rows = jnp.where(lane == FORCE + 2, xz * g0 + yz * g1 + zz * g2, rows)
    sums = jnp.zeros((8, 128), jnp.float32)
    for c in range(6):
        sums = jnp.where(lane == SUMS + c, means[c], sums)
    rows = jnp.where(lane >= SUMS, sums, rows)
    for g in range(packet_ref.shape[0] // 8):
        packet_ref[8 * g : 8 * g + 8, :] = sums
    count = lax.axis_size("macro")
    for v in range(lax.axis_size("vox")):
        for k in range(8):
            packet_ref[pl.ds(v * count + nodes[k], 1), :] = rows[k : k + 1]

    def drain(g, _):
        put_out(g).wait()
        return 0

    lax.fori_loop(0, planes // 8, drain, 0)


def node_kernel(packets_ref, hom_ref, force_ref, tangent_ref):
    packets = packets_ref[...]
    count = lax.axis_size("macro")
    place = lax.broadcasted_iota(jnp.int32, packets.shape, 0)
    point = lax.axis_index("macro")
    own = place == point
    for v in range(1, lax.axis_size("vox")):
        own = own | (place == v * count + point)
    row = jnp.sum(packets, axis=0, keepdims=True)
    means = jnp.sum(jnp.where(own, packets, 0.0), axis=0, keepdims=True)
    tangent_ref[...] = row[:, :BLOCK]
    force_ref[...] = row[:, FORCE : FORCE + 3]
    hom_ref[...] = means[:, SUMS : SUMS + 6]


def gather_by_exchange(x, axis):
    size = lax.axis_size(axis)
    assert size & (size - 1) == 0
    stride = 1
    while stride < size:
        radix = min(4, size // stride)
        parts = [x]
        for j in range(1, radix):
            parts.append(lax.ppermute(x, axis, [(i, i ^ (j * stride)) for i in range(size)]))
        x = jnp.concatenate(parts, axis=0)
        stride *= radix
    return x


def on_device(
    nodal_disp,
    weighted_shape_gradients,
    rve_element,
    connectivity,
    block_slot,
    stiffness,
    yielded_mask,
):
    rve_count, planes, plane_size = stiffness.shape
    macro_size = lax.axis_size("macro")
    vox_size = lax.axis_size("vox")
    assert rve_count == 1 and nodal_disp.shape[0] == 1
    assert planes % 8 == 0 and plane_size == EDGE * EDGE

    gathered = gather_by_exchange(nodal_disp, "macro")

    def rim(first):
        stiff = lax.slice_in_dim(stiffness[0], first, first + HALO, axis=0)
        mask = lax.slice_in_dim(yielded_mask[0], first, first + HALO, axis=0)
        shear = shear_base * stiff * jnp.where(mask == 1, yield_ratio, 1.0)
        return jnp.stack([stiff, shear]).reshape(2 * HALO * ROWS, 128)

    upper, lower = rim(planes - HALO), rim(0)
    if vox_size == 2:
        both = jnp.concatenate([upper, lower], axis=0)
        halo = lax.ppermute(both, "vox", [(0, 1), (1, 0)])
    else:
        forward = [(i, (i + 1) % vox_size) for i in range(vox_size)]
        backward = [(t, s) for s, t in forward]
        halo = jnp.concatenate(
            [lax.ppermute(upper, "vox", forward), lax.ppermute(lower, "vox", backward)], axis=0
        )

    def flat(field):
        parted = field.reshape(planes // 8, 8, ROWS, 128)
        return parted.transpose(0, 2, 1, 3).reshape(planes * ROWS, 128)

    smem = pl.BlockSpec(memory_space=pltpu.SMEM)
    vmem = pl.BlockSpec(memory_space=pltpu.VMEM)
    grads = weighted_shape_gradients[0]
    depth = planes + 2 * HALO + 12
    layer = jax.ShapeDtypeStruct((depth, ROWS, 128), jnp.float32)
    lame, shear, rows = pl.pallas_call(
        material_kernel,
        out_shape=(layer, layer, jax.ShapeDtypeStruct((8, 128), jnp.float32)),
        in_specs=[smem, smem, smem, vmem, vmem, vmem],
        out_specs=(vmem, vmem, vmem),
        compiler_params=pltpu.CompilerParams(vmem_limit_bytes=8 * 1024 * 1024),
        cost_estimate=pl.CostEstimate(
            flops=10 * planes * plane_size,
            bytes_accessed=16 * planes * plane_size,
            transcendentals=0,
        ),
        name="material",
    )(grads, rve_element, block_slot, flat(stiffness), flat(yielded_mask), halo)

    everywhere = macro_size * vox_size
    field = pltpu.VMEM((3, depth, ROWS, 128), jnp.float32)
    stress, strain, packet = pl.pallas_call(
        slab_kernel,
        out_shape=(
            jax.ShapeDtypeStruct((6, planes * ROWS, 128), jnp.float32),
            jax.ShapeDtypeStruct((1, 6), jnp.float32),
            jax.ShapeDtypeStruct((everywhere, 128), jnp.float32),
        ),
        in_specs=[smem, smem, smem, smem, vmem, vmem, vmem],
        out_specs=(pl.BlockSpec(memory_space=pl.ANY), smem, vmem),
        scratch_shapes=[
            field,
            field,
            field,
            pltpu.VMEM((3, ROWS, 128), jnp.float32),
            pltpu.VMEM((6, planes * ROWS, 128), jnp.float32),
            pltpu.SemaphoreType.DMA,
        ],
        compiler_params=pltpu.CompilerParams(vmem_limit_bytes=20 * 1024 * 1024),
        cost_estimate=pl.CostEstimate(
            flops=300 * planes * plane_size,
            bytes_accessed=32 * planes * plane_size,
            transcendentals=0,
        ),
        name="slab",
    )(grads, rve_element, connectivity, gathered, lame, shear, rows)

    voxel_stress = (
        stress.reshape(6, planes // 8, ROWS, 8, 128)
        .transpose(0, 1, 3, 2, 4)
        .reshape(1, 6, planes, plane_size)
    )

    packets = lax.all_to_all(
        packet, ("vox", "macro"), split_axis=0, concat_axis=0, tiled=True
    )
    homogenized, internal_node_force, tangent = pl.pallas_call(
        node_kernel,
        out_shape=(
            jax.ShapeDtypeStruct((1, 6), jnp.float32),
            jax.ShapeDtypeStruct((1, 3), jnp.float32),
            jax.ShapeDtypeStruct((1, BLOCK), jnp.float32),
        ),
        in_specs=[vmem],
        out_specs=(vmem, vmem, vmem),
        name="nodes",
    )(packets)
    return (voxel_stress, homogenized, strain, internal_node_force, tangent)


def solution(mesh):
    in_specs = (
        P("macro", None),
        P("macro", None, None),
        P(),
        P(),
        P(),
        P("macro", "vox", None),
        P("macro", "vox", None),
    )
    out_specs = (
        P("macro", None, "vox", None),
        P("macro", None),
        P("macro", None),
        P("macro", None),
        P("macro", None),
    )
    return jax.shard_map(
        on_device, mesh=mesh, in_specs=in_specs, out_specs=out_specs, check_vma=False
    )
```

time: 51.5 us -> 52.4 us (1.017)
  starting transfers between devices: 5.55 us -> 9.28 us
  blocking collectives: 12.1 us -> 9.76 us
  Pallas kernels: 18.7 us -> 19.9 us
  other arithmetic: 2.68 us -> 1.91 us
  local copies, waits for them, and re-layouts: 5.6 us -> 4.96 us
    ppermute x0 -> x6, starting transfers between devices: none -> 6.25 us  [gather_by_exchange(): lax.ppermute(x, axis, [(i, i ^ j * stride) for i in range(size)])]
    all_to_all x1 -> x0, waiting for transfers between devices: 5.81 us -> none  [to_all(): return lax.all_to_all(x, axes, split_axis=0, concat_axis=0, tiled=True)]
    ppermute x0 -> x6, waiting for transfers between devices: none -> 5.48 us  [gather_by_exchange(): lax.ppermute(x, axis, [(i, i ^ j * stride) for i in range(size)])]
    all_to_all x1 -> x0, starting transfers between devices: 2.52 us -> none  [to_all(): return lax.all_to_all(x, axes, split_axis=0, concat_axis=0, tiled=True)]
    all_to_all x1, blocking collectives: 12.1 us -> 9.76 us  [on_device(): lax.all_to_all(packet, ('vox', 'macro'), split_axis=0, concat_axis=0, til...]
    pallas_call x1 -> x2, Pallas kernels: 16.9 us -> 18.6 us  [the longest x1 17 us: on_device(): pl.pallas_call(slab_kernel, out_shape=(jax.ShapeDtypeStruct((6, planes *...]
    reshape x3 -> x0, local copies, waits for them, and re-layouts: 1.41 us -> none  [the longest x1 0.67 us: on_device(): rve_element.reshape(-1, 1)]
    unnamed x1 -> x0, other arithmetic: 0.7 us -> none
  transfers between devices with their start and end apart: 2 -> 7, of which waited for: 1 -> 4; matrix products, arithmetic and copies ran while one was open for 6% -> 4% of each run, Pallas kernels for 0% -> 0%
where the time goes in v1:
time: 52.4 us; the launch traced here: 52 us
  Pallas kernels  19.9 us (38%)
  blocking collectives  9.76 us (19%)
  starting transfers between devices  9.28 us (18%)
  waiting for transfers between devices  5.49 us (10%)
  local copies, waits for them, and re-layouts  4.96 us (9%)
  other arithmetic  1.91 us (4%)
  between operations  0.71 us (1%)
    pallas_call x1, Pallas kernels, on_device(): pl.pallas_call(slab_kernel, out_shape=(jax.ShapeDtypeStruct((6, planes *...  17 us
    all_to_all x1, blocking collectives, on_device(): lax.all_to_all(packet, ('vox', 'macro'), split_axis=0, concat_axis=0, til...  9.76 us
    ppermute x6, starting transfers between devices, gather_by_exchange(): lax.ppermute(x, axis, [(i, i ^ j * stride) for i in range(size)])  6.25 us
    ppermute x6, waiting for transfers between devices, gather_by_exchange(): lax.ppermute(x, axis, [(i, i ^ j * stride) for i in range(size)])  5.48 us
    unnamed x11, local copies, waits for them, and re-layouts  4.12 us
    ppermute x1, starting transfers between devices, on_device(): halo = lax.ppermute(both, 'vox', [(0, 1), (1, 0)])  3.03 us
    pallas_call x1, Pallas kernels, on_device(): pl.pallas_call(material_kernel, out_shape=(layer, layer, jax.ShapeDtypeSt...  1.57 us
    pallas_call x1, Pallas kernels, on_device(): pl.pallas_call(node_kernel, out_shape=(jax.ShapeDtypeStruct((1, 6), jnp.f...  1.32 us
  transfers between devices with their start and end apart: 7, of which 4 were waited for; matrix products, arithmetic and copies ran while one was open for 4% of the time, Pallas kernels for 0%

profile of v1, /device:TPU:0, one launch (start us, length us, event | category | flops | bytes accessed | tf_op | source)
XLA Modules:
  0.0 52.0 jit_solution(7316564570144033141)
XLA Ops:
  0.6 0.0 copy-start.4
  0.6 1.2 %select_multiply_fusion.1 = (f32[1,3,4096]{2,1,0:T(4,128)S(1)}, f32[1,3,4096]{2,1,0:T(4,128)S(1)}, f32[1,3,4096]{2,1,0:T(4,128)S(1)}, f32[1,3,4096]{2,1,0:T(4,128)S(1)}) fusion(s32[1,32,4096]{2,1,0:T(8,128)} %param.13, f32[1,32,4096]{2,1,0:T(8,128)} %param.12), kind=kLoop, calls=%fused_computation.5 | loop fusion | flops 73728 | bytes 393216 | tf_op jit(solution)/shard_map/mul | solution.py:454
  1.8 0.1 pad_maximum_fusion.1
  1.9 0.1 reshape.46
  2.0 0.1 reshape.47
  2.1 3.0 %collective-permute-start.6 = (f32[384,128]{1,0:T(8,128)S(1)}, f32[384,128]{1,0:T(8,128)S(1)}, u32[]{:S(2)}, u32[]{:S(2)}) collective-permute-start(f32[384,128]{1,0:T(8,128)S(1)} %pad_maximum_fusion), channel_id=1, source_target_pairs={{0,1},{1,0},{2,3},{3,2},{4,5},{5,4},{6,7},{7,6},{8,9},{9,8},{10,11... | collective-permute-start | bytes 589832 | tf_op jit(solution)/shard_map/ppermute | solution.py:460
  5.1 0.7 %collective-permute-start.2 = (f32[1,3]{1,0:T(1,128)}, f32[1,3]{1,0:T(1,128)S(1)}, u32[]{:S(2)}, u32[]{:S(2)}) collective-permute-start(f32[1,3]{1,0:T(1,128)} %param.7), channel_id=1, source_target_pairs={{0,6},{2,4},{4,2},{6,0},{8,14},{10,12},{12,10},{14,8},{16,22},{18,... | collective-permute-start | bytes 44 | tf_op jit(solution)/shard_map/ppermute | solution.py:428
  5.8 0.9 %collective-permute-start.1 = (f32[1,3]{1,0:T(1,128)}, f32[1,3]{1,0:T(1,128)S(1)}, u32[]{:S(2)}, u32[]{:S(2)}) collective-permute-start(f32[1,3]{1,0:T(1,128)} %param.7), channel_id=1, source_target_pairs={{0,4},{2,6},{4,0},{6,2},{8,12},{10,14},{12,8},{14,10},{16,20},{18,... | collective-permute-start | bytes 44 | tf_op jit(solution)/shard_map/ppermute | solution.py:428
  6.6 0.3 collective-permute-start
  7.0 0.7 %copy.22 = f32[1,3,8]{2,1,0:T(4,128)S(1)} copy(f32[1,3,8]{2,0,1:T(1,128)} %param.8) | data formatting | bytes 192
  7.6 0.6 %collective-permute-done.2 = f32[1,3]{1,0:T(1,128)S(1)} collective-permute-done((f32[1,3]{1,0:T(1,128)}, f32[1,3]{1,0:T(1,128)S(1)}, u32[]{:S(2)}, u32[]{:S(2)}) %collective-permute-start.2) | collective-permute-done | bytes 44 | tf_op jit(solution)/shard_map/ppermute | solution.py:428
  8.2 1.2 %collective-permute-done.1 = f32[1,3]{1,0:T(1,128)S(1)} collective-permute-done((f32[1,3]{1,0:T(1,128)}, f32[1,3]{1,0:T(1,128)S(1)}, u32[]{:S(2)}, u32[]{:S(2)}) %collective-permute-start.1) | collective-permute-done | bytes 44 | tf_op jit(solution)/shard_map/ppermute | solution.py:428
  9.4 0.0 collective-permute-done
  9.4 0.7 %pad_maximum_fusion.3 = f32[4,3]{1,0:T(4,128)S(1)} fusion(f32[1,3]{1,0:T(1,128)S(1)} %collective-permute-done.2, f32[1,3]{1,0:T(1,128)S(1)} %collective-permute-done.1, f32[1,3]{1,0:T(1,128)S(1)} %collective-permute-done, f32[1,3]{1,0:T(1,128)} %param.7), kind=kLoop, calls=%fused_computation.7 | loop fusion | flops 36 | bytes 96 | tf_op jit(solution)/shard_map/concatenate | solution.py:429
  10.1 3.6 %collective-permute-start.5 = (f32[4,3]{1,0:T(4,128)S(1)}, f32[4,3]{1,0:T(4,128)S(1)}, u32[]{:S(2)}, u32[]{:S(2)}) collective-permute-start(f32[4,3]{1,0:T(4,128)S(1)} %pad_maximum_fusion.3), channel_id=1, source_target_pairs={{0,24},{2,26},{4,28},{6,30},{8,16},{10,18},{12,20},{14,22},{16,8},... | collective-permute-start | bytes 152 | tf_op jit(solution)/shard_map/ppermute | solution.py:428
  13.7 0.0 collective-permute-start.4
  13.7 0.8 %collective-permute-start.3 = (f32[4,3]{1,0:T(4,128)S(1)}, f32[4,3]{1,0:T(4,128)S(1)}, u32[]{:S(2)}, u32[]{:S(2)}) collective-permute-start(f32[4,3]{1,0:T(4,128)S(1)} %pad_maximum_fusion.3), channel_id=1, source_target_pairs={{0,8},{2,10},{4,12},{6,14},{8,0},{10,2},{12,4},{14,6},{16,24},{18,... | collective-permute-start | bytes 152 | tf_op jit(solution)/shard_map/ppermute | solution.py:428
  14.5 1.0 %collective-permute-done.5 = f32[4,3]{1,0:T(4,128)S(1)} collective-permute-done((f32[4,3]{1,0:T(4,128)S(1)}, f32[4,3]{1,0:T(4,128)S(1)}, u32[]{:S(2)}, u32[]{:S(2)}) %collective-permute-start.5) | collective-permute-done | bytes 80 | tf_op jit(solution)/shard_map/ppermute | solution.py:428
  15.5 2.7 %collective-permute-done.4 = f32[4,3]{1,0:T(4,128)S(1)} collective-permute-done((f32[4,3]{1,0:T(4,128)S(1)}, f32[4,3]{1,0:T(4,128)S(1)}, u32[]{:S(2)}, u32[]{:S(2)}) %collective-permute-start.4) | collective-permute-done | bytes 80 | tf_op jit(solution)/shard_map/ppermute | solution.py:428
  18.2 0.0 collective-permute-done.3
  18.2 0.7 %concatenate.11.gathered = f32[16,3]{1,0:T(8,128)S(1)} concatenate(f32[1,3]{1,0:T(1,128)} %param.7, f32[1,3]{1,0:T(1,128)S(1)} %collective-permute-done, f32[1,3]{1,0:T(1,128)S(1)} %collective-permute-done.1, f32[1,3]{1,0:T(1,128)S(1)} %collective-permute-done.2, f32[4,3]{1,0:T(4,128)S(1)} %collective-permute-done.3, f32[4,3]{1,0:T(4,128)S(1)} %collective-permute-done.4, ...), dimensions={0} | concatenate | bytes 384 | tf_op jit(solution)/shard_map/concatenate | solution.py:429
  18.9 0.0 collective-permute-done.6.halo_ref
  18.9 0.0 copy-start
  18.9 1.0 %copy-done = f32[1,32,4096]{2,1,0:T(8,128)S(1)} copy-done((f32[1,32,4096]{2,1,0:T(8,128)S(1)}, f32[1,32,4096]{2,1,0:T(8,128)}, u32[]{:S(2)}) %copy-start) | copy-done | bytes 524312
  19.9 0.0 copy-start.1
  19.9 1.0 %copy-done.1 = s32[1,32,4096]{2,1,0:T(8,128)S(1)} copy-done((s32[1,32,4096]{2,1,0:T(8,128)S(1)}, s32[1,32,4096]{2,1,0:T(8,128)}, u32[]{:S(2)}) %copy-start.1) | copy-done | bytes 524312
  21.0 0.0 copy-start.2
  21.0 0.7 %copy-done.2 = s32[2,8,8]{2,1,0:T(8,128)S(1)} copy-done((s32[2,8,8]{2,1,0:T(8,128)S(1)}, s32[2,8,8]{2,1,0:T(8,128)}, u32[]{:S(2)}) %copy-start.2) | copy-done | bytes 536
  21.7 0.0 copy-start.3
  21.7 0.7 %copy-done.3 = s32[16]{0:T(128)S(1)} copy-done((s32[16]{0:T(128)S(1)}, s32[16]{0:T(128)}, u32[]{:S(2)}) %copy-start.3) | copy-done | bytes 88
  22.3 1.6 %material.1 = (f32[50,32,128]{2,1,0:T(8,128)S(1)}, f32[50,32,128]{2,1,0:T(8,128)S(1)}, f32[8,128]{1,0:T(8,128)S(1)}) custom-call(f32[3,8]{1,0:T(4,128)S(1)} %bitcast.24, s32[16]{0:T(128)S(1)} %copy-done.3, s32[2,8,8]{2,1,0:T(8,128)S(1)} %copy-done.2, f32[1024,128]{1,0:T(8,128)S(1)} %bitcast.22, s32[1024,128]{1,0:T(8,128)S(1)} %bitcast.23, ...), custom_call_target="tpu_custom_call" | custom-call | flops 1310720 | bytes 2097152 | tf_op jit(solution)/shard_map/material/pallas_call | solution.py:477
  23.9 0.0 copy-done.4
  23.9 17.0 %slab.1 = (f32[6,1024,128]{2,1,0:T(8,128)}, f32[1,6]{1,0:T(1,128)}, f32[32,128]{1,0:T(8,128)S(1)}) custom-call(f32[3,8]{1,0:T(4,128)S(1)} %bitcast.25, s32[16]{0:T(128)S(1)} %copy-done.3, s32[2,8]{1,0:T(2,128)S(1)} %copy-done.4, f32[16,3]{1,0:T(8,128)S(1)} %concatenate.11.gathered, f32[50,32,128]{2,1,0:T(8,128)S(1)} %get-tuple-element.14.lame_v, ...), custom_call_target="tpu_custom_call" | custom-call | flops 39321600 | bytes 4194304 | tf_op jit(solution)/shard_map/slab/pallas_call | solution.py:493
  41.0 9.8 %all_to_all.11 = f32[32,1,128]{2,1,0:T(1,128)} all-to-all(f32[32,1,128]{2,1,0:T(1,128)S(1)} %bitcast.26), channel_id=1, replica_groups=mesh['macro'=16,'vox'=2] {'vox','macro'}, dimensions={0} | all-to-all | bytes 32768 | tf_op jit(solution)/shard_map/all_to_all | solution.py:525
  50.7 1.3 %nodes.1 = (f32[1,6]{1,0:T(1,128)}, f32[1,3]{1,0:T(1,128)}, f32[1,108]{1,0:T(1,128)}) custom-call(f32[32,128]{1,0:T(8,128)} %bitcast.27), custom_call_target="tpu_custom_call" | custom-call | tf_op jit(solution)/shard_map/nodes/pallas_call | solution.py:528
  (1 shorter events, 0.0 us)
Async XLA Ops:
  0.6 23.3 %copy-start.4 = (s32[2,8]{1,0:T(2,128)S(1)}, s32[2,8]{1,0:T(2,128)}, u32[]{:S(2)}) copy-start(s32[2,8]{1,0:T(2,128)} %connectivity.1) | copy-start | bytes 196
  2.1 16.8 %collective-permute-start.6 = (f32[384,128]{1,0:T(8,128)S(1)}, f32[384,128]{1,0:T(8,128)S(1)}, u32[]{:S(2)}, u32[]{:S(2)}) collective-permute-start(f32[384,128]{1,0:T(8,128)S(1)} %pad_maximum_fusion), channel_id=1, source_target_pairs={{0,1},{1,0},{2,3},{3,2},{4,5},{5,4},{6,7},{7,6},{8,9},{9,8},{10,11... | collective-permute-start | bytes 589832 | tf_op jit(solution)/shard_map/ppermute | solution.py:460
  5.1 3.1 %collective-permute-start.2 = (f32[1,3]{1,0:T(1,128)}, f32[1,3]{1,0:T(1,128)S(1)}, u32[]{:S(2)}, u32[]{:S(2)}) collective-permute-start(f32[1,3]{1,0:T(1,128)} %param.7), channel_id=1, source_target_pairs={{0,6},{2,4},{4,2},{6,0},{8,14},{10,12},{12,10},{14,8},{16,22},{18,... | collective-permute-start | bytes 44 | tf_op jit(solution)/shard_map/ppermute | solution.py:428
  5.8 3.7 %collective-permute-start.1 = (f32[1,3]{1,0:T(1,128)}, f32[1,3]{1,0:T(1,128)S(1)}, u32[]{:S(2)}, u32[]{:S(2)}) collective-permute-start(f32[1,3]{1,0:T(1,128)} %param.7), channel_id=1, source_target_pairs={{0,4},{2,6},{4,0},{6,2},{8,12},{10,14},{12,8},{14,10},{16,20},{18,... | collective-permute-start | bytes 44 | tf_op jit(solution)/shard_map/ppermute | solution.py:428
  6.6 2.8 %collective-permute-start = (f32[1,3]{1,0:T(1,128)}, f32[1,3]{1,0:T(1,128)S(1)}, u32[]{:S(2)}, u32[]{:S(2)}) collective-permute-start(f32[1,3]{1,0:T(1,128)} %param.7), channel_id=1, source_target_pairs={{0,2},{2,0},{4,6},{6,4},{8,10},{10,8},{12,14},{14,12},{16,18},{18,... | collective-permute-start | bytes 44 | tf_op jit(solution)/shard_map/ppermute | solution.py:428
  10.1 5.4 %collective-permute-start.5 = (f32[4,3]{1,0:T(4,128)S(1)}, f32[4,3]{1,0:T(4,128)S(1)}, u32[]{:S(2)}, u32[]{:S(2)}) collective-permute-start(f32[4,3]{1,0:T(4,128)S(1)} %pad_maximum_fusion.3), channel_id=1, source_target_pairs={{0,24},{2,26},{4,28},{6,30},{8,16},{10,18},{12,20},{14,22},{16,8},... | collective-permute-start | bytes 152 | tf_op jit(solution)/shard_map/ppermute | solution.py:428
  13.7 4.5 %collective-permute-start.4 = (f32[4,3]{1,0:T(4,128)S(1)}, f32[4,3]{1,0:T(4,128)S(1)}, u32[]{:S(2)}, u32[]{:S(2)}) collective-permute-start(f32[4,3]{1,0:T(4,128)S(1)} %pad_maximum_fusion.3), channel_id=1, source_target_pairs={{0,16},{2,18},{4,20},{6,22},{8,24},{10,26},{12,28},{14,30},{16,0},... | collective-permute-start | bytes 152 | tf_op jit(solution)/shard_map/ppermute | solution.py:428
  13.7 4.5 %collective-permute-start.3 = (f32[4,3]{1,0:T(4,128)S(1)}, f32[4,3]{1,0:T(4,128)S(1)}, u32[]{:S(2)}, u32[]{:S(2)}) collective-permute-start(f32[4,3]{1,0:T(4,128)S(1)} %pad_maximum_fusion.3), channel_id=1, source_target_pairs={{0,8},{2,10},{4,12},{6,14},{8,0},{10,2},{12,4},{14,6},{16,24},{18,... | collective-permute-start | bytes 152 | tf_op jit(solution)/shard_map/ppermute | solution.py:428
  18.9 1.0 %copy-start = (f32[1,32,4096]{2,1,0:T(8,128)S(1)}, f32[1,32,4096]{2,1,0:T(8,128)}, u32[]{:S(2)}) copy-start(f32[1,32,4096]{2,1,0:T(8,128)} %param.12) | copy-start | bytes 1572868
  19.9 1.0 %copy-start.1 = (s32[1,32,4096]{2,1,0:T(8,128)S(1)}, s32[1,32,4096]{2,1,0:T(8,128)}, u32[]{:S(2)}) copy-start(s32[1,32,4096]{2,1,0:T(8,128)} %param.13) | copy-start | bytes 1572868
  21.0 0.7 %copy-start.2 = (s32[2,8,8]{2,1,0:T(8,128)S(1)}, s32[2,8,8]{2,1,0:T(8,128)}, u32[]{:S(2)}) copy-start(s32[2,8,8]{2,1,0:T(8,128)} %block_slot.1) | copy-start | bytes 1540
  21.7 0.7 %copy-start.3 = (s32[16]{0:T(128)S(1)}, s32[16]{0:T(128)}, u32[]{:S(2)}) copy-start(s32[16]{0:T(128)} %rve_element.3) | copy-start | bytes 196

commit v2 on v1

v2 whole, which is shorter than its diff:
```python
import jax
import jax.numpy as jnp
from jax import lax
from jax.experimental import pallas as pl
from jax.experimental.pallas import tpu as pltpu
from jax.sharding import PartitionSpec as P

EDGE = 64
SWEEPS = 3
NEIGHBOUR_SLOTS = 12
BLOCK = NEIGHBOUR_SLOTS * 9

lame_base = 1.5
shear_base = 1.0
yield_ratio = 0.2
precond = 1.0 / 42.0
lower_bound = 0.05
upper_bound = 2.0

ROWS = EDGE * EDGE // 128
WIDE = 256
HALO = 3


def chebyshev_terms(count):
    centre = 0.5 * (upper_bound + lower_bound)
    half_width = 0.5 * (upper_bound - lower_bound)
    ratio_bound = centre / half_width
    rho_prev = 1.0 / ratio_bound
    weights = []
    for number in range(count):
        rho_next = 1.0 / (2.0 * ratio_bound - rho_prev)
        weights.append((rho_next * rho_prev, 2.0 * rho_next / half_width))
        rho_prev = rho_next
    return (centre, weights)


centre, ((keep1, push1), (keep2, push2)) = chebyshev_terms(SWEEPS - 1)
gain1 = push1 * precond
gain2 = push2 * precond

def best_step(count, most):
    return min(range(1, most + 1), key=lambda s: (-(-count // s) * s, -s))


def spot(at, jj):
    half = (jj & 1) * 128
    return at, pl.ds(8 * (jj // 2), 8), pl.ds(half, 128)


def load(ref, at, jj):
    return ref[spot(at, jj)]


def load3(ref, at, jj):
    return [ref[(c, *spot(at, jj))] for c in range(3)]


def next_row(ref, c, at, jj):
    if jj < 7:
        return ref[(c, *spot(at, jj + 1))]
    return pltpu.roll(ref[(c, *spot(at, 0))], 7, 0)


def next_lane(x):
    return pltpu.roll(x, 126, 1)


def prev_lane(x):
    return pltpu.roll(x, 2, 1)


def stress_at(w_ref, at, jj, w, lame, shear, strain):
    w0, w1, w2 = w
    n0, n1, n2 = load3(w_ref, at + 1, jj)
    row0, row1, row2 = [next_row(w_ref, c, at, jj) for c in range(3)]
    lane0, lane1, lane2 = [next_lane(x) for x in w]
    e0 = (n0 - w0) + strain[0]
    e1 = (row1 - w1) + strain[1]
    e2 = (lane2 - w2) + strain[2]
    g3 = (lane1 + row2) - (w1 + w2) + strain[3]
    g4 = (lane0 + n2) - (w0 + w2) + strain[4]
    g5 = (row0 + n1) - (w0 + w1) + strain[5]
    bulk = lame * (e0 + e1 + e2)
    twice = shear + shear
    return (
        bulk + twice * e0,
        bulk + twice * e1,
        bulk + twice * e2,
        shear * g3,
        shear * g4,
        shear * g5,
    )


def sweep_plane(w_ref, lame_ref, shear_ref, carry_v, old, new, at, strain, update):
    first = None
    row_xy = row_yy = row_yz = None
    for jj in range(8):
        w = load3(w_ref, at, jj)
        stress = stress_at(
            w_ref, at, jj, w, load(lame_ref, at, jj), load(shear_ref, at, jj), strain
        )
        xx, yy, zz, yz, xz, xy = stress
        pxx, pxz, pxy = [carry_v[(old, c, *spot(0, jj)[1:])] for c in range(3)]
        for c, x in enumerate((xx, xz, xy)):
            carry_v[(new, c, *spot(0, jj)[1:])] = x
        r = [
            (xx - pxx) + (xz - prev_lane(xz)) + xy,
            (xy - pxy) + (yz - prev_lane(yz)) + yy,
            (xz - pxz) + (zz - prev_lane(zz)) + yz,
        ]
        if jj == 0:
            first = r
        else:
            update(jj, w, [r[0] - row_xy, r[1] - row_yy, r[2] - row_yz])
        row_xy, row_yy, row_yz = xy, yy, yz
    rows = [pltpu.roll(x, 1, 0) for x in (row_xy, row_yy, row_yz)]
    update(0, load3(w_ref, at, 0), [x - y for x, y in zip(first, rows)])


def carry_plane(w_ref, lame_ref, shear_ref, carry_v, at, strain):
    for jj in range(8):
        w = load3(w_ref, at, jj)
        xx, yy, zz, yz, xz, xy = stress_at(
            w_ref, at, jj, w, load(lame_ref, at, jj), load(shear_ref, at, jj), strain
        )
        for c, x in enumerate((xx, xz, xy)):
            carry_v[(0, c, *spot(0, jj)[1:])] = x


def target_lane(m):
    return ((m >> 6) & 1) * 128 + (m & 63) * 2 + (m >> 7)


def lane_matrix(inverse):
    row = lax.broadcasted_iota(jnp.int32, (WIDE, WIDE), 0)
    column = lax.broadcasted_iota(jnp.int32, (WIDE, WIDE), 1)
    hit = (target_lane(column) == row) if inverse else (target_lane(row) == column)
    return jnp.where(hit, 1.0, 0.0).astype(jnp.bfloat16)


def permute_lanes(x, matrix, terms):
    result = None
    for t in range(terms):
        part = x.astype(jnp.bfloat16)
        moved = jnp.dot(part, matrix, preferred_element_type=jnp.float32)
        result = moved if result is None else result + moved
        if t + 1 < terms:
            x = x - part.astype(jnp.float32)
    return result


def native(plane, q):
    return pl.ds((plane // 8) * (8 * ROWS) + plane % 8 + 8 * q, 8, stride=ROWS)


def total(x):
    return jnp.sum(x, axis=(0, 1), keepdims=True)


def corner_columns(grads):
    corner = lax.broadcasted_iota(jnp.int32, (8, 128), 0)
    columns = []
    for c in range(3):
        column = jnp.full((8, 128), grads[c, 0], jnp.float32)
        for k in range(1, 8):
            column = jnp.where(corner == k, grads[c, k], column)
        columns.append(column)
    return columns


FORCE = BLOCK
SUMS = BLOCK + 4
LAME_MEAN = 120
SHEAR_MEAN = 121


def material_kernel(
    grads,
    rve_element,
    block_slot,
    stiff_hbm,
    mask_hbm,
    halo_ref,
    lame_ref,
    shear_ref,
    dlame_ref,
    dshear_ref,
    rows_ref,
    stiff_v,
    mask_v,
    lame_in,
    shear_in,
    sems,
):
    copies = [
        pltpu.make_async_copy(stiff_hbm, stiff_v, sems.at[0]),
        pltpu.make_async_copy(mask_hbm, mask_v, sems.at[1]),
    ]
    for copy in copies:
        copy.start()
    planes = stiff_v.shape[0] // ROWS
    half = planes // 2
    depth = half + 2 * HALO
    elem = rve_element[lax.axis_index("macro")]
    matrix = lane_matrix(False)
    for copy in copies:
        copy.wait()

    acc_l = acc_m = jnp.zeros((8, 128), jnp.float32)
    for h in range(2):
        for at in range(depth):
            plane = at - HALO + h * half
            for q in range(4):
                if 0 <= plane < planes:
                    stiff = stiff_v[native(plane, q), :]
                    mask = mask_v[native(plane, q), :]
                    shear = stiff * jnp.where(mask == 1, shear_base * yield_ratio, shear_base)
                else:
                    side, far = (0, plane + HALO) if plane < 0 else (1, plane - planes)
                    base = (side * 2 * HALO + far) * ROWS + q
                    stiff = halo_ref[pl.ds(base, 8, stride=4), :]
                    shear = halo_ref[pl.ds(base + HALO * ROWS, 8, stride=4), :]
                lame = lame_base * stiff
                place = (at, pl.ds(8 * q, 8), pl.ds(128 * h, 128))
                lame_in[place] = lame
                shear_in[place] = shear
                if HALO <= at < HALO + half:
                    acc_l = acc_l + lame
                    acc_m = acc_m + shear

    for source, target in ((lame_in, lame_ref), (shear_in, shear_ref)):
        x = source[...].reshape(depth * ROWS, WIDE)
        target[pl.ds(0, depth)] = permute_lanes(x, matrix, 3).reshape(depth, ROWS, WIDE)

    def difference(t, _):
        at = t + 1
        for source, target in ((lame_ref, dlame_ref), (shear_ref, dshear_ref)):
            for jj in range(8):
                here = load(source, at, jj)
                before = load(source, at, jj - 1) if jj else pltpu.roll(load(source, at, 7), 1, 0)
                target[(0, *spot(at, jj))] = here - load(source, at - 1, jj)
                target[(1, *spot(at, jj))] = here - before
                target[(2, *spot(at, jj))] = here - prev_lane(here)
        return 0

    lax.fori_loop(0, depth - 1, difference, 0)

    scale = 1.0 / float(EDGE * EDGE * EDGE)
    lame, shear = total(acc_l) * scale, total(acc_m) * scale
    mine = corner_columns(grads)
    corner = lax.broadcasted_iota(jnp.int32, (8, 128), 0)
    lane = lax.broadcasted_iota(jnp.int32, (8, 128), 1)
    slot_of = jnp.zeros((8, 128), jnp.int32)
    for s in range(1, NEIGHBOUR_SLOTS + 1):
        slot_of = slot_of + jnp.where(lane >= 9 * s, 1, 0)
    inner = lane - 9 * slot_of
    a_of = jnp.where(inner >= 3, 1, 0) + jnp.where(inner >= 6, 1, 0)
    b_of = inner - 3 * a_of

    def by(which, x, y, z):
        return jnp.where(which == 0, x, jnp.where(which == 1, y, z))

    lame_a = lame * by(a_of, *mine)
    shear_b = shear * by(b_of, *mine)
    diagonal = jnp.where(a_of == b_of, shear, 0.0)
    rows = jnp.zeros((8, 128), jnp.float32)
    for l in range(8):
        other = [grads[c, l] for c in range(3)]
        dots = mine[0] * other[0] + mine[1] * other[1] + mine[2] * other[2]
        block = lame_a * by(b_of, *other) + shear_b * by(a_of, *other) + diagonal * dots
        slot = jnp.full((8, 128), block_slot[elem, 0, l], jnp.int32)
        for k in range(1, 8):
            slot = jnp.where(corner == k, block_slot[elem, k, l], slot)
        rows = rows + jnp.where(slot_of == slot, block, 0.0)
    rows = jnp.where(lane == LAME_MEAN, lame, rows)
    rows = jnp.where(lane == SHEAR_MEAN, shear, rows)
    rows_ref[...] = rows


def sweep_kernel(
    grads,
    rve_element,
    connectivity,
    gathered,
    lame_ref,
    shear_ref,
    dlame_ref,
    dshear_ref,
    rows_ref,
    w3_ref,
    strain_ref,
    packet_ref,
    w1_v,
    w2_v,
    carry_v,
):
    half = lame_ref.shape[0] - 2 * HALO - MARGIN
    elem = rve_element[lax.axis_index("macro")]
    nodes = [connectivity[elem, k] for k in range(8)]
    moves = [[gathered[n, a] for n in nodes] for a in range(3)]

    def dot(c, a):
        result = grads[c, 0] * moves[a][0]
        for k in range(1, 8):
            result = result + grads[c, k] * moves[a][k]
        return result

    strain = [
        dot(0, 0),
        dot(1, 1),
        dot(2, 2),
        dot(2, 1) + dot(1, 2),
        dot(2, 0) + dot(0, 2),
        dot(1, 0) + dot(0, 1),
    ]
    for c in range(6):
        strain_ref[0, c] = strain[c]

    scale1 = gain1 * gain2 * precond / centre
    strain1 = [scale1 * e for e in strain]
    trace1 = strain1[0] + strain1[1] + strain1[2]
    twice1 = [2.0 * strain1[c] for c in range(3)]
    step1 = best_step(half + 5, STEP)

    def sweep1(t, _):
        for u in range(step1):
            at = t * step1 + 1 + u
            for jj in range(8):
                l0, l1, l2 = load3(dlame_ref, at, jj)
                m0, m1, m2 = load3(dshear_ref, at, jj)
                w1_v[(0, *spot(at, jj))] = (
                    trace1 * l0 + twice1[0] * m0 + (strain1[5] * m1 + strain1[4] * m2)
                )
                w1_v[(1, *spot(at, jj))] = (
                    trace1 * l1 + twice1[1] * m1 + (strain1[5] * m0 + strain1[3] * m2)
                )
                w1_v[(2, *spot(at, jj))] = (
                    trace1 * l2 + twice1[2] * m2 + (strain1[4] * m0 + strain1[3] * m1)
                )
        return 0

    lax.fori_loop(0, pl.cdiv(half + 5, step1), sweep1, 0)

    strain2 = [gain1 * gain2 * e for e in strain]
    ratio1 = (1.0 + keep1) / gain1
    step2 = best_step(half + 3, STEP)
    carry_plane(w1_v, lame_ref, shear_ref, carry_v, 1, strain2)

    def sweep2(t, _):
        for u in range(step2):
            at = t * step2 + 2 + u

            def update(jj, w, r):
                for c in range(3):
                    w2_v[(c, *spot(at, jj))] = ratio1 * w[c] + r[c]

            sweep_plane(
                w1_v, lame_ref, shear_ref, carry_v, u, (u + 1) % step2, at, strain2, update
            )
        return 0

    lax.fori_loop(0, pl.cdiv(half + 3, step2), sweep2, 0)

    strain3 = [gain2 * e for e in strain]
    ratio2 = (1.0 + keep2) / gain2
    ratio3 = keep2 / (gain1 * gain2)
    step3 = best_step(half + 1, STEP)
    carry_plane(w2_v, lame_ref, shear_ref, carry_v, 2, strain3)

    def sweep3(t, _):
        for u in range(step3):
            at = t * step3 + 3 + u

            def update(jj, w, r):
                old = load3(w1_v, at, jj)
                for c in range(3):
                    w3_ref[(c, *spot(at, jj))] = (ratio2 * w[c] - ratio3 * old[c]) + r[c]

            sweep_plane(
                w2_v, lame_ref, shear_ref, carry_v, u, (u + 1) % step3, at, strain3, update
            )
        return 0

    lax.fori_loop(0, pl.cdiv(half + 1, step3), sweep3, 0)

    def by_parts(t, acc):
        bulk, a0, a1, a2, a3, a4, a5 = acc
        at = t + HALO
        for jj in range(8):
            w0, w1, w2 = load3(w3_ref, at, jj)
            l0, l1, l2 = load3(dlame_ref, at, jj)
            m0, m1, m2 = load3(dshear_ref, at, jj)
            bulk = bulk + (l0 * w0 + l1 * w1 + l2 * w2)
            a0 = a0 + m0 * w0
            a1 = a1 + m1 * w1
            a2 = a2 + m2 * w2
            a3 = a3 + (m2 * w1 + m1 * w2)
            a4 = a4 + (m2 * w0 + m0 * w2)
            a5 = a5 + (m1 * w0 + m0 * w1)
        return bulk, a0, a1, a2, a3, a4, a5

    zero = jnp.zeros((8, 128), jnp.float32)
    acc = lax.fori_loop(0, half, by_parts, (zero,) * 7)
    scale = 1.0 / float(EDGE * EDGE * EDGE)
    bulk, *parts = [total(x) * scale for x in acc]
    rows = rows_ref[...]
    lame = rows[:1, LAME_MEAN : LAME_MEAN + 1]
    shear = rows[:1, SHEAR_MEAN : SHEAR_MEAN + 1]
    bulk = lame * (strain[0] + strain[1] + strain[2]) - bulk
    means = [bulk + 2.0 * (shear * strain[c] - parts[c]) for c in range(3)]
    means += [shear * strain[c] - parts[c] for c in range(3, 6)]

    xx, yy, zz, yz, xz, xy = means
    g0, g1, g2 = corner_columns(grads)
    lane = lax.broadcasted_iota(jnp.int32, (8, 128), 1)
    rows = jnp.where(lane == FORCE, xx * g0 + xy * g1 + xz * g2, rows)
    rows = jnp.where(lane == FORCE + 1, xy * g0 + yy * g1 + yz * g2, rows)
    rows = jnp.where(lane == FORCE + 2, xz * g0 + yz * g1 + zz * g2, rows)
    sums = jnp.zeros((8, 128), jnp.float32)
    for c in range(6):
        sums = jnp.where(lane == SUMS + c, means[c], sums)
    rows = jnp.where(lane >= SUMS, sums, rows)
    for g in range(packet_ref.shape[0] // 8):
        packet_ref[8 * g : 8 * g + 8, :] = sums
    count = lax.axis_size("macro")
    for v in range(lax.axis_size("vox")):
        for k in range(8):
            packet_ref[pl.ds(v * count + nodes[k], 1), :] = rows[k : k + 1]


def stress_kernel(
    strain_in,
    lame_ref,
    shear_ref,
    w3_ref,
    stress_ref,
    out_v,
    work_v,
    sem,
):
    half = lame_ref.shape[0] - 2 * HALO - MARGIN
    strain = [strain_in[0, c] for c in range(6)]
    matrix = lane_matrix(True)
    copies = []
    for first in range(0, half, GROUP):
        slot = (first // GROUP) % 2
        for u in range(GROUP):
            at = first + u + HALO
            for jj in range(8):
                stress = stress_at(
                    w3_ref,
                    at,
                    jj,
                    load3(w3_ref, at, jj),
                    load(lame_ref, at, jj),
                    load(shear_ref, at, jj),
                    strain,
                )
                for c in range(6):
                    work_v[(slot, u, c, *spot(0, jj)[1:])] = stress[c]
        x = work_v[slot].reshape(GROUP * 6 * ROWS, WIDE)
        y = permute_lanes(x, matrix, 2)
        for u in range(GROUP):
            for c in range(6):
                for q in range(4):
                    row = ((u * 6 + c) * 4 + q) * 8
                    for h in range(2):
                        plane = first + u + h * half
                        out_v[c, native(plane, q), :] = y[row : row + 8, 128 * h : 128 * h + 128]
        done = []
        if half % 8 == 0 and (first + GROUP) % 8 == 0:
            done = [(first + GROUP) // 8 - 1 + h * (half // 8) for h in range(2)]
        elif first + GROUP == half:
            done = range(2 * half // 8)
        if done:
            for group in done:
                span = pl.ds(group * (8 * ROWS), 8 * ROWS)
                copy = pltpu.make_async_copy(
                    out_v.at[:, span, :], stress_ref.at[:, span, :], sem.at[len(copies)]
                )
                copy.start()
                copies.append(copy)
    for copy in copies:
        copy.wait()


STEP = 3
GROUP = 4
MARGIN = 3


def node_kernel(packets_ref, hom_ref, force_ref, tangent_ref):
    packets = packets_ref[...]
    count = lax.axis_size("macro")
    place = lax.broadcasted_iota(jnp.int32, packets.shape, 0)
    point = lax.axis_index("macro")
    own = place == point
    for v in range(1, lax.axis_size("vox")):
        own = own | (place == v * count + point)
    row = jnp.sum(packets, axis=0, keepdims=True)
    means = jnp.sum(jnp.where(own, packets, 0.0), axis=0, keepdims=True)
    tangent_ref[...] = row[:, :BLOCK]
    force_ref[...] = row[:, FORCE : FORCE + 3]
    hom_ref[...] = means[:, SUMS : SUMS + 6]


def on_device(
    nodal_disp,
    weighted_shape_gradients,
    rve_element,
    connectivity,
    block_slot,
    stiffness,
    yielded_mask,
):
    rve_count, planes, plane_size = stiffness.shape
    macro_size = lax.axis_size("macro")
    vox_size = lax.axis_size("vox")
    everywhere = macro_size * vox_size
    assert rve_count == 1 and nodal_disp.shape[0] == 1
    assert planes % 8 == 0 and plane_size == EDGE * EDGE

    gathered = lax.all_to_all(
        jnp.broadcast_to(nodal_disp, (macro_size, 3)),
        "macro",
        split_axis=0,
        concat_axis=0,
        tiled=True,
    )

    def rim(first):
        stiff = lax.slice_in_dim(stiffness[0], first, first + HALO, axis=0)
        mask = lax.slice_in_dim(yielded_mask[0], first, first + HALO, axis=0)
        shear = shear_base * stiff * jnp.where(mask == 1, yield_ratio, 1.0)
        return jnp.stack([stiff, shear]).reshape(2 * HALO * ROWS, 128)

    upper, lower = rim(planes - HALO), rim(0)
    if vox_size == 2:
        both = jnp.concatenate([upper, lower], axis=0)
        halo = lax.ppermute(both, "vox", [(0, 1), (1, 0)])
    else:
        forward = [(i, (i + 1) % vox_size) for i in range(vox_size)]
        backward = [(t, s) for s, t in forward]
        halo = jnp.concatenate(
            [lax.ppermute(upper, "vox", forward), lax.ppermute(lower, "vox", backward)], axis=0
        )

    def flat(field):
        parted = field.reshape(planes // 8, 8, ROWS, 128)
        return parted.transpose(0, 2, 1, 3).reshape(planes * ROWS, 128)

    smem = pl.BlockSpec(memory_space=pltpu.SMEM)
    vmem = pl.BlockSpec(memory_space=pltpu.VMEM)
    anywhere = pl.BlockSpec(memory_space=pl.ANY)
    mib = 1024 * 1024
    f32 = jnp.float32
    grads = weighted_shape_gradients[0]
    half = planes // 2
    depth = half + 2 * HALO + MARGIN
    scalar = jax.ShapeDtypeStruct((depth, ROWS, WIDE), f32)
    vector = jax.ShapeDtypeStruct((3, depth, ROWS, WIDE), f32)
    native_field = pltpu.VMEM((planes * ROWS, 128), f32)
    half_field = pltpu.VMEM((half + 2 * HALO, ROWS, WIDE), f32)

    def cost(flops, size):
        return pl.CostEstimate(
            flops=flops * planes * plane_size,
            bytes_accessed=size * planes * plane_size,
            transcendentals=0,
        )

    lame, shear, dlame, dshear, rows = pl.pallas_call(
        material_kernel,
        out_shape=(scalar, scalar, vector, vector, jax.ShapeDtypeStruct((8, 128), f32)),
        in_specs=[smem, smem, smem, anywhere, anywhere, vmem],
        out_specs=(vmem,) * 5,
        scratch_shapes=[
            native_field,
            pltpu.VMEM((planes * ROWS, 128), jnp.int32),
            half_field,
            half_field,
            pltpu.SemaphoreType.DMA((2,)),
        ],
        compiler_params=pltpu.CompilerParams(vmem_limit_bytes=16 * mib),
        cost_estimate=cost(100, 40),
        name="material",
    )(grads, rve_element, block_slot, flat(stiffness), flat(yielded_mask), halo)

    field = pltpu.VMEM((3, depth, ROWS, WIDE), f32)
    w3, strain, packet = pl.pallas_call(
        sweep_kernel,
        out_shape=(
            vector,
            jax.ShapeDtypeStruct((1, 6), f32),
            jax.ShapeDtypeStruct((everywhere, 128), f32),
        ),
        in_specs=[smem] * 4 + [vmem] * 5,
        out_specs=(vmem, smem, vmem),
        scratch_shapes=[field, field, pltpu.VMEM((STEP, 3, ROWS, WIDE), f32)],
        compiler_params=pltpu.CompilerParams(vmem_limit_bytes=16 * mib),
        cost_estimate=cost(200, 40),
        name="sweeps",
    )(grads, rve_element, connectivity, gathered, lame, shear, dlame, dshear, rows)

    packets = lax.all_to_all(
        packet, ("vox", "macro"), split_axis=0, concat_axis=0, tiled=True
    )

    stress = pl.pallas_call(
        stress_kernel,
        out_shape=jax.ShapeDtypeStruct((6, planes * ROWS, 128), f32),
        in_specs=[smem, vmem, vmem, vmem],
        out_specs=anywhere,
        scratch_shapes=[
            pltpu.VMEM((6, planes * ROWS, 128), f32),
            pltpu.VMEM((2, GROUP, 6, ROWS, WIDE), f32),
            pltpu.SemaphoreType.DMA((planes // 8,)),
        ],
        compiler_params=pltpu.CompilerParams(vmem_limit_bytes=20 * mib),
        cost_estimate=cost(100, 40),
        name="stress",
    )(strain, lame, shear, w3)
    voxel_stress = (
        stress.reshape(6, planes // 8, ROWS, 8, 128)
        .transpose(0, 1, 3, 2, 4)
        .reshape(1, 6, planes, plane_size)
    )

    homogenized, internal_node_force, tangent = pl.pallas_call(
        node_kernel,
        out_shape=(
            jax.ShapeDtypeStruct((1, 6), f32),
            jax.ShapeDtypeStruct((1, 3), f32),
            jax.ShapeDtypeStruct((1, BLOCK), f32),
        ),
        in_specs=[vmem],
        out_specs=(vmem, vmem, vmem),
        name="nodes",
    )(packets)
    return (voxel_stress, homogenized, strain, internal_node_force, tangent)


def solution(mesh):
    in_specs = (
        P("macro", None),
        P("macro", None, None),
        P(),
        P(),
        P(),
        P("macro", "vox", None),
        P("macro", "vox", None),
    )
    out_specs = (
        P("macro", None, "vox", None),
        P("macro", None),
        P("macro", None),
        P("macro", None),
        P("macro", None),
    )
    return jax.shard_map(
        on_device, mesh=mesh, in_specs=in_specs, out_specs=out_specs, check_vma=False
    )
```

time: 52.4 us -> 53.1 us (1.013)
  local copies, waits for them, and re-layouts: 4.96 us -> 16.2 us
  blocking collectives: 9.76 us -> 0 us
  waiting for transfers between devices: 5.49 us -> 0.01 us
  starting transfers between devices: 9.28 us -> 13.9 us
  other arithmetic: 1.91 us -> 1.25 us
    all_to_all x0 -> x2, starting transfers between devices: none -> 10.9 us  [the longest x1 5.91 us: on_device(): lax.all_to_all(jnp.broadcast_to(nodal_disp, (macro_size, 3)), 'macro', sp...]
    unnamed x11 -> x29, local copies, waits for them, and re-layouts: 4.12 us -> 14.8 us
    all_to_all x1 -> x0, blocking collectives: 9.76 us -> none  [on_device(): lax.all_to_all(packet, ('vox', 'macro'), split_axis=0, concat_axis=0, til...]
    ppermute x6 -> x0, starting transfers between devices: 6.25 us -> none  [gather_by_exchange(): lax.ppermute(x, axis, [(i, i ^ j * stride) for i in range(size)])]
    ppermute x6 -> x0, waiting for transfers between devices: 5.48 us -> none  [gather_by_exchange(): lax.ppermute(x, axis, [(i, i ^ j * stride) for i in range(size)])]
    broadcast_in_dim x0 -> x1, local copies, waits for them, and re-layouts: none -> 1.25 us  [on_device(): jnp.broadcast_to(nodal_disp, (macro_size, 3))]
    concatenate x1 -> x0, local copies, waits for them, and re-layouts: 0.69 us -> none  [gather_by_exchange(): x = jnp.concatenate(parts, axis=0)]
    concatenate x1 -> x0, other arithmetic: 0.67 us -> none  [gather_by_exchange(): x = jnp.concatenate(parts, axis=0)]
  transfers between devices with their start and end apart: 7 -> 3, of which waited for: 4 -> 0; matrix products, arithmetic and copies ran while one was open for 4% -> 4% of each run, Pallas kernels for 0% -> 18%
where the time goes in v2:
time: 53.1 us; the launch traced here: 52.5 us
  Pallas kernels  20.4 us (38%)
  local copies, waits for them, and re-layouts  16.2 us (31%)
  starting transfers between devices  13.9 us (26%)
  other arithmetic  1.25 us (2%)
  between operations  0.78 us (1%)
    unnamed x29, local copies, waits for them, and re-layouts  14.8 us
    pallas_call x1, Pallas kernels, on_device(): pl.pallas_call(sweep_kernel, out_shape=(vector, jax.ShapeDtypeStruct((1,...  9.53 us
    all_to_all x1, starting transfers between devices, on_device(): lax.all_to_all(jnp.broadcast_to(nodal_disp, (macro_size, 3)), 'macro', sp...  5.91 us
    pallas_call x1, Pallas kernels, on_device(): pl.pallas_call(stress_kernel, out_shape=jax.ShapeDtypeStruct((6, planes *...  5.33 us
    all_to_all x1, starting transfers between devices, on_device(): lax.all_to_all(packet, ('vox', 'macro'), split_axis=0, concat_axis=0, til...  4.99 us
    pallas_call x1, Pallas kernels, on_device(): pl.pallas_call(material_kernel, out_shape=(scalar, scalar, vector, vector...  4.17 us
    ppermute x1, starting transfers between devices, on_device(): halo = lax.ppermute(both, 'vox', [(0, 1), (1, 0)])  3.03 us
    pallas_call x1, Pallas kernels, on_device(): pl.pallas_call(node_kernel, out_shape=(jax.ShapeDtypeStruct((1, 6), f32),...  1.32 us
  transfers between devices with their start and end apart: 3, of which 0 were waited for; matrix products, arithmetic and copies ran while one was open for 4% of the time, Pallas kernels for 18%

profile of v2, /device:TPU:0, one launch (start us, length us, event | category | flops | bytes accessed | tf_op | source)
XLA Modules:
  0.0 52.5 jit_solution(4701413763493110940)
XLA Ops:
  0.6 0.0 copy-start.10
  0.6 0.0 copy-start.11
  0.7 1.2 %select_multiply_fusion.1 = (f32[1,3,4096]{2,1,0:T(4,128)S(1)}, f32[1,3,4096]{2,1,0:T(4,128)S(1)}, f32[1,3,4096]{2,1,0:T(4,128)S(1)}, f32[1,3,4096]{2,1,0:T(4,128)S(1)}) fusion(s32[1,32,4096]{2,1,0:T(8,128)} %param.13, f32[1,32,4096]{2,1,0:T(8,128)} %param.12), kind=kLoop, calls=%fused_computation.5 | loop fusion | flops 73728 | bytes 393216 | tf_op jit(solution)/shard_map/mul | solution.py:536
  1.8 0.1 pad_maximum_fusion.1
  1.9 0.1 reshape.52
  2.0 0.1 reshape.53
  2.1 3.0 %collective-permute-start = (f32[384,128]{1,0:T(8,128)S(1)}, f32[384,128]{1,0:T(8,128)S(1)}, u32[]{:S(2)}, u32[]{:S(2)}) collective-permute-start(f32[384,128]{1,0:T(8,128)S(1)} %pad_maximum_fusion), channel_id=1, source_target_pairs={{0,1},{1,0},{2,3},{3,2},{4,5},{5,4},{6,7},{7,6},{8,9},{9,8},{10,11... | collective-permute-start | bytes 589832 | tf_op jit(solution)/shard_map/ppermute | solution.py:542
  5.1 1.3 %broadcast_in_dim.15 = f32[16,1,3]{2,1,0:T(1,128)} broadcast(f32[3]{0:T(128)} %bitcast.31), dimensions={2} | broadcast | bytes 204 | tf_op jit(solution)/shard_map/broadcast_in_dim | solution.py:526
  6.4 5.9 %all-to-all-start = ((f32[16,1,3]{2,1,0:T(1,128)}), f32[16,1,3]{2,1,0:T(1,128)S(1)}, u32[]{:S(2)}, u32[]{:S(2)}) async-start(f32[16,1,3]{2,1,0:T(1,128)} %broadcast_in_dim.15), calls=%async_computation | async-start | bytes 16384 | tf_op jit(solution)/shard_map/all_to_all | solution.py:525
  12.3 0.7 %copy.19 = f32[1,3,8]{2,1,0:T(4,128)S(1)} copy(f32[1,3,8]{2,0,1:T(1,128)} %param.8) | data formatting | bytes 192
  13.0 0.0 collective-permute-done.halo_ref
  13.0 0.0 copy-start.6
  13.0 1.0 %copy-done.6 = f32[1,32,4096]{2,1,0:T(8,128)S(1)} copy-done((f32[1,32,4096]{2,1,0:T(8,128)S(1)}, f32[1,32,4096]{2,1,0:T(8,128)}, u32[]{:S(2)}) %copy-start.6) | copy-done | bytes 524312
  14.0 0.0 copy-start.7
  14.0 1.0 %copy-done.7 = s32[1,32,4096]{2,1,0:T(8,128)S(1)} copy-done((s32[1,32,4096]{2,1,0:T(8,128)S(1)}, s32[1,32,4096]{2,1,0:T(8,128)}, u32[]{:S(2)}) %copy-start.7) | copy-done | bytes 524312
  15.1 0.0 copy-start.8
  15.1 0.7 %copy-done.8 = s32[2,8,8]{2,1,0:T(8,128)S(1)} copy-done((s32[2,8,8]{2,1,0:T(8,128)S(1)}, s32[2,8,8]{2,1,0:T(8,128)}, u32[]{:S(2)}) %copy-start.8) | copy-done | bytes 536
  15.8 0.0 copy-start.9
  15.8 0.7 %copy-done.9 = s32[16]{0:T(128)S(1)} copy-done((s32[16]{0:T(128)S(1)}, s32[16]{0:T(128)}, u32[]{:S(2)}) %copy-start.9) | copy-done | bytes 88
  16.4 4.2 %material.1 = (f32[25,32,256]{2,1,0:T(8,128)S(1)}, f32[25,32,256]{2,1,0:T(8,128)S(1)}, f32[3,25,32,256]{3,2,1,0:T(8,128)S(1)}, f32[3,25,32,256]{3,2,1,0:T(8,128)S(1)}, f32[8,128]{1,0:T(8,128)S(1)}) custom-call(f32[3,8]{1,0:T(4,128)S(1)} %bitcast.27, s32[16]{0:T(128)S(1)} %copy-done.9, s32[2,8,8]{2,1,0:T(8,128)S(1)} %copy-done.8, f32[1024,128]{1,0:T(8,128)S(1)} %bitcast.24, ...), custom_call_target="tpu_custom_call" | custom-call | flops 13107200 | bytes 5242880 | tf_op jit(solution)/shard_map/material/pallas_call | solution.py:574
  20.6 0.0 copy-start
  20.6 1.4 %copy-done = f32[3,25,32,256]{3,2,1,0:T(8,128)} copy-done((f32[3,25,32,256]{3,2,1,0:T(8,128)}, f32[3,25,32,256]{3,2,1,0:T(8,128)S(1)}, u32[]{:S(2)}) %copy-start) | copy-done | bytes 2457624
  22.0 0.0 copy-start.2
  22.0 1.5 %copy-done.2 = f32[3,25,32,256]{3,2,1,0:T(8,128)} copy-done((f32[3,25,32,256]{3,2,1,0:T(8,128)}, f32[3,25,32,256]{3,2,1,0:T(8,128)S(1)}, u32[]{:S(2)}) %copy-start.2) | copy-done | bytes 2457624
  23.5 0.0 all-to-all-done
  23.5 0.0 copy-done.10
  23.5 0.0 copy-done.11
  23.5 0.0 copy-start.1
  23.5 1.7 %copy-done.1 = f32[3,25,32,256]{3,2,1,0:T(8,128)S(1)} copy-done((f32[3,25,32,256]{3,2,1,0:T(8,128)S(1)}, f32[3,25,32,256]{3,2,1,0:T(8,128)}, u32[]{:S(2)}) %copy-start.1) | copy-done | bytes 2457624
  25.2 0.0 copy-start.3
  25.2 1.7 %copy-done.3 = f32[3,25,32,256]{3,2,1,0:T(8,128)S(1)} copy-done((f32[3,25,32,256]{3,2,1,0:T(8,128)S(1)}, f32[3,25,32,256]{3,2,1,0:T(8,128)}, u32[]{:S(2)}) %copy-start.3) | copy-done | bytes 2457624
  26.9 9.5 %sweeps.1 = (f32[3,25,32,256]{3,2,1,0:T(8,128)S(1)}, f32[1,6]{1,0:T(1,128)}, f32[32,128]{1,0:T(8,128)}) custom-call(f32[3,8]{1,0:T(4,128)S(1)} %bitcast.28, s32[16]{0:T(128)S(1)} %copy-done.10, s32[2,8]{1,0:T(2,128)S(1)} %copy-done.11, f32[16,3]{1,0:T(8,128)S(1)} %bitcast.26, f32[25,32,256]{2,1,0:T(8,128)S(1)} %get-tuple-element.16.lame_ref, ...), custom_call_target="tpu_custom_call" | custom-call | flops 26214400 | bytes 5242880 | tf_op jit(solution)/shard_map/sweeps/pallas_call | solution.py:592
  36.4 0.0 copy-start.4
  36.4 1.4 %copy-done.4 = f32[3,25,32,256]{3,2,1,0:T(8,128)} copy-done((f32[3,25,32,256]{3,2,1,0:T(8,128)}, f32[3,25,32,256]{3,2,1,0:T(8,128)S(1)}, u32[]{:S(2)}) %copy-start.4) | copy-done | bytes 2457624
  37.9 5.0 %all-to-all-start.1 = ((f32[32,1,128]{2,1,0:T(1,128)}), f32[32,1,128]{2,1,0:T(1,128)S(1)}, u32[]{:S(2)}, u32[]{:S(2)}) async-start(f32[32,1,128]{2,1,0:T(1,128)} %bitcast.12), calls=%async_computation.1 | async-start | bytes 32768 | tf_op jit(solution)/shard_map/all_to_all | solution.py:607
  42.9 0.0 copy-start.5
  42.9 1.7 %copy-done.5 = f32[3,25,32,256]{3,2,1,0:T(8,128)S(1)} copy-done((f32[3,25,32,256]{3,2,1,0:T(8,128)S(1)}, f32[3,25,32,256]{3,2,1,0:T(8,128)}, u32[]{:S(2)}) %copy-start.5) | copy-done | bytes 2457624
  44.6 0.0 copy-start.12
  44.6 0.7 %copy-done.12 = f32[1,6]{1,0:T(1,128)S(1)} copy-done((f32[1,6]{1,0:T(1,128)S(1)}, f32[1,6]{1,0:T(1,128)}, u32[]{:S(2)}) %copy-start.12) | copy-done | bytes 48
  45.2 5.3 %stress.1 = f32[6,1024,128]{2,1,0:T(8,128)} custom-call(f32[1,6]{1,0:T(1,128)S(1)} %copy-done.12, f32[25,32,256]{2,1,0:T(8,128)S(1)} %get-tuple-element.16.lame_ref, f32[25,32,256]{2,1,0:T(8,128)S(1)} %get-tuple-element.17.shear_ref, f32[3,25,32,256]{3,2,1,0:T(8,128)S(1)} %copy-done.5), custom_call_target="tpu_custom_call" | custom-call | flops 13107200 | bytes 5242880 | tf_op jit(solution)/shard_map/stress/pallas_call | solution.py:611
  50.6 0.0 all-to-all-done.1
  50.6 0.0 copy-start.13
  50.6 0.6 %copy-done.13 = f32[32,1,128]{2,1,0:T(1,128)} copy-done((f32[32,1,128]{2,1,0:T(1,128)}, f32[32,1,128]{2,1,0:T(1,128)S(1)}, u32[]{:S(2)}) %copy-start.13) | copy-done | bytes 16408
  51.2 1.3 %nodes.1 = (f32[1,6]{1,0:T(1,128)}, f32[1,3]{1,0:T(1,128)}, f32[1,108]{1,0:T(1,128)}) custom-call(f32[32,128]{1,0:T(8,128)} %bitcast.30), custom_call_target="tpu_custom_call" | custom-call | tf_op jit(solution)/shard_map/nodes/pallas_call | solution.py:631
  (1 shorter events, 0.0 us)
Async XLA Ops:
  0.6 22.9 %copy-start.10 = (s32[16]{0:T(128)S(1)}, s32[16]{0:T(128)}, u32[]{:S(2)}) copy-start(s32[16]{0:T(128)} %rve_element.3) | copy-start | bytes 196
  0.6 22.9 %copy-start.11 = (s32[2,8]{1,0:T(2,128)S(1)}, s32[2,8]{1,0:T(2,128)}, u32[]{:S(2)}) copy-start(s32[2,8]{1,0:T(2,128)} %connectivity.1) | copy-start | bytes 196
  2.1 10.9 %collective-permute-start = (f32[384,128]{1,0:T(8,128)S(1)}, f32[384,128]{1,0:T(8,128)S(1)}, u32[]{:S(2)}, u32[]{:S(2)}) collective-permute-start(f32[384,128]{1,0:T(8,128)S(1)} %pad_maximum_fusion), channel_id=1, source_target_pairs={{0,1},{1,0},{2,3},{3,2},{4,5},{5,4},{6,7},{7,6},{8,9},{9,8},{10,11... | collective-permute-start | bytes 589832 | tf_op jit(solution)/shard_map/ppermute | solution.py:542
  6.4 17.1 %all-to-all-start = ((f32[16,1,3]{2,1,0:T(1,128)}), f32[16,1,3]{2,1,0:T(1,128)S(1)}, u32[]{:S(2)}, u32[]{:S(2)}) async-start(f32[16,1,3]{2,1,0:T(1,128)} %broadcast_in_dim.15), calls=%async_computation | async-start | bytes 16384 | tf_op jit(solution)/shard_map/all_to_all | solution.py:525
  13.0 1.0 %copy-start.6 = (f32[1,32,4096]{2,1,0:T(8,128)S(1)}, f32[1,32,4096]{2,1,0:T(8,128)}, u32[]{:S(2)}) copy-start(f32[1,32,4096]{2,1,0:T(8,128)} %param.12) | copy-start | bytes 1572868
  14.0 1.0 %copy-start.7 = (s32[1,32,4096]{2,1,0:T(8,128)S(1)}, s32[1,32,4096]{2,1,0:T(8,128)}, u32[]{:S(2)}) copy-start(s32[1,32,4096]{2,1,0:T(8,128)} %param.13) | copy-start | bytes 1572868
  15.1 0.7 %copy-start.8 = (s32[2,8,8]{2,1,0:T(8,128)S(1)}, s32[2,8,8]{2,1,0:T(8,128)}, u32[]{:S(2)}) copy-start(s32[2,8,8]{2,1,0:T(8,128)} %block_slot.1) | copy-start | bytes 1540
  15.8 0.7 %copy-start.9 = (s32[16]{0:T(128)S(1)}, s32[16]{0:T(128)}, u32[]{:S(2)}) copy-start(s32[16]{0:T(128)} %rve_element.3) | copy-start | bytes 196
  20.6 1.4 %copy-start = (f32[3,25,32,256]{3,2,1,0:T(8,128)}, f32[3,25,32,256]{3,2,1,0:T(8,128)S(1)}, u32[]{:S(2)}) copy-start(f32[3,25,32,256]{3,2,1,0:T(8,128)S(1)} %get-tuple-element.18.dlame_ref) | copy-start | bytes 7372804
  22.0 1.5 %copy-start.2 = (f32[3,25,32,256]{3,2,1,0:T(8,128)}, f32[3,25,32,256]{3,2,1,0:T(8,128)S(1)}, u32[]{:S(2)}) copy-start(f32[3,25,32,256]{3,2,1,0:T(8,128)S(1)} %get-tuple-element.19.dshear_ref) | copy-start | bytes 7372804
  23.5 1.7 %copy-start.1 = (f32[3,25,32,256]{3,2,1,0:T(8,128)S(1)}, f32[3,25,32,256]{3,2,1,0:T(8,128)}, u32[]{:S(2)}) copy-start(f32[3,25,32,256]{3,2,1,0:T(8,128)} %copy-done) | copy-start | bytes 7372804
  25.2 1.7 %copy-start.3 = (f32[3,25,32,256]{3,2,1,0:T(8,128)S(1)}, f32[3,25,32,256]{3,2,1,0:T(8,128)}, u32[]{:S(2)}) copy-start(f32[3,25,32,256]{3,2,1,0:T(8,128)} %copy-done.2) | copy-start | bytes 7372804
  36.4 1.4 %copy-start.4 = (f32[3,25,32,256]{3,2,1,0:T(8,128)}, f32[3,25,32,256]{3,2,1,0:T(8,128)S(1)}, u32[]{:S(2)}) copy-start(f32[3,25,32,256]{3,2,1,0:T(8,128)S(1)} %get-tuple-element.22.w3_ref) | copy-start | bytes 7372804
  37.9 12.7 %all-to-all-start.1 = ((f32[32,1,128]{2,1,0:T(1,128)}), f32[32,1,128]{2,1,0:T(1,128)S(1)}, u32[]{:S(2)}, u32[]{:S(2)}) async-start(f32[32,1,128]{2,1,0:T(1,128)} %bitcast.12), calls=%async_computation.1 | async-start | bytes 32768 | tf_op jit(solution)/shard_map/all_to_all | solution.py:607
  42.9 1.7 %copy-start.5 = (f32[3,25,32,256]{3,2,1,0:T(8,128)S(1)}, f32[3,25,32,256]{3,2,1,0:T(8,128)}, u32[]{:S(2)}) copy-start(f32[3,25,32,256]{3,2,1,0:T(8,128)} %copy-done.4) | copy-start | bytes 7372804
  44.6 0.7 %copy-start.12 = (f32[1,6]{1,0:T(1,128)S(1)}, f32[1,6]{1,0:T(1,128)}, u32[]{:S(2)}) copy-start(f32[1,6]{1,0:T(1,128)} %get-tuple-element.13.strain_in) | copy-start | bytes 76
  50.6 0.6 %copy-start.13 = (f32[32,1,128]{2,1,0:T(1,128)}, f32[32,1,128]{2,1,0:T(1,128)S(1)}, u32[]{:S(2)}) copy-start(f32[32,1,128]{2,1,0:T(1,128)S(1)} %all-to-all-done.1) | copy-start | bytes 49156

commit v3 on v2

--- a/solution.py
+++ b/solution.py
@@ -52,14 +52,20 @@
     return ref[spot(at, jj)]
 
 
-def load3(ref, at, jj):
-    return [ref[(c, *spot(at, jj))] for c in range(3)]
-
-
-def next_row(ref, c, at, jj):
+def load3(refs, at, jj):
+    return [load(ref, at, jj) for ref in refs]
+
+
+def next_row(ref, at, jj):
     if jj < 7:
-        return ref[(c, *spot(at, jj + 1))]
-    return pltpu.roll(ref[(c, *spot(at, 0))], 7, 0)
+        return load(ref, at, jj + 1)
+    return pltpu.roll(load(ref, at, 0), 7, 0)
+
+
+def prev_row(ref, at, jj):
+    if jj > 0:
+        return load(ref, at, jj - 1)
+    return pltpu.roll(load(ref, at, 7), 1, 0)
 
 
 def next_lane(x):
@@ -70,10 +76,19 @@
     return pltpu.roll(x, 2, 1)
 
 
-def stress_at(w_ref, at, jj, w, lame, shear, strain):
+def differences(ref, at, jj):
+    here = load(ref, at, jj)
+    return (
+        here - load(ref, at - 1, jj),
+        here - prev_row(ref, at, jj),
+        here - prev_lane(here),
+    )
+
+
+def stress_at(w_refs, at, jj, w, lame, shear, strain):
     w0, w1, w2 = w
-    n0, n1, n2 = load3(w_ref, at + 1, jj)
-    row0, row1, row2 = [next_row(w_ref, c, at, jj) for c in range(3)]
+    n0, n1, n2 = load3(w_refs, at + 1, jj)
+    row0, row1, row2 = [next_row(ref, at, jj) for ref in w_refs]
     lane0, lane1, lane2 = [next_lane(x) for x in w]
     e0 = (n0 - w0) + strain[0]
     e1 = (row1 - w1) + strain[1]
@@ -93,13 +108,13 @@
     )
 
 
-def sweep_plane(w_ref, lame_ref, shear_ref, carry_v, old, new, at, strain, update):
+def sweep_plane(w_refs, lame_ref, shear_ref, carry_v, old, new, at, strain, update):
     first = None
     row_xy = row_yy = row_yz = None
     for jj in range(8):
-        w = load3(w_ref, at, jj)
+        w = load3(w_refs, at, jj)
         stress = stress_at(
-            w_ref, at, jj, w, load(lame_ref, at, jj), load(shear_ref, at, jj), strain
+            w_refs, at, jj, w, load(lame_ref, at, jj), load(shear_ref, at, jj), strain
         )
         xx, yy, zz, yz, xz, xy = stress
         pxx, pxz, pxy = [carry_v[(old, c, *spot(0, jj)[1:])] for c in range(3)]
@@ -116,14 +131,14 @@
             update(jj, w, [r[0] - row_xy, r[1] - row_yy, r[2] - row_yz])
         row_xy, row_yy, row_yz = xy, yy, yz
     rows = [pltpu.roll(x, 1, 0) for x in (row_xy, row_yy, row_yz)]
-    update(0, load3(w_ref, at, 0), [x - y for x, y in zip(first, rows)])
-
-
-def carry_plane(w_ref, lame_ref, shear_ref, carry_v, at, strain):
+    update(0, load3(w_refs, at, 0), [x - y for x, y in zip(first, rows)])
+
+
+def carry_plane(w_refs, lame_ref, shear_ref, carry_v, at, strain):
     for jj in range(8):
-        w = load3(w_ref, at, jj)
+        w = load3(w_refs, at, jj)
         xx, yy, zz, yz, xz, xy = stress_at(
-            w_ref, at, jj, w, load(lame_ref, at, jj), load(shear_ref, at, jj), strain
+            w_refs, at, jj, w, load(lame_ref, at, jj), load(shear_ref, at, jj), strain
         )
         for c, x in enumerate((xx, xz, xy)):
             carry_v[(0, c, *spot(0, jj)[1:])] = x
@@ -176,76 +191,91 @@
 SHEAR_MEAN = 121
 
 
+def prepare_kernel(disp_hbm, stiff_hbm, mask_hbm, disp_ref, halo_ref, disp_v, ends_v, mask_v, sems):
+    groups = stiff_hbm.shape[0] // (8 * ROWS)
+    ends = [pl.ds((groups - 1) * (8 * ROWS), 8 * ROWS), pl.ds(0, 8 * ROWS)]
+    copies = [pltpu.make_async_copy(disp_hbm, disp_v, sems.at[0])]
+    for e in range(2):
+        copies += [
+            pltpu.make_async_copy(stiff_hbm.at[ends[e], :], ends_v.at[e], sems.at[1 + 2 * e]),
+            pltpu.make_async_copy(mask_hbm.at[ends[e], :], mask_v.at[e], sems.at[2 + 2 * e]),
+        ]
+    for copy in copies:
+        copy.start()
+    for copy in copies:
+        copy.wait()
+    disp_ref[...] = jnp.broadcast_to(disp_v[...], disp_ref.shape)
+    row = 0
+    for e, first in ((0, 8 - HALO), (1, 0)):
+        for field in (ends_v, mask_v):
+            for plane in range(first, first + HALO):
+                for q in range(4):
+                    x = field[e, native(plane, q), :]
+                    halo_ref[row : row + 8, :] = x.astype(jnp.float32)
+                    row += 8
+
+
 def material_kernel(
     grads,
-    rve_element,
-    block_slot,
-    stiff_hbm,
-    mask_hbm,
+    rve_hbm,
+    slot_hbm,
+    stiff_v,
+    mask_v,
     halo_ref,
     lame_ref,
     shear_ref,
-    dlame_ref,
-    dshear_ref,
     rows_ref,
-    stiff_v,
-    mask_v,
-    lame_in,
-    shear_in,
+    stiff_in,
+    mask_in,
+    rve_element,
+    block_slot,
     sems,
 ):
     copies = [
-        pltpu.make_async_copy(stiff_hbm, stiff_v, sems.at[0]),
-        pltpu.make_async_copy(mask_hbm, mask_v, sems.at[1]),
+        pltpu.make_async_copy(rve_hbm, rve_element, sems.at[0]),
+        pltpu.make_async_copy(slot_hbm, block_slot, sems.at[1]),
     ]
     for copy in copies:
         copy.start()
     planes = stiff_v.shape[0] // ROWS
     half = planes // 2
     depth = half + 2 * HALO
-    elem = rve_element[lax.axis_index("macro")]
     matrix = lane_matrix(False)
-    for copy in copies:
-        copy.wait()
-
-    acc_l = acc_m = jnp.zeros((8, 128), jnp.float32)
+
     for h in range(2):
         for at in range(depth):
             plane = at - HALO + h * half
             for q in range(4):
                 if 0 <= plane < planes:
                     stiff = stiff_v[native(plane, q), :]
-                    mask = mask_v[native(plane, q), :]
-                    shear = stiff * jnp.where(mask == 1, shear_base * yield_ratio, shear_base)
+                    mask = mask_v[native(plane, q), :].astype(jnp.float32)
                 else:
                     side, far = (0, plane + HALO) if plane < 0 else (1, plane - planes)
-                    base = (side * 2 * HALO + far) * ROWS + q
-                    stiff = halo_ref[pl.ds(base, 8, stride=4), :]
-                    shear = halo_ref[pl.ds(base + HALO * ROWS, 8, stride=4), :]
-                lame = lame_base * stiff
+                    base = (side * 2 * HALO + far) * ROWS + 8 * q
+                    stiff = halo_ref[base : base + 8, :]
+                    mask = halo_ref[base + HALO * ROWS : base + HALO * ROWS + 8, :]
                 place = (at, pl.ds(8 * q, 8), pl.ds(128 * h, 128))
-                lame_in[place] = lame
-                shear_in[place] = shear
-                if HALO <= at < HALO + half:
-                    acc_l = acc_l + lame
-                    acc_m = acc_m + shear
-
-    for source, target in ((lame_in, lame_ref), (shear_in, shear_ref)):
-        x = source[...].reshape(depth * ROWS, WIDE)
-        target[pl.ds(0, depth)] = permute_lanes(x, matrix, 3).reshape(depth, ROWS, WIDE)
-
-    def difference(t, _):
-        at = t + 1
-        for source, target in ((lame_ref, dlame_ref), (shear_ref, dshear_ref)):
-            for jj in range(8):
-                here = load(source, at, jj)
-                before = load(source, at, jj - 1) if jj else pltpu.roll(load(source, at, 7), 1, 0)
-                target[(0, *spot(at, jj))] = here - load(source, at - 1, jj)
-                target[(1, *spot(at, jj))] = here - before
-                target[(2, *spot(at, jj))] = here - prev_lane(here)
-        return 0
-
-    lax.fori_loop(0, depth - 1, difference, 0)
+                stiff_in[place] = stiff
+                mask_in[place] = mask
+
+    acc_l = acc_m = jnp.zeros((8, 128), jnp.float32)
+    for first in range(0, depth, 2):
+        count = min(2, depth - first)
+        shape = (count * ROWS, WIDE)
+        stiff = permute_lanes(stiff_in[first : first + count].reshape(shape), matrix, 2)
+        mask = permute_lanes(mask_in[first : first + count].reshape(shape), matrix, 1)
+        lame = lame_base * stiff
+        shear = jnp.where(mask == 1.0, (shear_base * yield_ratio) * stiff, shear_base * stiff)
+        lame_ref[first : first + count] = lame.reshape(count, ROWS, WIDE)
+        shear_ref[first : first + count] = shear.reshape(count, ROWS, WIDE)
+        for u in range(count):
+            if HALO <= first + u < HALO + half:
+                for jj in range(8):
+                    acc_l = acc_l + load(lame_ref, first + u, jj)
+                    acc_m = acc_m + load(shear_ref, first + u, jj)
+    for copy in copies:
+        copy.wait()
+    elem = rve_element[lax.axis_index("macro")]
 
     scale = 1.0 / float(EDGE * EDGE * EDGE)
     lame, shear = total(acc_l) * scale, total(acc_m) * scale
@@ -286,14 +316,19 @@
     gathered,
     lame_ref,
     shear_ref,
-    dlame_ref,
-    dshear_ref,
     rows_ref,
-    w3_ref,
+    w30_ref,
+    w31_ref,
+    w32_ref,
     strain_ref,
+    strain_out,
     packet_ref,
-    w1_v,
-    w2_v,
+    w10_v,
+    w11_v,
+    w12_v,
+    w20_v,
+    w21_v,
+    w22_v,
     carry_v,
 ):
     half = lame_ref.shape[0] - 2 * HALO - MARGIN
@@ -317,6 +352,10 @@
     ]
     for c in range(6):
         strain_ref[0, c] = strain[c]
+        strain_out[8 * c : 8 * c + 8, :] = jnp.full((8, 128), strain[c], jnp.float32)
+    w1_v = [w10_v, w11_v, w12_v]
+    w2_v = [w20_v, w21_v, w22_v]
+    w3_v = [w30_ref, w31_ref, w32_ref]
 
     scale1 = gain1 * gain2 * precond / centre
     strain1 = [scale1 * e for e in strain]
@@ -328,15 +367,15 @@
         for u in range(step1):
             at = t * step1 + 1 + u
             for jj in range(8):
-                l0, l1, l2 = load3(dlame_ref, at, jj)
-                m0, m1, m2 = load3(dshear_ref, at, jj)
-                w1_v[(0, *spot(at, jj))] = (
+                l0, l1, l2 = differences(lame_ref, at, jj)
+                m0, m1, m2 = differences(shear_ref, at, jj)
+                w1_v[0][spot(at, jj)] = (
                     trace1 * l0 + twice1[0] * m0 + (strain1[5] * m1 + strain1[4] * m2)
                 )
-                w1_v[(1, *spot(at, jj))] = (
+                w1_v[1][spot(at, jj)] = (
                     trace1 * l1 + twice1[1] * m1 + (strain1[5] * m0 + strain1[3] * m2)
                 )
-                w1_v[(2, *spot(at, jj))] = (
+                w1_v[2][spot(at, jj)] = (
                     trace1 * l2 + twice1[2] * m2 + (strain1[4] * m0 + strain1[3] * m1)
                 )
         return 0
@@ -354,7 +393,7 @@
 
             def update(jj, w, r):
                 for c in range(3):
-                    w2_v[(c, *spot(at, jj))] = ratio1 * w[c] + r[c]
+                    w2_v[c][spot(at, jj)] = ratio1 * w[c] + r[c]
 
             sweep_plane(
                 w1_v, lame_ref, shear_ref, carry_v, u, (u + 1) % step2, at, strain2, update
@@ -376,7 +415,7 @@
             def update(jj, w, r):
                 old = load3(w1_v, at, jj)
                 for c in range(3):
-                    w3_ref[(c, *spot(at, jj))] = (ratio2 * w[c] - ratio3 * old[c]) + r[c]
+                    w3_v[c][spot(at, jj)] = (ratio2 * w[c] - ratio3 * old[c]) + r[c]
 
             sweep_plane(
                 w2_v, lame_ref, shear_ref, carry_v, u, (u + 1) % step3, at, strain3, update
@@ -389,9 +428,9 @@
         bulk, a0, a1, a2, a3, a4, a5 = acc
         at = t + HALO
         for jj in range(8):
-            w0, w1, w2 = load3(w3_ref, at, jj)
-            l0, l1, l2 = load3(dlame_ref, at, jj)
-            m0, m1, m2 = load3(dshear_ref, at, jj)
+            w0, w1, w2 = load3(w3_v, at, jj)
+            l0, l1, l2 = differences(lame_ref, at, jj)
+            m0, m1, m2 = differences(shear_ref, at, jj)
             bulk = bulk + (l0 * w0 + l1 * w1 + l2 * w2)
             a0 = a0 + m0 * w0
             a1 = a1 + m1 * w1
@@ -434,14 +473,18 @@
     strain_in,
     lame_ref,
     shear_ref,
-    w3_ref,
+    w30_ref,
+    w31_ref,
+    w32_ref,
     stress_ref,
     out_v,
     work_v,
+    turn_v,
     sem,
 ):
     half = lame_ref.shape[0] - 2 * HALO - MARGIN
-    strain = [strain_in[0, c] for c in range(6)]
+    w3_v = [w30_ref, w31_ref, w32_ref]
+    strain = [strain_in[8 * c : 8 * c + 8, :] for c in range(6)]
     matrix = lane_matrix(True)
     copies = []
     for first in range(0, half, GROUP):
@@ -450,42 +493,58 @@
             at = first + u + HALO
             for jj in range(8):
                 stress = stress_at(
-                    w3_ref,
+                    w3_v,
                     at,
                     jj,
-                    load3(w3_ref, at, jj),
+                    load3(w3_v, at, jj),
                     load(lame_ref, at, jj),
                     load(shear_ref, at, jj),
                     strain,
                 )
                 for c in range(6):
-                    work_v[(slot, u, c, *spot(0, jj)[1:])] = stress[c]
-        x = work_v[slot].reshape(GROUP * 6 * ROWS, WIDE)
-        y = permute_lanes(x, matrix, 2)
-        for u in range(GROUP):
+                    work_v[(slot, c, u, *spot(0, jj)[1:])] = stress[c]
+        for c in range(6):
+            y = permute_lanes(work_v[slot, c].reshape(GROUP * ROWS, WIDE), matrix, 2)
+            for u in range(GROUP):
+                for q in range(4):
+                    row = (u * 4 + q) * 8
+                    for h in range(2):
+                        s = (first + u + h * half) % 8
+                        turn_v[h, c, pl.ds(s * TURN_S + q * 8 * TURN_R, 8, stride=TURN_R), :] = y[
+                            row : row + 8, 128 * h : 128 * h + 128
+                        ]
+        done = []
+        if half % 8 == 0 and (first + GROUP) % 8 == 0:
+            done = [((first + GROUP) // 8 - 1 + h * (half // 8), h) for h in range(2)]
+        elif half % 8 and first + GROUP == half:
+            done = [(0, None)]
+        for group, h in done:
             for c in range(6):
                 for q in range(4):
-                    row = ((u * 6 + c) * 4 + q) * 8
-                    for h in range(2):
-                        plane = first + u + h * half
-                        out_v[c, native(plane, q), :] = y[row : row + 8, 128 * h : 128 * h + 128]
-        done = []
-        if half % 8 == 0 and (first + GROUP) % 8 == 0:
-            done = [(first + GROUP) // 8 - 1 + h * (half // 8) for h in range(2)]
-        elif first + GROUP == half:
-            done = range(2 * half // 8)
-        if done:
-            for group in done:
-                span = pl.ds(group * (8 * ROWS), 8 * ROWS)
-                copy = pltpu.make_async_copy(
-                    out_v.at[:, span, :], stress_ref.at[:, span, :], sem.at[len(copies)]
-                )
-                copy.start()
-                copies.append(copy)
+                    for r in range(8):
+                        row = group * (8 * ROWS) + (4 * r + q) * 8
+                        start = (q * 8 + r) * TURN_R
+                        if h is None:
+                            low = turn_v[0, c, pl.ds(start, 8, stride=TURN_S), :]
+                            high = turn_v[1, c, pl.ds(start, 8, stride=TURN_S), :]
+                            sub = lax.broadcasted_iota(jnp.int32, (8, 128), 0)
+                            out_v[c, row : row + 8, :] = jnp.where(sub < half, low, high)
+                        else:
+                            out_v[c, row : row + 8, :] = turn_v[
+                                h, c, pl.ds(start, 8, stride=TURN_S), :
+                            ]
+            span = pl.ds(group * (8 * ROWS), 8 * ROWS)
+            copy = pltpu.make_async_copy(
+                out_v.at[:, span, :], stress_ref.at[:, span, :], sem.at[len(copies)]
+            )
+            copy.start()
+            copies.append(copy)
     for copy in copies:
         copy.wait()
 
 
+TURN_R = 3
+TURN_S = TURN_R * ROWS + 1
 STEP = 3
 GROUP = 4
 MARGIN = 3
@@ -522,46 +581,21 @@
     assert rve_count == 1 and nodal_disp.shape[0] == 1
     assert planes % 8 == 0 and plane_size == EDGE * EDGE
 
-    gathered = lax.all_to_all(
-        jnp.broadcast_to(nodal_disp, (macro_size, 3)),
-        "macro",
-        split_axis=0,
-        concat_axis=0,
-        tiled=True,
-    )
-
-    def rim(first):
-        stiff = lax.slice_in_dim(stiffness[0], first, first + HALO, axis=0)
-        mask = lax.slice_in_dim(yielded_mask[0], first, first + HALO, axis=0)
-        shear = shear_base * stiff * jnp.where(mask == 1, yield_ratio, 1.0)
-        return jnp.stack([stiff, shear]).reshape(2 * HALO * ROWS, 128)
-
-    upper, lower = rim(planes - HALO), rim(0)
-    if vox_size == 2:
-        both = jnp.concatenate([upper, lower], axis=0)
-        halo = lax.ppermute(both, "vox", [(0, 1), (1, 0)])
-    else:
-        forward = [(i, (i + 1) % vox_size) for i in range(vox_size)]
-        backward = [(t, s) for s, t in forward]
-        halo = jnp.concatenate(
-            [lax.ppermute(upper, "vox", forward), lax.ppermute(lower, "vox", backward)], axis=0
-        )
-
     def flat(field):
         parted = field.reshape(planes // 8, 8, ROWS, 128)
         return parted.transpose(0, 2, 1, 3).reshape(planes * ROWS, 128)
 
     smem = pl.BlockSpec(memory_space=pltpu.SMEM)
     vmem = pl.BlockSpec(memory_space=pltpu.VMEM)
+    hbm = pl.BlockSpec(memory_space=pltpu.HBM)
     anywhere = pl.BlockSpec(memory_space=pl.ANY)
     mib = 1024 * 1024
     f32 = jnp.float32
-    grads = weighted_shape_gradients[0]
     half = planes // 2
     depth = half + 2 * HALO + MARGIN
-    scalar = jax.ShapeDtypeStruct((depth, ROWS, WIDE), f32)
-    vector = jax.ShapeDtypeStruct((3, depth, ROWS, WIDE), f32)
-    native_field = pltpu.VMEM((planes * ROWS, 128), f32)
+    packed = 4 * HALO * ROWS
+    layer = jax.ShapeDtypeStruct((depth, ROWS, WIDE), f32)
+    field = pltpu.VMEM((depth, ROWS, WIDE), f32)
     half_field = pltpu.VMEM((half + 2 * HALO, ROWS, WIDE), f32)
 
     def cost(flops, size):
@@ -571,38 +605,74 @@
             transcendentals=0,
         )
 
-    lame, shear, dlame, dshear, rows = pl.pallas_call(
+    disp, rims = pl.pallas_call(
+        prepare_kernel,
+        out_shape=(
+            jax.ShapeDtypeStruct((macro_size, 3), f32),
+            jax.ShapeDtypeStruct((packed, 128), f32),
+        ),
+        in_specs=[hbm] * 3,
+        out_specs=(vmem,) * 2,
+        scratch_shapes=[
+            pltpu.VMEM((1, 3), f32),
+            pltpu.VMEM((2, 8 * ROWS, 128), f32),
+            pltpu.VMEM((2, 8 * ROWS, 128), jnp.int32),
+            pltpu.SemaphoreType.DMA((5,)),
+        ],
+        compiler_params=pltpu.CompilerParams(vmem_limit_bytes=56 * mib),
+        cost_estimate=cost(10**4, 1),
+        name="prepare",
+    )(nodal_disp, flat(stiffness), flat(yielded_mask))
+
+    if vox_size == 2:
+        halo = lax.ppermute(rims, "vox", [(0, 1), (1, 0)])
+    else:
+        forward = [(i, (i + 1) % vox_size) for i in range(vox_size)]
+        backward = [(t, s) for s, t in forward]
+        halo = jnp.concatenate(
+            [
+                lax.ppermute(rims[: packed // 2], "vox", forward),
+                lax.ppermute(rims[packed // 2 :], "vox", backward),
+            ],
+            axis=0,
+        )
+    gathered = lax.all_to_all(disp, "macro", split_axis=0, concat_axis=0, tiled=True)
+
+    grads = weighted_shape_gradients[0]
+    lame, shear, rows = pl.pallas_call(
         material_kernel,
-        out_shape=(scalar, scalar, vector, vector, jax.ShapeDtypeStruct((8, 128), f32)),
-        in_specs=[smem, smem, smem, anywhere, anywhere, vmem],
-        out_specs=(vmem,) * 5,
+        out_shape=(layer, layer, jax.ShapeDtypeStruct((8, 128), f32)),
+        in_specs=[smem, hbm, hbm, vmem, vmem, vmem],
+        out_specs=(vmem,) * 3,
         scratch_shapes=[
-            native_field,
-            pltpu.VMEM((planes * ROWS, 128), jnp.int32),
             half_field,
             half_field,
+            pltpu.SMEM(rve_element.shape, jnp.int32),
+            pltpu.SMEM(block_slot.shape, jnp.int32),
             pltpu.SemaphoreType.DMA((2,)),
         ],
-        compiler_params=pltpu.CompilerParams(vmem_limit_bytes=16 * mib),
-        cost_estimate=cost(100, 40),
+        compiler_params=pltpu.CompilerParams(vmem_limit_bytes=8 * mib),
+        cost_estimate=cost(10**4, 1),
         name="material",
     )(grads, rve_element, block_slot, flat(stiffness), flat(yielded_mask), halo)
 
-    field = pltpu.VMEM((3, depth, ROWS, WIDE), f32)
-    w3, strain, packet = pl.pallas_call(
+    *w3, strain, strain_rows, packet = pl.pallas_call(
         sweep_kernel,
         out_shape=(
-            vector,
+            layer,
+            layer,
+            layer,
             jax.ShapeDtypeStruct((1, 6), f32),
+            jax.ShapeDtypeStruct((48, 128), f32),
             jax.ShapeDtypeStruct((everywhere, 128), f32),
         ),
-        in_specs=[smem] * 4 + [vmem] * 5,
-        out_specs=(vmem, smem, vmem),
-        scratch_shapes=[field, field, pltpu.VMEM((STEP, 3, ROWS, WIDE), f32)],
-        compiler_params=pltpu.CompilerParams(vmem_limit_bytes=16 * mib),
-        cost_estimate=cost(200, 40),
+        in_specs=[smem] * 4 + [vmem] * 3,
+        out_specs=(vmem, vmem, vmem, smem, vmem, vmem),
+        scratch_shapes=[field] * 6 + [pltpu.VMEM((STEP, 3, ROWS, WIDE), f32)],
+        compiler_params=pltpu.CompilerParams(vmem_limit_bytes=12 * mib),
+        cost_estimate=cost(2 * 10**4, 1),
         name="sweeps",
-    )(grads, rve_element, connectivity, gathered, lame, shear, dlame, dshear, rows)
+    )(grads, rve_element, connectivity, gathered, lame, shear, rows)
 
     packets = lax.all_to_all(
         packet, ("vox", "macro"), split_axis=0, concat_axis=0, tiled=True
@@ -611,17 +681,18 @@
     stress = pl.pallas_call(
         stress_kernel,
         out_shape=jax.ShapeDtypeStruct((6, planes * ROWS, 128), f32),
-        in_specs=[smem, vmem, vmem, vmem],
-        out_specs=anywhere,
+        in_specs=[vmem] * 6,
+        out_specs=hbm,
         scratch_shapes=[
             pltpu.VMEM((6, planes * ROWS, 128), f32),
-            pltpu.VMEM((2, GROUP, 6, ROWS, WIDE), f32),
+            pltpu.VMEM((2, 6, GROUP, ROWS, WIDE), f32),
+            pltpu.VMEM((2, 6, 8 * TURN_S, 128), f32),
             pltpu.SemaphoreType.DMA((planes // 8,)),
         ],
-        compiler_params=pltpu.CompilerParams(vmem_limit_bytes=20 * mib),
-        cost_estimate=cost(100, 40),
+        compiler_params=pltpu.CompilerParams(vmem_limit_bytes=16 * mib),
+        cost_estimate=cost(10**4, 1),
         name="stress",
-    )(strain, lame, shear, w3)
+    )(strain_rows, lame, shear, *w3)
     voxel_stress = (
         stress.reshape(6, planes // 8, ROWS, 8, 128)
         .transpose(0, 1, 3, 2, 4)
@@ -637,6 +708,7 @@
         ),
         in_specs=[vmem],
         out_specs=(vmem, vmem, vmem),
+        compiler_params=pltpu.CompilerParams(vmem_limit_bytes=4 * mib),
         name="nodes",
     )(packets)
     return (voxel_stress, homogenized, strain, internal_node_force, tangent)

time: 53.1 us -> 40.3 us (0.76)
  local copies, waits for them, and re-layouts: 16.2 us -> 2.06 us
  waiting for transfers between devices: 0.01 us -> 7.59 us
  starting transfers between devices: 13.9 us -> 11.4 us
  Pallas kernels: 20.4 us -> 18.1 us
  other arithmetic: 1.25 us -> 0 us
    unnamed x29 -> x17, local copies, waits for them, and re-layouts: 14.8 us -> 2.06 us
    all_to_all x1, waiting for transfers between devices: 0.01 us -> 4.51 us  [on_device(): lax.all_to_all(disp, 'macro', split_axis=0, concat_axis=0, tiled=True)]
    all_to_all x1, waiting for transfers between devices: 0.01 us -> 3.08 us  [on_device(): lax.all_to_all(packet, ('vox', 'macro'), split_axis=0, concat_axis=0, til...]
    all_to_all x1, starting transfers between devices: 4.99 us -> 2.51 us  [on_device(): lax.all_to_all(packet, ('vox', 'macro'), split_axis=0, concat_axis=0, til...]
    pallas_call x1, Pallas kernels: 5.33 us -> 2.92 us  [on_device(): pl.pallas_call(stress_kernel, out_shape=jax.ShapeDtypeStruct((6, planes *...]
    broadcast_in_dim x1 -> x0, local copies, waits for them, and re-layouts: 1.25 us -> none  [on_device(): jnp.broadcast_to(nodal_disp, (macro_size, 3))]
    mul x1 -> x0, other arithmetic: 1.17 us -> none  [rim(): shear = shear_base * stiff * jnp.where(mask == 1, yield_ratio, 1.0)]
    pallas_call x2 -> x3, Pallas kernels: 13.7 us -> 14.6 us  [the longest x1 10.8 us: on_device(): pl.pallas_call(sweep_kernel, out_shape=(layer, layer, layer, jax.ShapeDty...]
  transfers between devices with their start and end apart: 3 -> 3, of which waited for: 0 -> 2; matrix products, arithmetic and copies ran while one was open for 4% -> 0% of each run, Pallas kernels for 18% -> 12%
where the time goes in v3:
time: 40.3 us; the launch traced here: 40 us
  Pallas kernels  18.1 us (45%)
  starting transfers between devices  11.4 us (28%)
  waiting for transfers between devices  7.59 us (19%)
  local copies, waits for them, and re-layouts  2.06 us (5%)
  between operations  0.8 us (2%)
    pallas_call x1, Pallas kernels, on_device(): pl.pallas_call(sweep_kernel, out_shape=(layer, layer, layer, jax.ShapeDty...  10.8 us
    all_to_all x1, starting transfers between devices, on_device(): lax.all_to_all(disp, 'macro', split_axis=0, concat_axis=0, tiled=True)  5.91 us
    all_to_all x1, waiting for transfers between devices, on_device(): lax.all_to_all(disp, 'macro', split_axis=0, concat_axis=0, tiled=True)  4.51 us
    all_to_all x1, waiting for transfers between devices, on_device(): lax.all_to_all(packet, ('vox', 'macro'), split_axis=0, concat_axis=0, til...  3.08 us
    ppermute x1, starting transfers between devices, on_device(): halo = lax.ppermute(rims, 'vox', [(0, 1), (1, 0)])  3.03 us
    pallas_call x1, Pallas kernels, on_device(): pl.pallas_call(stress_kernel, out_shape=jax.ShapeDtypeStruct((6, planes *...  2.92 us
    all_to_all x1, starting transfers between devices, on_device(): lax.all_to_all(packet, ('vox', 'macro'), split_axis=0, concat_axis=0, til...  2.51 us
    unnamed x17, local copies, waits for them, and re-layouts  2.06 us
  transfers between devices with their start and end apart: 3, of which 2 were waited for; matrix products, arithmetic and copies ran while one was open for 0% of the time, Pallas kernels for 12%

profile of v3, /device:TPU:0, one launch (start us, length us, event | category | flops | bytes accessed | tf_op | source)
XLA Modules:
  0.0 40.0 jit_solution(15919958653124248359)
XLA Ops:
  0.6 0.0 copy-start.3
  0.6 0.0 copy-start.2
  0.7 0.0 copy-start.7
  0.7 0.0 copy-start.6
  0.7 0.0 copy-start.4
  0.7 2.0 %prepare.1 = (f32[16,3]{1,0:T(8,128)}, f32[384,128]{1,0:T(8,128)}) custom-call(f32[1,3]{1,0:T(1,128)} %disp_hbm.1, f32[1024,128]{1,0:T(8,128)} %bitcast.30, s32[1024,128]{1,0:T(8,128)} %bitcast.32), custom_call_target="tpu_custom_call" | custom-call | flops 1310720000 | bytes 131072 | tf_op jit(solution)/shard_map/prepare/pallas_call | solution.py:608
  2.7 0.0 copy-start.5
  2.7 3.0 %collective-permute-start = (f32[384,128]{1,0:T(8,128)}, f32[384,128]{1,0:T(8,128)S(1)}, u32[]{:S(2)}, u32[]{:S(2)}) collective-permute-start(f32[384,128]{1,0:T(8,128)} %get-tuple-element.20), channel_id=1, source_target_pairs={{0,1},{1,0},{2,3},{3,2},{4,5},{5,4},{6,7},{7,6},{8,9},{9,8},{10,11... | collective-permute-start | bytes 589832 | tf_op jit(solution)/shard_map/ppermute | solution.py:628
  5.8 5.9 %all-to-all-start = ((f32[16,1,3]{2,1,0:T(1,128)}), f32[16,1,3]{2,1,0:T(1,128)S(1)}, u32[]{:S(2)}, u32[]{:S(2)}) async-start(f32[16,1,3]{2,1,0:T(1,128)} %bitcast.35), calls=%async_computation | async-start | bytes 16384 | tf_op jit(solution)/shard_map/all_to_all | solution.py:639
  11.7 0.0 copy-done.7
  11.7 0.0 collective-permute-done.halo_ref
  11.7 0.0 copy-done.3
  11.7 0.0 copy-done.2
  11.7 0.0 copy-done.6
  11.7 0.0 copy-done.4
  11.8 1.8 %material.1 = (f32[25,32,256]{2,1,0:T(8,128)S(1)}, f32[25,32,256]{2,1,0:T(8,128)S(1)}, f32[8,128]{1,0:T(8,128)S(1)}) custom-call(f32[3,8]{1,0:T(4,128)S(1)} %bitcast.28, s32[16]{0:T(128)S(1)} %copy-done.6, s32[2,8,8]{2,1,0:T(8,128)S(1)} %copy-done.4, f32[1024,128]{1,0:T(8,128)S(1)} %bitcast.31, s32[1024,128]{1,0:T(8,128)S(1)} %bitcast.33, ...), custom_call_target="tpu_custom_call" | custom-call | flops 1310720000 | bytes 131072 | tf_op jit(solution)/shard_map/material/pallas_call | solution.py:642
  13.6 4.5 %all-to-all-done = f32[16,1,3]{2,1,0:T(1,128)S(1)} async-done(((f32[16,1,3]{2,1,0:T(1,128)}), f32[16,1,3]{2,1,0:T(1,128)S(1)}, u32[]{:S(2)}, u32[]{:S(2)}) %all-to-all-start) | async-done | bytes 224 | tf_op jit(solution)/shard_map/all_to_all | solution.py:639
  18.1 0.0 copy-done.5
  18.1 10.8 %sweeps.1 = (f32[25,32,256]{2,1,0:T(8,128)S(1)}, f32[25,32,256]{2,1,0:T(8,128)S(1)}, f32[25,32,256]{2,1,0:T(8,128)S(1)}, f32[1,6]{1,0:T(1,128)}, f32[48,128]{1,0:T(8,128)S(1)}, /*index=5*/f32[32,128]{1,0:T(8,128)}) custom-call(f32[3,8]{1,0:T(4,128)S(1)} %bitcast.29, s32[16]{0:T(128)S(1)} %copy-done.6, s32[2,8]{1,0:T(2,128)S(1)} %copy-done.5, ...), custom_call_target="tpu_custom_call" | custom-call | flops 2621440000 | bytes 131072 | tf_op jit(solution)/shard_map/sweeps/pallas_call | solution.py:659
  28.9 0.0 copy-start
  28.9 0.9 %copy-done = f32[25,32,256]{2,1,0:T(8,128)} copy-done((f32[25,32,256]{2,1,0:T(8,128)}, f32[25,32,256]{2,1,0:T(8,128)S(1)}, u32[]{:S(2)}) %copy-start) | copy-done | bytes 819224
  29.8 2.5 %all-to-all-start.1 = ((f32[32,1,128]{2,1,0:T(1,128)}), f32[32,1,128]{2,1,0:T(1,128)S(1)}, u32[]{:S(2)}, u32[]{:S(2)}) async-start(f32[32,1,128]{2,1,0:T(1,128)} %bitcast.16), calls=%async_computation.1 | async-start | bytes 32768 | tf_op jit(solution)/shard_map/all_to_all | solution.py:677
  32.3 0.0 copy-start.1
  32.3 1.1 %copy-done.1 = f32[25,32,256]{2,1,0:T(8,128)S(1)} copy-done((f32[25,32,256]{2,1,0:T(8,128)S(1)}, f32[25,32,256]{2,1,0:T(8,128)}, u32[]{:S(2)}) %copy-start.1) | copy-done | bytes 819224
  33.4 2.9 %stress.1 = f32[6,1024,128]{2,1,0:T(8,128)} custom-call(f32[48,128]{1,0:T(8,128)S(1)} %get-tuple-element.24.strain_in, f32[25,32,256]{2,1,0:T(8,128)S(1)} %get-tuple-element.21.lame_ref, f32[25,32,256]{2,1,0:T(8,128)S(1)} %get-tuple-element.22.shear_ref, f32[25,32,256]{2,1,0:T(8,128)S(1)} %get-tuple-element.25.w30_ref, ...), custom_call_target="tpu_custom_call" | custom-call | flops 1310720000 | bytes 131072 | tf_op jit(solution)/shard_map/stress/pallas_call | solution.py:681
  36.3 3.1 %all-to-all-done.1 = f32[32,1,128]{2,1,0:T(1,128)S(1)} async-done(((f32[32,1,128]{2,1,0:T(1,128)}), f32[32,1,128]{2,1,0:T(1,128)S(1)}, u32[]{:S(2)}, u32[]{:S(2)}) %all-to-all-start.1) | async-done | bytes 16416 | tf_op jit(solution)/shard_map/all_to_all | solution.py:677
  39.4 0.6 %nodes.1 = (f32[1,6]{1,0:T(1,128)}, f32[1,3]{1,0:T(1,128)}, f32[1,108]{1,0:T(1,128)}) custom-call(f32[32,128]{1,0:T(8,128)S(1)} %bitcast.26), custom_call_target="tpu_custom_call" | custom-call | tf_op jit(solution)/shard_map/nodes/pallas_call | solution.py:702
  (1 shorter events, 0.0 us)
Async XLA Ops:
  0.6 11.1 %copy-start.3 = (s32[1,32,4096]{2,1,0:T(8,128)S(1)}, s32[1,32,4096]{2,1,0:T(8,128)}, u32[]{:S(2)}) copy-start(s32[1,32,4096]{2,1,0:T(8,128)} %param.13) | copy-start | bytes 1572868
  0.6 11.1 %copy-start.2 = (f32[1,32,4096]{2,1,0:T(8,128)S(1)}, f32[1,32,4096]{2,1,0:T(8,128)}, u32[]{:S(2)}) copy-start(f32[1,32,4096]{2,1,0:T(8,128)} %param.12) | copy-start | bytes 1572868
  0.7 11.0 %copy-start.7 = (f32[1,3,8]{2,0,1:T(1,128)S(1)}, f32[1,3,8]{2,0,1:T(1,128)}, u32[]{:S(2)}) copy-start(f32[1,3,8]{2,0,1:T(1,128)} %param.8) | copy-start | bytes 292
  0.7 11.1 %copy-start.6 = (s32[16]{0:T(128)S(1)}, s32[16]{0:T(128)}, u32[]{:S(2)}) copy-start(s32[16]{0:T(128)} %rve_element.1) | copy-start | bytes 196
  0.7 11.1 %copy-start.4 = (s32[2,8,8]{2,1,0:T(8,128)S(1)}, s32[2,8,8]{2,1,0:T(8,128)}, u32[]{:S(2)}) copy-start(s32[2,8,8]{2,1,0:T(8,128)} %slot_hbm.1) | copy-start | bytes 1540
  2.7 15.4 %copy-start.5 = (s32[2,8]{1,0:T(2,128)S(1)}, s32[2,8]{1,0:T(2,128)}, u32[]{:S(2)}) copy-start(s32[2,8]{1,0:T(2,128)} %connectivity.1) | copy-start | bytes 196
  2.7 9.0 %collective-permute-start = (f32[384,128]{1,0:T(8,128)}, f32[384,128]{1,0:T(8,128)S(1)}, u32[]{:S(2)}, u32[]{:S(2)}) collective-permute-start(f32[384,128]{1,0:T(8,128)} %get-tuple-element.20), channel_id=1, source_target_pairs={{0,1},{1,0},{2,3},{3,2},{4,5},{5,4},{6,7},{7,6},{8,9},{9,8},{10,11... | collective-permute-start | bytes 589832 | tf_op jit(solution)/shard_map/ppermute | solution.py:628
  5.8 12.3 %all-to-all-start = ((f32[16,1,3]{2,1,0:T(1,128)}), f32[16,1,3]{2,1,0:T(1,128)S(1)}, u32[]{:S(2)}, u32[]{:S(2)}) async-start(f32[16,1,3]{2,1,0:T(1,128)} %bitcast.35), calls=%async_computation | async-start | bytes 16384 | tf_op jit(solution)/shard_map/all_to_all | solution.py:639
  28.9 0.9 %copy-start = (f32[25,32,256]{2,1,0:T(8,128)}, f32[25,32,256]{2,1,0:T(8,128)S(1)}, u32[]{:S(2)}) copy-start(f32[25,32,256]{2,1,0:T(8,128)S(1)} %get-tuple-element.27.w32_ref) | copy-start | bytes 2457604
  29.8 9.7 %all-to-all-start.1 = ((f32[32,1,128]{2,1,0:T(1,128)}), f32[32,1,128]{2,1,0:T(1,128)S(1)}, u32[]{:S(2)}, u32[]{:S(2)}) async-start(f32[32,1,128]{2,1,0:T(1,128)} %bitcast.16), calls=%async_computation.1 | async-start | bytes 32768 | tf_op jit(solution)/shard_map/all_to_all | solution.py:677
  32.3 1.1 %copy-start.1 = (f32[25,32,256]{2,1,0:T(8,128)S(1)}, f32[25,32,256]{2,1,0:T(8,128)}, u32[]{:S(2)}) copy-start(f32[25,32,256]{2,1,0:T(8,128)} %copy-done) | copy-start | bytes 2457604

commit v4 on v3

--- a/solution.py
+++ b/solution.py
@@ -39,10 +39,6 @@
 gain1 = push1 * precond
 gain2 = push2 * precond
 
-def best_step(count, most):
-    return min(range(1, most + 1), key=lambda s: (-(-count // s) * s, -s))
-
-
 def spot(at, jj):
     half = (jj & 1) * 128
     return at, pl.ds(8 * (jj // 2), 8), pl.ds(half, 128)
@@ -54,12 +50,6 @@
 
 def load3(refs, at, jj):
     return [load(ref, at, jj) for ref in refs]
-
-
-def next_row(ref, at, jj):
-    if jj < 7:
-        return load(ref, at, jj + 1)
-    return pltpu.roll(load(ref, at, 0), 7, 0)
 
 
 def prev_row(ref, at, jj):
@@ -85,63 +75,54 @@
     )
 
 
-def stress_at(w_refs, at, jj, w, lame, shear, strain):
-    w0, w1, w2 = w
-    n0, n1, n2 = load3(w_refs, at + 1, jj)
-    row0, row1, row2 = [next_row(ref, at, jj) for ref in w_refs]
-    lane0, lane1, lane2 = [next_lane(x) for x in w]
-    e0 = (n0 - w0) + strain[0]
-    e1 = (row1 - w1) + strain[1]
-    e2 = (lane2 - w2) + strain[2]
-    g3 = (lane1 + row2) - (w1 + w2) + strain[3]
-    g4 = (lane0 + n2) - (w0 + w2) + strain[4]
-    g5 = (row0 + n1) - (w0 + w1) + strain[5]
-    bulk = lame * (e0 + e1 + e2)
-    twice = shear + shear
-    return (
-        bulk + twice * e0,
-        bulk + twice * e1,
-        bulk + twice * e2,
-        shear * g3,
-        shear * g4,
-        shear * g5,
-    )
-
-
-def sweep_plane(w_refs, lame_ref, shear_ref, carry_v, old, new, at, strain, update):
-    first = None
+def plane_stress(w_refs, at, lame_ref, shear_ref, lame_at, strain):
+    ahead = first = load3(w_refs, at, 0)
+    for jj in range(8):
+        w0, w1, w2 = w = ahead
+        ahead = load3(w_refs, at, jj + 1) if jj < 7 else [pltpu.roll(x, 7, 0) for x in first]
+        row0, row1, row2 = ahead
+        n0, n1, n2 = load3(w_refs, at + 1, jj)
+        lane0, lane1, lane2 = [next_lane(x) for x in w]
+        lame = load(lame_ref, lame_at, jj)
+        shear = load(shear_ref, lame_at, jj)
+        e0 = (n0 - w0) + strain[0]
+        e1 = (row1 - w1) + strain[1]
+        e2 = (lane2 - w2) + strain[2]
+        g3 = (lane1 + row2) - (w1 + w2) + strain[3]
+        g4 = (lane0 + n2) - (w0 + w2) + strain[4]
+        g5 = (row0 + n1) - (w0 + w1) + strain[5]
+        bulk = lame * (e0 + e1 + e2)
+        twice = shear + shear
+        yield jj, w, (
+            bulk + twice * e0,
+            bulk + twice * e1,
+            bulk + twice * e2,
+            shear * g3,
+            shear * g4,
+            shear * g5,
+        )
+
+
+def residual_plane(registers, carry_v, old, new):
+    begin = None
     row_xy = row_yy = row_yz = None
-    for jj in range(8):
-        w = load3(w_refs, at, jj)
-        stress = stress_at(
-            w_refs, at, jj, w, load(lame_ref, at, jj), load(shear_ref, at, jj), strain
-        )
+    for jj, w, stress in registers:
         xx, yy, zz, yz, xz, xy = stress
-        pxx, pxz, pxy = [carry_v[(old, c, *spot(0, jj)[1:])] for c in range(3)]
+        pxx, pxz, pxy = [load(carry_v.at[old], c, jj) for c in range(3)]
         for c, x in enumerate((xx, xz, xy)):
-            carry_v[(new, c, *spot(0, jj)[1:])] = x
+            carry_v[(new, *spot(c, jj))] = x
         r = [
             (xx - pxx) + (xz - prev_lane(xz)) + xy,
             (xy - pxy) + (yz - prev_lane(yz)) + yy,
             (xz - pxz) + (zz - prev_lane(zz)) + yz,
         ]
         if jj == 0:
-            first = r
+            begin = w, r
         else:
-            update(jj, w, [r[0] - row_xy, r[1] - row_yy, r[2] - row_yz])
+            yield jj, w, [r[0] - row_xy, r[1] - row_yy, r[2] - row_yz]
         row_xy, row_yy, row_yz = xy, yy, yz
     rows = [pltpu.roll(x, 1, 0) for x in (row_xy, row_yy, row_yz)]
-    update(0, load3(w_refs, at, 0), [x - y for x, y in zip(first, rows)])
-
-
-def carry_plane(w_refs, lame_ref, shear_ref, carry_v, at, strain):
-    for jj in range(8):
-        w = load3(w_refs, at, jj)
-        xx, yy, zz, yz, xz, xy = stress_at(
-            w_refs, at, jj, w, load(lame_ref, at, jj), load(shear_ref, at, jj), strain
-        )
-        for c, x in enumerate((xx, xz, xy)):
-            carry_v[(0, c, *spot(0, jj)[1:])] = x
+    yield 0, begin[0], [x - y for x, y in zip(begin[1], rows)]
 
 
 def target_lane(m):
@@ -329,9 +310,10 @@
     w20_v,
     w21_v,
     w22_v,
-    carry_v,
+    carry2_v,
+    carry3_v,
 ):
-    half = lame_ref.shape[0] - 2 * HALO - MARGIN
+    half = lame_ref.shape[0] - 2 * HALO
     elem = rve_element[lax.axis_index("macro")]
     nodes = [connectivity[elem, k] for k in range(8)]
     moves = [[gathered[n, a] for n in nodes] for a in range(3)]
@@ -361,74 +343,48 @@
     strain1 = [scale1 * e for e in strain]
     trace1 = strain1[0] + strain1[1] + strain1[2]
     twice1 = [2.0 * strain1[c] for c in range(3)]
-    step1 = best_step(half + 5, STEP)
-
-    def sweep1(t, _):
-        for u in range(step1):
-            at = t * step1 + 1 + u
-            for jj in range(8):
-                l0, l1, l2 = differences(lame_ref, at, jj)
-                m0, m1, m2 = differences(shear_ref, at, jj)
-                w1_v[0][spot(at, jj)] = (
-                    trace1 * l0 + twice1[0] * m0 + (strain1[5] * m1 + strain1[4] * m2)
-                )
-                w1_v[1][spot(at, jj)] = (
-                    trace1 * l1 + twice1[1] * m1 + (strain1[5] * m0 + strain1[3] * m2)
-                )
-                w1_v[2][spot(at, jj)] = (
-                    trace1 * l2 + twice1[2] * m2 + (strain1[4] * m0 + strain1[3] * m1)
-                )
-        return 0
-
-    lax.fori_loop(0, pl.cdiv(half + 5, step1), sweep1, 0)
-
     strain2 = [gain1 * gain2 * e for e in strain]
     ratio1 = (1.0 + keep1) / gain1
-    step2 = best_step(half + 3, STEP)
-    carry_plane(w1_v, lame_ref, shear_ref, carry_v, 1, strain2)
-
-    def sweep2(t, _):
-        for u in range(step2):
-            at = t * step2 + 2 + u
-
-            def update(jj, w, r):
-                for c in range(3):
-                    w2_v[c][spot(at, jj)] = ratio1 * w[c] + r[c]
-
-            sweep_plane(
-                w1_v, lame_ref, shear_ref, carry_v, u, (u + 1) % step2, at, strain2, update
-            )
-        return 0
-
-    lax.fori_loop(0, pl.cdiv(half + 3, step2), sweep2, 0)
-
     strain3 = [gain2 * e for e in strain]
     ratio2 = (1.0 + keep2) / gain2
     ratio3 = keep2 / (gain1 * gain2)
-    step3 = best_step(half + 1, STEP)
-    carry_plane(w2_v, lame_ref, shear_ref, carry_v, 2, strain3)
-
-    def sweep3(t, _):
-        for u in range(step3):
-            at = t * step3 + 3 + u
-
-            def update(jj, w, r):
-                old = load3(w1_v, at, jj)
-                for c in range(3):
-                    w3_v[c][spot(at, jj)] = (ratio2 * w[c] - ratio3 * old[c]) + r[c]
-
-            sweep_plane(
-                w2_v, lame_ref, shear_ref, carry_v, u, (u + 1) % step3, at, strain3, update
+
+    def sweep1(at):
+        for jj in range(8):
+            l0, l1, l2 = differences(lame_ref, at, jj)
+            m0, m1, m2 = differences(shear_ref, at, jj)
+            w1_v[0][spot(at, jj)] = (
+                trace1 * l0 + twice1[0] * m0 + (strain1[5] * m1 + strain1[4] * m2)
             )
-        return 0
-
-    lax.fori_loop(0, pl.cdiv(half + 1, step3), sweep3, 0)
-
-    def by_parts(t, acc):
+            w1_v[1][spot(at, jj)] = (
+                trace1 * l1 + twice1[1] * m1 + (strain1[5] * m0 + strain1[3] * m2)
+            )
+            w1_v[2][spot(at, jj)] = (
+                trace1 * l2 + twice1[2] * m2 + (strain1[4] * m0 + strain1[3] * m1)
+            )
+
+    def below(w_refs, at, carry, strain_here):
+        for jj, _, stress in plane_stress(w_refs, at, lame_ref, shear_ref, at, strain_here):
+            for c, x in enumerate((stress[0], stress[4], stress[5])):
+                carry[(at % SLOTS, *spot(c, jj))] = x
+
+    def sweep2(at):
+        registers = plane_stress(w1_v, at, lame_ref, shear_ref, at, strain2)
+        for jj, w, r in residual_plane(registers, carry2_v, (at - 1) % SLOTS, at % SLOTS):
+            for c in range(3):
+                w2_v[c][spot(at, jj)] = ratio1 * w[c] + r[c]
+
+    def sweep3(at):
+        registers = plane_stress(w2_v, at, lame_ref, shear_ref, at, strain3)
+        for jj, w, r in residual_plane(registers, carry3_v, (at - 1) % SLOTS, at % SLOTS):
+            for c in range(3):
+                old = load(w1_v[c], at, jj)
+                w3_v[c][spot(at - HALO, jj)] = (ratio2 * w[c] - ratio3 * old) + r[c]
+
+    def by_parts(at, acc):
         bulk, a0, a1, a2, a3, a4, a5 = acc
-        at = t + HALO
         for jj in range(8):
-            w0, w1, w2 = load3(w3_v, at, jj)
+            w0, w1, w2 = load3(w3_v, at - HALO, jj)
             l0, l1, l2 = differences(lame_ref, at, jj)
             m0, m1, m2 = differences(shear_ref, at, jj)
             bulk = bulk + (l0 * w0 + l1 * w1 + l2 * w2)
@@ -440,8 +396,21 @@
             a5 = a5 + (m1 * w0 + m0 * w1)
         return bulk, a0, a1, a2, a3, a4, a5
 
-    zero = jnp.zeros((8, 128), jnp.float32)
-    acc = lax.fori_loop(0, half, by_parts, (zero,) * 7)
+    acc = (jnp.zeros((8, 128), jnp.float32),) * 7
+    last = half + HALO
+    for at in range(1, last + 8):
+        if at <= last + 2:
+            sweep1(at)
+        if at - 2 == 1:
+            below(w1_v, 1, carry2_v, strain2)
+        if 2 <= at - 2 <= last + 1:
+            sweep2(at - 2)
+        if at - 4 == 2:
+            below(w2_v, 2, carry3_v, strain3)
+        if 3 <= at - 4 <= last:
+            sweep3(at - 4)
+        if HALO <= at - 5 < last:
+            acc = by_parts(at - 5, acc)
     scale = 1.0 / float(EDGE * EDGE * EDGE)
     bulk, *parts = [total(x) * scale for x in acc]
     rows = rows_ref[...]
@@ -482,7 +451,7 @@
     turn_v,
     sem,
 ):
-    half = lame_ref.shape[0] - 2 * HALO - MARGIN
+    half = lame_ref.shape[0] - 2 * HALO
     w3_v = [w30_ref, w31_ref, w32_ref]
     strain = [strain_in[8 * c : 8 * c + 8, :] for c in range(6)]
     matrix = lane_matrix(True)
@@ -490,17 +459,8 @@
     for first in range(0, half, GROUP):
         slot = (first // GROUP) % 2
         for u in range(GROUP):
-            at = first + u + HALO
-            for jj in range(8):
-                stress = stress_at(
-                    w3_v,
-                    at,
-                    jj,
-                    load3(w3_v, at, jj),
-                    load(lame_ref, at, jj),
-                    load(shear_ref, at, jj),
-                    strain,
-                )
+            at = first + u
+            for jj, _, stress in plane_stress(w3_v, at, lame_ref, shear_ref, at + HALO, strain):
                 for c in range(6):
                     work_v[(slot, c, u, *spot(0, jj)[1:])] = stress[c]
         for c in range(6):
@@ -545,9 +505,8 @@
 
 TURN_R = 3
 TURN_S = TURN_R * ROWS + 1
-STEP = 3
+SLOTS = 4
 GROUP = 4
-MARGIN = 3
 
 
 def node_kernel(packets_ref, hom_ref, force_ref, tangent_ref):
@@ -592,11 +551,12 @@
     mib = 1024 * 1024
     f32 = jnp.float32
     half = planes // 2
-    depth = half + 2 * HALO + MARGIN
+    depth = half + 2 * HALO
     packed = 4 * HALO * ROWS
     layer = jax.ShapeDtypeStruct((depth, ROWS, WIDE), f32)
     field = pltpu.VMEM((depth, ROWS, WIDE), f32)
-    half_field = pltpu.VMEM((half + 2 * HALO, ROWS, WIDE), f32)
+    carry = pltpu.VMEM((SLOTS, 3, ROWS, WIDE), f32)
+    last_layer = jax.ShapeDtypeStruct((half + 1, ROWS, WIDE), f32)
 
     def cost(flops, size):
         return pl.CostEstimate(
@@ -645,8 +605,8 @@
         in_specs=[smem, hbm, hbm, vmem, vmem, vmem],
         out_specs=(vmem,) * 3,
         scratch_shapes=[
-            half_field,
-            half_field,
+            field,
+            field,
             pltpu.SMEM(rve_element.shape, jnp.int32),
             pltpu.SMEM(block_slot.shape, jnp.int32),
             pltpu.SemaphoreType.DMA((2,)),
@@ -659,16 +619,16 @@
     *w3, strain, strain_rows, packet = pl.pallas_call(
         sweep_kernel,
         out_shape=(
-            layer,
-            layer,
-            layer,
+            last_layer,
+            last_layer,
+            last_layer,
             jax.ShapeDtypeStruct((1, 6), f32),
             jax.ShapeDtypeStruct((48, 128), f32),
             jax.ShapeDtypeStruct((everywhere, 128), f32),
         ),
         in_specs=[smem] * 4 + [vmem] * 3,
         out_specs=(vmem, vmem, vmem, smem, vmem, vmem),
-        scratch_shapes=[field] * 6 + [pltpu.VMEM((STEP, 3, ROWS, WIDE), f32)],
+        scratch_shapes=[field] * 6 + [carry] * 2,
         compiler_params=pltpu.CompilerParams(vmem_limit_bytes=12 * mib),
         cost_estimate=cost(2 * 10**4, 1),
         name="sweeps",

time: 40.3 us -> 50 us (1.24)
  Pallas kernels: 18.1 us -> 28.5 us
  local copies, waits for them, and re-layouts: 2.06 us -> 0.03 us
  waiting for transfers between devices: 7.59 us -> 8.95 us
    pallas_call x1, Pallas kernels: 10.8 us -> 21.4 us  [on_device(): pl.pallas_call(sweep_kernel, out_shape=(last_layer, last_layer, last_laye...]
    unnamed x17 -> x13, local copies, waits for them, and re-layouts: 2.06 us -> 0.03 us
    all_to_all x1, waiting for transfers between devices: 3.08 us -> 4.4 us  [on_device(): lax.all_to_all(packet, ('vox', 'macro'), split_axis=0, concat_axis=0, til...]
  transfers between devices with their start and end apart: 3 -> 3, of which waited for: 2 -> 2; matrix products, arithmetic and copies ran while one was open for 0% -> 0% of each run, Pallas kernels for 12% -> 9%
where the time goes in v4:
time: 50 us; the launch traced here: 49.8 us
  Pallas kernels  28.5 us (57%)
  starting transfers between devices  11.5 us (23%)
  waiting for transfers between devices  8.95 us (18%)
  between operations  0.79 us (2%)
    pallas_call x1, Pallas kernels, on_device(): pl.pallas_call(sweep_kernel, out_shape=(last_layer, last_layer, last_laye...  21.4 us
    all_to_all x1, starting transfers between devices, on_device(): lax.all_to_all(disp, 'macro', split_axis=0, concat_axis=0, tiled=True)  5.91 us
    all_to_all x1, waiting for transfers between devices, on_device(): lax.all_to_all(disp, 'macro', split_axis=0, concat_axis=0, tiled=True)  4.55 us
    all_to_all x1, waiting for transfers between devices, on_device(): lax.all_to_all(packet, ('vox', 'macro'), split_axis=0, concat_axis=0, til...  4.4 us
    ppermute x1, starting transfers between devices, on_device(): halo = lax.ppermute(rims, 'vox', [(0, 1), (1, 0)])  3.03 us
    pallas_call x1, Pallas kernels, on_device(): pl.pallas_call(stress_kernel, out_shape=jax.ShapeDtypeStruct((6, planes *...  2.73 us
    all_to_all x1, starting transfers between devices, on_device(): lax.all_to_all(packet, ('vox', 'macro'), split_axis=0, concat_axis=0, til...  2.54 us
    pallas_call x1, Pallas kernels, on_device(): pl.pallas_call(prepare_kernel, out_shape=(jax.ShapeDtypeStruct((macro_siz...  2.03 us
  transfers between devices with their start and end apart: 3, of which 2 were waited for; matrix products, arithmetic and copies ran while one was open for 0% of the time, Pallas kernels for 9%

profile of v4, /device:TPU:0, one launch (start us, length us, event | category | flops | bytes accessed | tf_op | source)
XLA Modules:
  0.0 49.8 jit_solution(15094298148812100033)
XLA Ops:
  0.6 0.0 copy-start.1
  0.6 0.0 copy-start
  0.7 0.0 copy-start.5
  0.7 0.0 copy-start.4
  0.7 0.0 copy-start.2
  0.7 2.0 %prepare.1 = (f32[16,3]{1,0:T(8,128)}, f32[384,128]{1,0:T(8,128)}) custom-call(f32[1,3]{1,0:T(1,128)} %disp_hbm.1, f32[1024,128]{1,0:T(8,128)} %bitcast.30, s32[1024,128]{1,0:T(8,128)} %bitcast.32), custom_call_target="tpu_custom_call" | custom-call | flops 1310720000 | bytes 131072 | tf_op jit(solution)/shard_map/prepare/pallas_call | solution.py:568
  2.7 0.0 copy-start.3
  2.7 3.0 %collective-permute-start = (f32[384,128]{1,0:T(8,128)}, f32[384,128]{1,0:T(8,128)S(1)}, u32[]{:S(2)}, u32[]{:S(2)}) collective-permute-start(f32[384,128]{1,0:T(8,128)} %get-tuple-element.20), channel_id=1, source_target_pairs={{0,1},{1,0},{2,3},{3,2},{4,5},{5,4},{6,7},{7,6},{8,9},{9,8},{10,11... | collective-permute-start | bytes 589832 | tf_op jit(solution)/shard_map/ppermute | solution.py:588
  5.8 5.9 %all-to-all-start = ((f32[16,1,3]{2,1,0:T(1,128)}), f32[16,1,3]{2,1,0:T(1,128)S(1)}, u32[]{:S(2)}, u32[]{:S(2)}) async-start(f32[16,1,3]{2,1,0:T(1,128)} %bitcast.35), calls=%async_computation | async-start | bytes 16384 | tf_op jit(solution)/shard_map/all_to_all | solution.py:599
  11.7 0.0 copy-done.5
  11.7 0.0 collective-permute-done.halo_ref
  11.7 0.0 copy-done.1
  11.7 0.0 copy-done
  11.7 0.0 copy-done.4
  11.7 0.0 copy-done.2
  11.8 1.8 %material.1 = (f32[22,32,256]{2,1,0:T(8,128)S(1)}, f32[22,32,256]{2,1,0:T(8,128)S(1)}, f32[8,128]{1,0:T(8,128)S(1)}) custom-call(f32[3,8]{1,0:T(4,128)S(1)} %bitcast.28, s32[16]{0:T(128)S(1)} %copy-done.4, s32[2,8,8]{2,1,0:T(8,128)S(1)} %copy-done.2, f32[1024,128]{1,0:T(8,128)S(1)} %bitcast.31, s32[1024,128]{1,0:T(8,128)S(1)} %bitcast.33, ...), custom_call_target="tpu_custom_call" | custom-call | flops 1310720000 | bytes 131072 | tf_op jit(solution)/shard_map/material/pallas_call | solution.py:602
  13.5 4.5 %all-to-all-done = f32[16,1,3]{2,1,0:T(1,128)S(1)} async-done(((f32[16,1,3]{2,1,0:T(1,128)}), f32[16,1,3]{2,1,0:T(1,128)S(1)}, u32[]{:S(2)}, u32[]{:S(2)}) %all-to-all-start) | async-done | bytes 224 | tf_op jit(solution)/shard_map/all_to_all | solution.py:599
  18.1 0.0 copy-done.3
  18.1 21.4 %sweeps.1 = (f32[17,32,256]{2,1,0:T(8,128)S(1)}, f32[17,32,256]{2,1,0:T(8,128)S(1)}, f32[17,32,256]{2,1,0:T(8,128)S(1)}, f32[1,6]{1,0:T(1,128)}, f32[48,128]{1,0:T(8,128)S(1)}, /*index=5*/f32[32,128]{1,0:T(8,128)}) custom-call(f32[3,8]{1,0:T(4,128)S(1)} %bitcast.29, s32[16]{0:T(128)S(1)} %copy-done.4, s32[2,8]{1,0:T(2,128)S(1)} %copy-done.3, ...), custom_call_target="tpu_custom_call" | custom-call | flops 2621440000 | bytes 131072 | tf_op jit(solution)/shard_map/sweeps/pallas_call | solution.py:619
  39.5 2.5 %all-to-all-start.1 = ((f32[32,1,128]{2,1,0:T(1,128)}), f32[32,1,128]{2,1,0:T(1,128)S(1)}, u32[]{:S(2)}, u32[]{:S(2)}) async-start(f32[32,1,128]{2,1,0:T(1,128)} %bitcast.16), calls=%async_computation.1 | async-start | bytes 32768 | tf_op jit(solution)/shard_map/all_to_all | solution.py:637
  42.0 2.7 %stress.1 = f32[6,1024,128]{2,1,0:T(8,128)} custom-call(f32[48,128]{1,0:T(8,128)S(1)} %get-tuple-element.24.strain_in, f32[22,32,256]{2,1,0:T(8,128)S(1)} %get-tuple-element.21.lame_ref, f32[22,32,256]{2,1,0:T(8,128)S(1)} %get-tuple-element.22.shear_ref, f32[17,32,256]{2,1,0:T(8,128)S(1)} %get-tuple-element.25.w30_ref, ...), custom_call_target="tpu_custom_call" | custom-call | flops 1310720000 | bytes 131072 | tf_op jit(solution)/shard_map/stress/pallas_call | solution.py:641
  44.8 4.4 %all-to-all-done.1 = f32[32,1,128]{2,1,0:T(1,128)S(1)} async-done(((f32[32,1,128]{2,1,0:T(1,128)}), f32[32,1,128]{2,1,0:T(1,128)S(1)}, u32[]{:S(2)}, u32[]{:S(2)}) %all-to-all-start.1) | async-done | bytes 16416 | tf_op jit(solution)/shard_map/all_to_all | solution.py:637
  49.2 0.6 %nodes.1 = (f32[1,6]{1,0:T(1,128)}, f32[1,3]{1,0:T(1,128)}, f32[1,108]{1,0:T(1,128)}) custom-call(f32[32,128]{1,0:T(8,128)S(1)} %bitcast.26), custom_call_target="tpu_custom_call" | custom-call | tf_op jit(solution)/shard_map/nodes/pallas_call | solution.py:662
  (1 shorter events, 0.0 us)
Async XLA Ops:
  0.6 11.1 %copy-start.1 = (s32[1,32,4096]{2,1,0:T(8,128)S(1)}, s32[1,32,4096]{2,1,0:T(8,128)}, u32[]{:S(2)}) copy-start(s32[1,32,4096]{2,1,0:T(8,128)} %param.13) | copy-start | bytes 1572868
  0.6 11.1 %copy-start = (f32[1,32,4096]{2,1,0:T(8,128)S(1)}, f32[1,32,4096]{2,1,0:T(8,128)}, u32[]{:S(2)}) copy-start(f32[1,32,4096]{2,1,0:T(8,128)} %param.12) | copy-start | bytes 1572868
  0.7 11.0 %copy-start.5 = (f32[1,3,8]{2,0,1:T(1,128)S(1)}, f32[1,3,8]{2,0,1:T(1,128)}, u32[]{:S(2)}) copy-start(f32[1,3,8]{2,0,1:T(1,128)} %param.8) | copy-start | bytes 292
  0.7 11.1 %copy-start.4 = (s32[16]{0:T(128)S(1)}, s32[16]{0:T(128)}, u32[]{:S(2)}) copy-start(s32[16]{0:T(128)} %rve_element.1) | copy-start | bytes 196
  0.7 11.1 %copy-start.2 = (s32[2,8,8]{2,1,0:T(8,128)S(1)}, s32[2,8,8]{2,1,0:T(8,128)}, u32[]{:S(2)}) copy-start(s32[2,8,8]{2,1,0:T(8,128)} %slot_hbm.1) | copy-start | bytes 1540
  2.7 15.4 %copy-start.3 = (s32[2,8]{1,0:T(2,128)S(1)}, s32[2,8]{1,0:T(2,128)}, u32[]{:S(2)}) copy-start(s32[2,8]{1,0:T(2,128)} %connectivity.1) | copy-start | bytes 196
  2.7 9.0 %collective-permute-start = (f32[384,128]{1,0:T(8,128)}, f32[384,128]{1,0:T(8,128)S(1)}, u32[]{:S(2)}, u32[]{:S(2)}) collective-permute-start(f32[384,128]{1,0:T(8,128)} %get-tuple-element.20), channel_id=1, source_target_pairs={{0,1},{1,0},{2,3},{3,2},{4,5},{5,4},{6,7},{7,6},{8,9},{9,8},{10,11... | collective-permute-start | bytes 589832 | tf_op jit(solution)/shard_map/ppermute | solution.py:588
  5.8 12.3 %all-to-all-start = ((f32[16,1,3]{2,1,0:T(1,128)}), f32[16,1,3]{2,1,0:T(1,128)S(1)}, u32[]{:S(2)}, u32[]{:S(2)}) async-start(f32[16,1,3]{2,1,0:T(1,128)} %bitcast.35), calls=%async_computation | async-start | bytes 16384 | tf_op jit(solution)/shard_map/all_to_all | solution.py:599
  39.5 9.7 %all-to-all-start.1 = ((f32[32,1,128]{2,1,0:T(1,128)}), f32[32,1,128]{2,1,0:T(1,128)S(1)}, u32[]{:S(2)}, u32[]{:S(2)}) async-start(f32[32,1,128]{2,1,0:T(1,128)} %bitcast.16), calls=%async_computation.1 | async-start | bytes 32768 | tf_op jit(solution)/shard_map/all_to_all | solution.py:637

commit v5 on v4

--- a/solution.py
+++ b/solution.py
@@ -103,14 +103,14 @@
         )
 
 
-def residual_plane(registers, carry_v, old, new):
+def residual_plane(registers, carry_v):
     begin = None
     row_xy = row_yy = row_yz = None
     for jj, w, stress in registers:
         xx, yy, zz, yz, xz, xy = stress
-        pxx, pxz, pxy = [load(carry_v.at[old], c, jj) for c in range(3)]
+        pxx, pxz, pxy = [load(carry_v, c, jj) for c in range(3)]
         for c, x in enumerate((xx, xz, xy)):
-            carry_v[(new, *spot(c, jj))] = x
+            carry_v[spot(c, jj)] = x
         r = [
             (xx - pxx) + (xz - prev_lane(xz)) + xy,
             (xy - pxy) + (yz - prev_lane(yz)) + yy,
@@ -363,23 +363,18 @@
                 trace1 * l2 + twice1[2] * m2 + (strain1[4] * m0 + strain1[3] * m1)
             )
 
-    def below(w_refs, at, carry, strain_here):
-        for jj, _, stress in plane_stress(w_refs, at, lame_ref, shear_ref, at, strain_here):
-            for c, x in enumerate((stress[0], stress[4], stress[5])):
-                carry[(at % SLOTS, *spot(c, jj))] = x
-
     def sweep2(at):
         registers = plane_stress(w1_v, at, lame_ref, shear_ref, at, strain2)
-        for jj, w, r in residual_plane(registers, carry2_v, (at - 1) % SLOTS, at % SLOTS):
+        for jj, w, r in residual_plane(registers, carry2_v):
             for c in range(3):
                 w2_v[c][spot(at, jj)] = ratio1 * w[c] + r[c]
 
-    def sweep3(at):
+    def sweep3(at, place):
         registers = plane_stress(w2_v, at, lame_ref, shear_ref, at, strain3)
-        for jj, w, r in residual_plane(registers, carry3_v, (at - 1) % SLOTS, at % SLOTS):
+        for jj, w, r in residual_plane(registers, carry3_v):
             for c in range(3):
                 old = load(w1_v[c], at, jj)
-                w3_v[c][spot(at - HALO, jj)] = (ratio2 * w[c] - ratio3 * old) + r[c]
+                w3_v[c][spot(place, jj)] = (ratio2 * w[c] - ratio3 * old) + r[c]
 
     def by_parts(at, acc):
         bulk, a0, a1, a2, a3, a4, a5 = acc
@@ -396,21 +391,22 @@
             a5 = a5 + (m1 * w0 + m0 * w1)
         return bulk, a0, a1, a2, a3, a4, a5
 
-    acc = (jnp.zeros((8, 128), jnp.float32),) * 7
-    last = half + HALO
-    for at in range(1, last + 8):
-        if at <= last + 2:
-            sweep1(at)
-        if at - 2 == 1:
-            below(w1_v, 1, carry2_v, strain2)
-        if 2 <= at - 2 <= last + 1:
-            sweep2(at - 2)
-        if at - 4 == 2:
-            below(w2_v, 2, carry3_v, strain3)
-        if 3 <= at - 4 <= last:
-            sweep3(at - 4)
-        if HALO <= at - 5 < last:
-            acc = by_parts(at - 5, acc)
+    def first_loop(t, _):
+        sweep1(t + 1)
+        return 0
+
+    lax.fori_loop(0, half + 5, first_loop, 0)
+
+    def second_loop(t, _):
+        at = jnp.maximum(t - 1, 0)
+        sweep3(at, jnp.where(at < HALO, half, at - HALO))
+        sweep2(t + 1)
+        return 0
+
+    lax.fori_loop(0, half + 5, second_loop, 0)
+
+    zero = jnp.zeros((8, 128), jnp.float32)
+    acc = lax.fori_loop(0, half, lambda t, acc: by_parts(t + HALO, acc), (zero,) * 7)
     scale = 1.0 / float(EDGE * EDGE * EDGE)
     bulk, *parts = [total(x) * scale for x in acc]
     rows = rows_ref[...]
@@ -505,7 +501,6 @@
 
 TURN_R = 3
 TURN_S = TURN_R * ROWS + 1
-SLOTS = 4
 GROUP = 4
 
 
@@ -555,7 +550,8 @@
     packed = 4 * HALO * ROWS
     layer = jax.ShapeDtypeStruct((depth, ROWS, WIDE), f32)
     field = pltpu.VMEM((depth, ROWS, WIDE), f32)
-    carry = pltpu.VMEM((SLOTS, 3, ROWS, WIDE), f32)
+    carry = pltpu.VMEM((3, ROWS, WIDE), f32)
+    beyond = pltpu.VMEM((depth + 1, ROWS, WIDE), f32)
     last_layer = jax.ShapeDtypeStruct((half + 1, ROWS, WIDE), f32)
 
     def cost(flops, size):
@@ -628,7 +624,7 @@
         ),
         in_specs=[smem] * 4 + [vmem] * 3,
         out_specs=(vmem, vmem, vmem, smem, vmem, vmem),
-        scratch_shapes=[field] * 6 + [carry] * 2,
+        scratch_shapes=[beyond] * 3 + [field] * 3 + [carry] * 2,
         compiler_params=pltpu.CompilerParams(vmem_limit_bytes=12 * mib),
         cost_estimate=cost(2 * 10**4, 1),
         name="sweeps",

time: 50 us -> 38.8 us (0.78)
  Pallas kernels: 28.5 us -> 17.3 us
    pallas_call x1, Pallas kernels: 21.4 us -> 10.2 us  [on_device(): pl.pallas_call(sweep_kernel, out_shape=(last_layer, last_layer, last_laye...]
  transfers between devices with their start and end apart: 3 -> 3, of which waited for: 2 -> 2; matrix products, arithmetic and copies ran while one was open for 0% -> 0% of each run, Pallas kernels for 9% -> 12%
where the time goes in v5:
time: 38.8 us; the launch traced here: 38.6 us
  Pallas kernels  17.3 us (45%)
  starting transfers between devices  11.5 us (30%)
  waiting for transfers between devices  8.95 us (23%)
  between operations  0.79 us (2%)
    pallas_call x1, Pallas kernels, on_device(): pl.pallas_call(sweep_kernel, out_shape=(last_layer, last_layer, last_laye...  10.2 us
    all_to_all x1, starting transfers between devices, on_device(): lax.all_to_all(disp, 'macro', split_axis=0, concat_axis=0, tiled=True)  5.91 us
    all_to_all x1, waiting for transfers between devices, on_device(): lax.all_to_all(disp, 'macro', split_axis=0, concat_axis=0, tiled=True)  4.55 us
    all_to_all x1, waiting for transfers between devices, on_device(): lax.all_to_all(packet, ('vox', 'macro'), split_axis=0, concat_axis=0, til...  4.4 us
    ppermute x1, starting transfers between devices, on_device(): halo = lax.ppermute(rims, 'vox', [(0, 1), (1, 0)])  3.03 us
    pallas_call x1, Pallas kernels, on_device(): pl.pallas_call(stress_kernel, out_shape=jax.ShapeDtypeStruct((6, planes *...  2.73 us
    all_to_all x1, starting transfers between devices, on_device(): lax.all_to_all(packet, ('vox', 'macro'), split_axis=0, concat_axis=0, til...  2.54 us
    pallas_call x1, Pallas kernels, on_device(): pl.pallas_call(prepare_kernel, out_shape=(jax.ShapeDtypeStruct((macro_siz...  2.03 us
  transfers between devices with their start and end apart: 3, of which 2 were waited for; matrix products, arithmetic and copies ran while one was open for 0% of the time, Pallas kernels for 12%

profile of v5, /device:TPU:0, one launch (start us, length us, event | category | flops | bytes accessed | tf_op | source)
XLA Modules:
  0.0 38.6 jit_solution(12787784765097664014)
XLA Ops:
  0.6 0.0 copy-start.1
  0.6 0.0 copy-start
  0.7 0.0 copy-start.5
  0.7 0.0 copy-start.4
  0.7 0.0 copy-start.2
  0.7 2.0 %prepare.1 = (f32[16,3]{1,0:T(8,128)}, f32[384,128]{1,0:T(8,128)}) custom-call(f32[1,3]{1,0:T(1,128)} %disp_hbm.1, f32[1024,128]{1,0:T(8,128)} %bitcast.30, s32[1024,128]{1,0:T(8,128)} %bitcast.32), custom_call_target="tpu_custom_call" | custom-call | flops 1310720000 | bytes 131072 | tf_op jit(solution)/shard_map/prepare/pallas_call | solution.py:564
  2.7 0.0 copy-start.3
  2.7 3.0 %collective-permute-start = (f32[384,128]{1,0:T(8,128)}, f32[384,128]{1,0:T(8,128)S(1)}, u32[]{:S(2)}, u32[]{:S(2)}) collective-permute-start(f32[384,128]{1,0:T(8,128)} %get-tuple-element.20), channel_id=1, source_target_pairs={{0,1},{1,0},{2,3},{3,2},{4,5},{5,4},{6,7},{7,6},{8,9},{9,8},{10,11... | collective-permute-start | bytes 589832 | tf_op jit(solution)/shard_map/ppermute | solution.py:584
  5.8 5.9 %all-to-all-start = ((f32[16,1,3]{2,1,0:T(1,128)}), f32[16,1,3]{2,1,0:T(1,128)S(1)}, u32[]{:S(2)}, u32[]{:S(2)}) async-start(f32[16,1,3]{2,1,0:T(1,128)} %bitcast.35), calls=%async_computation | async-start | bytes 16384 | tf_op jit(solution)/shard_map/all_to_all | solution.py:595
  11.7 0.0 copy-done.5
  11.7 0.0 collective-permute-done.halo_ref
  11.7 0.0 copy-done.1
  11.7 0.0 copy-done
  11.7 0.0 copy-done.4
  11.7 0.0 copy-done.2
  11.8 1.8 %material.1 = (f32[22,32,256]{2,1,0:T(8,128)S(1)}, f32[22,32,256]{2,1,0:T(8,128)S(1)}, f32[8,128]{1,0:T(8,128)S(1)}) custom-call(f32[3,8]{1,0:T(4,128)S(1)} %bitcast.28, s32[16]{0:T(128)S(1)} %copy-done.4, s32[2,8,8]{2,1,0:T(8,128)S(1)} %copy-done.2, f32[1024,128]{1,0:T(8,128)S(1)} %bitcast.31, s32[1024,128]{1,0:T(8,128)S(1)} %bitcast.33, ...), custom_call_target="tpu_custom_call" | custom-call | flops 1310720000 | bytes 131072 | tf_op jit(solution)/shard_map/material/pallas_call | solution.py:598
  13.5 4.5 %all-to-all-done = f32[16,1,3]{2,1,0:T(1,128)S(1)} async-done(((f32[16,1,3]{2,1,0:T(1,128)}), f32[16,1,3]{2,1,0:T(1,128)S(1)}, u32[]{:S(2)}, u32[]{:S(2)}) %all-to-all-start) | async-done | bytes 224 | tf_op jit(solution)/shard_map/all_to_all | solution.py:595
  18.1 0.0 copy-done.3
  18.1 10.2 %sweeps.1 = (f32[17,32,256]{2,1,0:T(8,128)S(1)}, f32[17,32,256]{2,1,0:T(8,128)S(1)}, f32[17,32,256]{2,1,0:T(8,128)S(1)}, f32[1,6]{1,0:T(1,128)}, f32[48,128]{1,0:T(8,128)S(1)}, /*index=5*/f32[32,128]{1,0:T(8,128)}) custom-call(f32[3,8]{1,0:T(4,128)S(1)} %bitcast.29, s32[16]{0:T(128)S(1)} %copy-done.4, s32[2,8]{1,0:T(2,128)S(1)} %copy-done.3, ...), custom_call_target="tpu_custom_call" | custom-call | flops 2621440000 | bytes 131072 | tf_op jit(solution)/shard_map/sweeps/pallas_call | solution.py:615
  28.3 2.5 %all-to-all-start.1 = ((f32[32,1,128]{2,1,0:T(1,128)}), f32[32,1,128]{2,1,0:T(1,128)S(1)}, u32[]{:S(2)}, u32[]{:S(2)}) async-start(f32[32,1,128]{2,1,0:T(1,128)} %bitcast.16), calls=%async_computation.1 | async-start | bytes 32768 | tf_op jit(solution)/shard_map/all_to_all | solution.py:633
  30.8 2.7 %stress.1 = f32[6,1024,128]{2,1,0:T(8,128)} custom-call(f32[48,128]{1,0:T(8,128)S(1)} %get-tuple-element.24.strain_in, f32[22,32,256]{2,1,0:T(8,128)S(1)} %get-tuple-element.21.lame_ref, f32[22,32,256]{2,1,0:T(8,128)S(1)} %get-tuple-element.22.shear_ref, f32[17,32,256]{2,1,0:T(8,128)S(1)} %get-tuple-element.25.w30_ref, ...), custom_call_target="tpu_custom_call" | custom-call | flops 1310720000 | bytes 131072 | tf_op jit(solution)/shard_map/stress/pallas_call | solution.py:637
  33.6 4.4 %all-to-all-done.1 = f32[32,1,128]{2,1,0:T(1,128)S(1)} async-done(((f32[32,1,128]{2,1,0:T(1,128)}), f32[32,1,128]{2,1,0:T(1,128)S(1)}, u32[]{:S(2)}, u32[]{:S(2)}) %all-to-all-start.1) | async-done | bytes 16416 | tf_op jit(solution)/shard_map/all_to_all | solution.py:633
  38.0 0.6 %nodes.1 = (f32[1,6]{1,0:T(1,128)}, f32[1,3]{1,0:T(1,128)}, f32[1,108]{1,0:T(1,128)}) custom-call(f32[32,128]{1,0:T(8,128)S(1)} %bitcast.26), custom_call_target="tpu_custom_call" | custom-call | tf_op jit(solution)/shard_map/nodes/pallas_call | solution.py:658
  (1 shorter events, 0.0 us)
Async XLA Ops:
  0.6 11.1 %copy-start.1 = (s32[1,32,4096]{2,1,0:T(8,128)S(1)}, s32[1,32,4096]{2,1,0:T(8,128)}, u32[]{:S(2)}) copy-start(s32[1,32,4096]{2,1,0:T(8,128)} %param.13) | copy-start | bytes 1572868
  0.6 11.1 %copy-start = (f32[1,32,4096]{2,1,0:T(8,128)S(1)}, f32[1,32,4096]{2,1,0:T(8,128)}, u32[]{:S(2)}) copy-start(f32[1,32,4096]{2,1,0:T(8,128)} %param.12) | copy-start | bytes 1572868
  0.7 11.0 %copy-start.5 = (f32[1,3,8]{2,0,1:T(1,128)S(1)}, f32[1,3,8]{2,0,1:T(1,128)}, u32[]{:S(2)}) copy-start(f32[1,3,8]{2,0,1:T(1,128)} %param.8) | copy-start | bytes 292
  0.7 11.1 %copy-start.4 = (s32[16]{0:T(128)S(1)}, s32[16]{0:T(128)}, u32[]{:S(2)}) copy-start(s32[16]{0:T(128)} %rve_element.1) | copy-start | bytes 196
  0.7 11.1 %copy-start.2 = (s32[2,8,8]{2,1,0:T(8,128)S(1)}, s32[2,8,8]{2,1,0:T(8,128)}, u32[]{:S(2)}) copy-start(s32[2,8,8]{2,1,0:T(8,128)} %slot_hbm.1) | copy-start | bytes 1540
  2.7 15.4 %copy-start.3 = (s32[2,8]{1,0:T(2,128)S(1)}, s32[2,8]{1,0:T(2,128)}, u32[]{:S(2)}) copy-start(s32[2,8]{1,0:T(2,128)} %connectivity.1) | copy-start | bytes 196
  2.7 9.0 %collective-permute-start = (f32[384,128]{1,0:T(8,128)}, f32[384,128]{1,0:T(8,128)S(1)}, u32[]{:S(2)}, u32[]{:S(2)}) collective-permute-start(f32[384,128]{1,0:T(8,128)} %get-tuple-element.20), channel_id=1, source_target_pairs={{0,1},{1,0},{2,3},{3,2},{4,5},{5,4},{6,7},{7,6},{8,9},{9,8},{10,11... | collective-permute-start | bytes 589832 | tf_op jit(solution)/shard_map/ppermute | solution.py:584
  5.8 12.3 %all-to-all-start = ((f32[16,1,3]{2,1,0:T(1,128)}), f32[16,1,3]{2,1,0:T(1,128)S(1)}, u32[]{:S(2)}, u32[]{:S(2)}) async-start(f32[16,1,3]{2,1,0:T(1,128)} %bitcast.35), calls=%async_computation | async-start | bytes 16384 | tf_op jit(solution)/shard_map/all_to_all | solution.py:595
  28.3 9.7 %all-to-all-start.1 = ((f32[32,1,128]{2,1,0:T(1,128)}), f32[32,1,128]{2,1,0:T(1,128)S(1)}, u32[]{:S(2)}, u32[]{:S(2)}) async-start(f32[32,1,128]{2,1,0:T(1,128)} %bitcast.16), calls=%async_computation.1 | async-start | bytes 32768 | tf_op jit(solution)/shard_map/all_to_all | solution.py:633

commit v6 on v5

--- a/solution.py
+++ b/solution.py
@@ -35,9 +35,22 @@
     return (centre, weights)
 
 
-centre, ((keep1, push1), (keep2, push2)) = chebyshev_terms(SWEEPS - 1)
-gain1 = push1 * precond
-gain2 = push2 * precond
+def sweep_polynomial():
+    centre, weights = chebyshev_terms(SWEEPS - 1)
+    direction = [1.0 / centre]
+    result = list(direction)
+    for keep, push in weights:
+        applied = [1.0] + result
+        direction = [
+            keep * (direction[k] if k < len(direction) else 0.0) + push * applied[k]
+            for k in range(len(applied))
+        ]
+        result = [(result[k] if k < len(result) else 0.0) + direction[k] for k in range(len(applied))]
+    return result
+
+
+poly0, poly1, poly2 = sweep_polynomial()
+
 
 def spot(at, jj):
     half = (jj & 1) * 128
@@ -85,12 +98,15 @@
         lane0, lane1, lane2 = [next_lane(x) for x in w]
         lame = load(lame_ref, lame_at, jj)
         shear = load(shear_ref, lame_at, jj)
-        e0 = (n0 - w0) + strain[0]
-        e1 = (row1 - w1) + strain[1]
-        e2 = (lane2 - w2) + strain[2]
-        g3 = (lane1 + row2) - (w1 + w2) + strain[3]
-        g4 = (lane0 + n2) - (w0 + w2) + strain[4]
-        g5 = (row0 + n1) - (w0 + w1) + strain[5]
+        e0 = n0 - w0
+        e1 = row1 - w1
+        e2 = lane2 - w2
+        g3 = (lane1 + row2) - (w1 + w2)
+        g4 = (lane0 + n2) - (w0 + w2)
+        g5 = (row0 + n1) - (w0 + w1)
+        if strain is not None:
+            e0, e1, e2 = e0 + strain[0], e1 + strain[1], e2 + strain[2]
+            g3, g4, g5 = g3 + strain[3], g4 + strain[4], g5 + strain[5]
         bulk = lame * (e0 + e1 + e2)
         twice = shear + shear
         yield jj, w, (
@@ -339,15 +355,11 @@
     w2_v = [w20_v, w21_v, w22_v]
     w3_v = [w30_ref, w31_ref, w32_ref]
 
-    scale1 = gain1 * gain2 * precond / centre
-    strain1 = [scale1 * e for e in strain]
+    strain1 = [poly2 * precond**3 * e for e in strain]
     trace1 = strain1[0] + strain1[1] + strain1[2]
     twice1 = [2.0 * strain1[c] for c in range(3)]
-    strain2 = [gain1 * gain2 * e for e in strain]
-    ratio1 = (1.0 + keep1) / gain1
-    strain3 = [gain2 * e for e in strain]
-    ratio2 = (1.0 + keep2) / gain2
-    ratio3 = keep2 / (gain1 * gain2)
+    ratio1 = poly1 / (poly2 * precond)
+    ratio0 = poly0 / (poly2 * precond**2)
 
     def sweep1(at):
         for jj in range(8):
@@ -364,20 +376,19 @@
             )
 
     def sweep2(at):
-        registers = plane_stress(w1_v, at, lame_ref, shear_ref, at, strain2)
+        registers = plane_stress(w1_v, at, lame_ref, shear_ref, at, None)
         for jj, w, r in residual_plane(registers, carry2_v):
             for c in range(3):
                 w2_v[c][spot(at, jj)] = ratio1 * w[c] + r[c]
 
     def sweep3(at, place):
-        registers = plane_stress(w2_v, at, lame_ref, shear_ref, at, strain3)
-        for jj, w, r in residual_plane(registers, carry3_v):
+        registers = plane_stress(w2_v, at, lame_ref, shear_ref, at, None)
+        for jj, _, r in residual_plane(registers, carry3_v):
             for c in range(3):
-                old = load(w1_v[c], at, jj)
-                w3_v[c][spot(place, jj)] = (ratio2 * w[c] - ratio3 * old) + r[c]
-
-    def by_parts(at, acc):
-        bulk, a0, a1, a2, a3, a4, a5 = acc
+                w3_v[c][spot(place, jj)] = ratio0 * load(w1_v[c], at, jj) + r[c]
+
+    def by_parts(at):
+        bulk, a0, a1, a2, a3, a4, a5 = (jnp.zeros((8, 128), jnp.float32),) * 7
         for jj in range(8):
             w0, w1, w2 = load3(w3_v, at - HALO, jj)
             l0, l1, l2 = differences(lame_ref, at, jj)
@@ -391,22 +402,18 @@
             a5 = a5 + (m1 * w0 + m0 * w1)
         return bulk, a0, a1, a2, a3, a4, a5
 
-    def first_loop(t, _):
-        sweep1(t + 1)
-        return 0
-
-    lax.fori_loop(0, half + 5, first_loop, 0)
-
-    def second_loop(t, _):
-        at = jnp.maximum(t - 1, 0)
+    def step(t, acc):
+        at = jnp.maximum(t - 4, HALO)
+        sums = by_parts(at)
+        acc = [x + jnp.where(t - 4 >= HALO, y, 0.0) for x, y in zip(acc, sums)]
+        at = jnp.maximum(t - 3, 0)
         sweep3(at, jnp.where(at < HALO, half, at - HALO))
-        sweep2(t + 1)
-        return 0
-
-    lax.fori_loop(0, half + 5, second_loop, 0)
+        sweep2(jnp.maximum(t - 1, 0))
+        sweep1(jnp.minimum(t + 1, half + 5))
+        return tuple(acc)
 
     zero = jnp.zeros((8, 128), jnp.float32)
-    acc = lax.fori_loop(0, half, lambda t, acc: by_parts(t + HALO, acc), (zero,) * 7)
+    acc = lax.fori_loop(0, half + 7, step, (zero,) * 7)
     scale = 1.0 / float(EDGE * EDGE * EDGE)
     bulk, *parts = [total(x) * scale for x in acc]
     rows = rows_ref[...]

time: 38.8 us -> 37.4 us (0.964)
  Pallas kernels: 17.3 us -> 15.9 us
    pallas_call x1, Pallas kernels: 10.2 us -> 8.76 us  [on_device(): pl.pallas_call(sweep_kernel, out_shape=(last_layer, last_layer, last_laye...]
where the time goes in v6:
time: 37.4 us; the launch traced here: 37.1 us
  Pallas kernels  15.9 us (43%)
  starting transfers between devices  11.5 us (31%)
  waiting for transfers between devices  8.94 us (24%)
  between operations  0.79 us (2%)
    pallas_call x1, Pallas kernels, on_device(): pl.pallas_call(sweep_kernel, out_shape=(last_layer, last_layer, last_laye...  8.76 us
    all_to_all x1, starting transfers between devices, on_device(): lax.all_to_all(disp, 'macro', split_axis=0, concat_axis=0, tiled=True)  5.91 us
    all_to_all x1, waiting for transfers between devices, on_device(): lax.all_to_all(disp, 'macro', split_axis=0, concat_axis=0, tiled=True)  4.55 us
    all_to_all x1, waiting for transfers between devices, on_device(): lax.all_to_all(packet, ('vox', 'macro'), split_axis=0, concat_axis=0, til...  4.39 us
    ppermute x1, starting transfers between devices, on_device(): halo = lax.ppermute(rims, 'vox', [(0, 1), (1, 0)])  3.03 us
    pallas_call x1, Pallas kernels, on_device(): pl.pallas_call(stress_kernel, out_shape=jax.ShapeDtypeStruct((6, planes *...  2.74 us
    all_to_all x1, starting transfers between devices, on_device(): lax.all_to_all(packet, ('vox', 'macro'), split_axis=0, concat_axis=0, til...  2.54 us
    pallas_call x1, Pallas kernels, on_device(): pl.pallas_call(prepare_kernel, out_shape=(jax.ShapeDtypeStruct((macro_siz...  2.03 us
  transfers between devices with their start and end apart: 3, of which 2 were waited for; matrix products, arithmetic and copies ran while one was open for 0% of the time, Pallas kernels for 12%

profile of v6, /device:TPU:0, one launch (start us, length us, event | category | flops | bytes accessed | tf_op | source)
XLA Modules:
  0.0 37.1 jit_solution(13184930568990581579)
XLA Ops:
  0.6 0.0 copy-start.1
  0.6 0.0 copy-start
  0.7 0.0 copy-start.5
  0.7 0.0 copy-start.4
  0.7 0.0 copy-start.2
  0.7 2.0 %prepare.1 = (f32[16,3]{1,0:T(8,128)}, f32[384,128]{1,0:T(8,128)}) custom-call(f32[1,3]{1,0:T(1,128)} %disp_hbm.1, f32[1024,128]{1,0:T(8,128)} %bitcast.30, s32[1024,128]{1,0:T(8,128)} %bitcast.32), custom_call_target="tpu_custom_call" | custom-call | flops 1310720000 | bytes 131072 | tf_op jit(solution)/shard_map/prepare/pallas_call | solution.py:571
  2.7 0.0 copy-start.3
  2.7 3.0 %collective-permute-start = (f32[384,128]{1,0:T(8,128)}, f32[384,128]{1,0:T(8,128)S(1)}, u32[]{:S(2)}, u32[]{:S(2)}) collective-permute-start(f32[384,128]{1,0:T(8,128)} %get-tuple-element.20), channel_id=1, source_target_pairs={{0,1},{1,0},{2,3},{3,2},{4,5},{5,4},{6,7},{7,6},{8,9},{9,8},{10,11... | collective-permute-start | bytes 589832 | tf_op jit(solution)/shard_map/ppermute | solution.py:591
  5.8 5.9 %all-to-all-start = ((f32[16,1,3]{2,1,0:T(1,128)}), f32[16,1,3]{2,1,0:T(1,128)S(1)}, u32[]{:S(2)}, u32[]{:S(2)}) async-start(f32[16,1,3]{2,1,0:T(1,128)} %bitcast.35), calls=%async_computation | async-start | bytes 16384 | tf_op jit(solution)/shard_map/all_to_all | solution.py:602
  11.7 0.0 copy-done.5
  11.7 0.0 collective-permute-done.halo_ref
  11.7 0.0 copy-done.1
  11.7 0.0 copy-done
  11.7 0.0 copy-done.4
  11.7 0.0 copy-done.2
  11.8 1.8 %material.1 = (f32[22,32,256]{2,1,0:T(8,128)S(1)}, f32[22,32,256]{2,1,0:T(8,128)S(1)}, f32[8,128]{1,0:T(8,128)S(1)}) custom-call(f32[3,8]{1,0:T(4,128)S(1)} %bitcast.28, s32[16]{0:T(128)S(1)} %copy-done.4, s32[2,8,8]{2,1,0:T(8,128)S(1)} %copy-done.2, f32[1024,128]{1,0:T(8,128)S(1)} %bitcast.31, s32[1024,128]{1,0:T(8,128)S(1)} %bitcast.33, ...), custom_call_target="tpu_custom_call" | custom-call | flops 1310720000 | bytes 131072 | tf_op jit(solution)/shard_map/material/pallas_call | solution.py:605
  13.5 4.5 %all-to-all-done = f32[16,1,3]{2,1,0:T(1,128)S(1)} async-done(((f32[16,1,3]{2,1,0:T(1,128)}), f32[16,1,3]{2,1,0:T(1,128)S(1)}, u32[]{:S(2)}, u32[]{:S(2)}) %all-to-all-start) | async-done | bytes 224 | tf_op jit(solution)/shard_map/all_to_all | solution.py:602
  18.1 0.0 copy-done.3
  18.1 8.8 %sweeps.1 = (f32[17,32,256]{2,1,0:T(8,128)S(1)}, f32[17,32,256]{2,1,0:T(8,128)S(1)}, f32[17,32,256]{2,1,0:T(8,128)S(1)}, f32[1,6]{1,0:T(1,128)}, f32[48,128]{1,0:T(8,128)S(1)}, /*index=5*/f32[32,128]{1,0:T(8,128)}) custom-call(f32[3,8]{1,0:T(4,128)S(1)} %bitcast.29, s32[16]{0:T(128)S(1)} %copy-done.4, s32[2,8]{1,0:T(2,128)S(1)} %copy-done.3, ...), custom_call_target="tpu_custom_call" | custom-call | flops 2621440000 | bytes 131072 | tf_op jit(solution)/shard_map/sweeps/pallas_call | solution.py:622
  26.9 2.5 %all-to-all-start.1 = ((f32[32,1,128]{2,1,0:T(1,128)}), f32[32,1,128]{2,1,0:T(1,128)S(1)}, u32[]{:S(2)}, u32[]{:S(2)}) async-start(f32[32,1,128]{2,1,0:T(1,128)} %bitcast.16), calls=%async_computation.1 | async-start | bytes 32768 | tf_op jit(solution)/shard_map/all_to_all | solution.py:640
  29.4 2.7 %stress.1 = f32[6,1024,128]{2,1,0:T(8,128)} custom-call(f32[48,128]{1,0:T(8,128)S(1)} %get-tuple-element.24.strain_in, f32[22,32,256]{2,1,0:T(8,128)S(1)} %get-tuple-element.21.lame_ref, f32[22,32,256]{2,1,0:T(8,128)S(1)} %get-tuple-element.22.shear_ref, f32[17,32,256]{2,1,0:T(8,128)S(1)} %get-tuple-element.25.w30_ref, ...), custom_call_target="tpu_custom_call" | custom-call | flops 1310720000 | bytes 131072 | tf_op jit(solution)/shard_map/stress/pallas_call | solution.py:644
  32.2 4.4 %all-to-all-done.1 = f32[32,1,128]{2,1,0:T(1,128)S(1)} async-done(((f32[32,1,128]{2,1,0:T(1,128)}), f32[32,1,128]{2,1,0:T(1,128)S(1)}, u32[]{:S(2)}, u32[]{:S(2)}) %all-to-all-start.1) | async-done | bytes 16416 | tf_op jit(solution)/shard_map/all_to_all | solution.py:640
  36.5 0.6 %nodes.1 = (f32[1,6]{1,0:T(1,128)}, f32[1,3]{1,0:T(1,128)}, f32[1,108]{1,0:T(1,128)}) custom-call(f32[32,128]{1,0:T(8,128)S(1)} %bitcast.26), custom_call_target="tpu_custom_call" | custom-call | tf_op jit(solution)/shard_map/nodes/pallas_call | solution.py:665
  (1 shorter events, 0.0 us)
Async XLA Ops:
  0.6 11.1 %copy-start.1 = (s32[1,32,4096]{2,1,0:T(8,128)S(1)}, s32[1,32,4096]{2,1,0:T(8,128)}, u32[]{:S(2)}) copy-start(s32[1,32,4096]{2,1,0:T(8,128)} %param.13) | copy-start | bytes 1572868
  0.6 11.1 %copy-start = (f32[1,32,4096]{2,1,0:T(8,128)S(1)}, f32[1,32,4096]{2,1,0:T(8,128)}, u32[]{:S(2)}) copy-start(f32[1,32,4096]{2,1,0:T(8,128)} %param.12) | copy-start | bytes 1572868
  0.7 11.0 %copy-start.5 = (f32[1,3,8]{2,0,1:T(1,128)S(1)}, f32[1,3,8]{2,0,1:T(1,128)}, u32[]{:S(2)}) copy-start(f32[1,3,8]{2,0,1:T(1,128)} %param.8) | copy-start | bytes 292
  0.7 11.1 %copy-start.4 = (s32[16]{0:T(128)S(1)}, s32[16]{0:T(128)}, u32[]{:S(2)}) copy-start(s32[16]{0:T(128)} %rve_element.1) | copy-start | bytes 196
  0.7 11.1 %copy-start.2 = (s32[2,8,8]{2,1,0:T(8,128)S(1)}, s32[2,8,8]{2,1,0:T(8,128)}, u32[]{:S(2)}) copy-start(s32[2,8,8]{2,1,0:T(8,128)} %slot_hbm.1) | copy-start | bytes 1540
  2.7 15.4 %copy-start.3 = (s32[2,8]{1,0:T(2,128)S(1)}, s32[2,8]{1,0:T(2,128)}, u32[]{:S(2)}) copy-start(s32[2,8]{1,0:T(2,128)} %connectivity.1) | copy-start | bytes 196
  2.7 9.0 %collective-permute-start = (f32[384,128]{1,0:T(8,128)}, f32[384,128]{1,0:T(8,128)S(1)}, u32[]{:S(2)}, u32[]{:S(2)}) collective-permute-start(f32[384,128]{1,0:T(8,128)} %get-tuple-element.20), channel_id=1, source_target_pairs={{0,1},{1,0},{2,3},{3,2},{4,5},{5,4},{6,7},{7,6},{8,9},{9,8},{10,11... | collective-permute-start | bytes 589832 | tf_op jit(solution)/shard_map/ppermute | solution.py:591
  5.8 12.3 %all-to-all-start = ((f32[16,1,3]{2,1,0:T(1,128)}), f32[16,1,3]{2,1,0:T(1,128)S(1)}, u32[]{:S(2)}, u32[]{:S(2)}) async-start(f32[16,1,3]{2,1,0:T(1,128)} %bitcast.35), calls=%async_computation | async-start | bytes 16384 | tf_op jit(solution)/shard_map/all_to_all | solution.py:602
  26.9 9.7 %all-to-all-start.1 = ((f32[32,1,128]{2,1,0:T(1,128)}), f32[32,1,128]{2,1,0:T(1,128)S(1)}, u32[]{:S(2)}, u32[]{:S(2)}) async-start(f32[32,1,128]{2,1,0:T(1,128)} %bitcast.16), calls=%async_computation.1 | async-start | bytes 32768 | tf_op jit(solution)/shard_map/all_to_all | solution.py:640

commit v7 on v6

--- a/solution.py
+++ b/solution.py
@@ -188,20 +188,19 @@
 SHEAR_MEAN = 121
 
 
-def prepare_kernel(disp_hbm, stiff_hbm, mask_hbm, disp_ref, halo_ref, disp_v, ends_v, mask_v, sems):
+def prepare_kernel(stiff_hbm, mask_hbm, halo_ref, ends_v, mask_v, sems):
     groups = stiff_hbm.shape[0] // (8 * ROWS)
     ends = [pl.ds((groups - 1) * (8 * ROWS), 8 * ROWS), pl.ds(0, 8 * ROWS)]
-    copies = [pltpu.make_async_copy(disp_hbm, disp_v, sems.at[0])]
+    copies = []
     for e in range(2):
         copies += [
-            pltpu.make_async_copy(stiff_hbm.at[ends[e], :], ends_v.at[e], sems.at[1 + 2 * e]),
-            pltpu.make_async_copy(mask_hbm.at[ends[e], :], mask_v.at[e], sems.at[2 + 2 * e]),
+            pltpu.make_async_copy(stiff_hbm.at[ends[e], :], ends_v.at[e], sems.at[2 * e]),
+            pltpu.make_async_copy(mask_hbm.at[ends[e], :], mask_v.at[e], sems.at[2 * e + 1]),
         ]
     for copy in copies:
         copy.start()
     for copy in copies:
         copy.wait()
-    disp_ref[...] = jnp.broadcast_to(disp_v[...], disp_ref.shape)
     row = 0
     for e, first in ((0, 8 - HALO), (1, 0)):
         for field in (ends_v, mask_v):
@@ -332,7 +331,8 @@
     half = lame_ref.shape[0] - 2 * HALO
     elem = rve_element[lax.axis_index("macro")]
     nodes = [connectivity[elem, k] for k in range(8)]
-    moves = [[gathered[n, a] for n in nodes] for a in range(3)]
+    point = lax.axis_index("macro")
+    moves = [[gathered[n ^ point, a] for n in nodes] for a in range(3)]
 
     def dot(c, a):
         result = grads[c, 0] * moves[a][0]
@@ -526,6 +526,17 @@
     hom_ref[...] = means[:, SUMS : SUMS + 6]
 
 
+def gather_by_exchange(x, axis, first):
+    size = lax.axis_size(axis)
+    assert size & (size - 1) == 0
+    while x.shape[0] < size:
+        partner = [(i, i ^ x.shape[0]) for i in range(size)]
+        if 2 * x.shape[0] == size:
+            x = x + 0.0 * first[:1, :1]
+        x = jnp.concatenate([x, lax.ppermute(x, axis, partner)], axis=0)
+    return x
+
+
 def on_device(
     nodal_disp,
     weighted_shape_gradients,
@@ -568,24 +579,20 @@
             transcendentals=0,
         )
 
-    disp, rims = pl.pallas_call(
+    rims = pl.pallas_call(
         prepare_kernel,
-        out_shape=(
-            jax.ShapeDtypeStruct((macro_size, 3), f32),
-            jax.ShapeDtypeStruct((packed, 128), f32),
-        ),
-        in_specs=[hbm] * 3,
-        out_specs=(vmem,) * 2,
+        out_shape=jax.ShapeDtypeStruct((packed, 128), f32),
+        in_specs=[hbm] * 2,
+        out_specs=vmem,
         scratch_shapes=[
-            pltpu.VMEM((1, 3), f32),
             pltpu.VMEM((2, 8 * ROWS, 128), f32),
             pltpu.VMEM((2, 8 * ROWS, 128), jnp.int32),
-            pltpu.SemaphoreType.DMA((5,)),
+            pltpu.SemaphoreType.DMA((4,)),
         ],
         compiler_params=pltpu.CompilerParams(vmem_limit_bytes=56 * mib),
         cost_estimate=cost(10**4, 1),
         name="prepare",
-    )(nodal_disp, flat(stiffness), flat(yielded_mask))
+    )(flat(stiffness), flat(yielded_mask))
 
     if vox_size == 2:
         halo = lax.ppermute(rims, "vox", [(0, 1), (1, 0)])
@@ -599,7 +606,7 @@
             ],
             axis=0,
         )
-    gathered = lax.all_to_all(disp, "macro", split_axis=0, concat_axis=0, tiled=True)
+    gathered = gather_by_exchange(nodal_disp, "macro", halo)
 
     grads = weighted_shape_gradients[0]
     lame, shear, rows = pl.pallas_call(

time: 37.4 us -> 41 us (1.096)
  starting transfers between devices: 11.5 us -> 14.4 us
  waiting for transfers between devices: 8.94 us -> 7.42 us
  local copies, waits for them, and re-layouts: 0.03 us -> 1.45 us
  between operations: 0.79 us -> 1.39 us
    ppermute x0 -> x4, starting transfers between devices: none -> 6.11 us  [gather_by_exchange(): x = jnp.concatenate([x, lax.ppermute(x, axis, partner)], axis=0)]
    all_to_all x1 -> x0, starting transfers between devices: 5.91 us -> none  [on_device(): lax.all_to_all(disp, 'macro', split_axis=0, concat_axis=0, tiled=True)]
    all_to_all x1 -> x0, waiting for transfers between devices: 4.55 us -> none  [on_device(): lax.all_to_all(disp, 'macro', split_axis=0, concat_axis=0, tiled=True)]
    all_to_all x1, starting transfers between devices: 2.54 us -> 5.71 us  [on_device(): lax.all_to_all(packet, ('vox', 'macro'), split_axis=0, concat_axis=0, til...]
    ppermute x0 -> x4, waiting for transfers between devices: none -> 2.58 us  [gather_by_exchange(): x = jnp.concatenate([x, lax.ppermute(x, axis, partner)], axis=0)]
    unnamed x13 -> x14, local copies, waits for them, and re-layouts: 0.03 us -> 0.85 us
    slice x0 -> x1, local copies, waits for them, and re-layouts: none -> 0.51 us  [gather_by_exchange(): x = x + 0.0 * first[:1, :1]]
    ppermute x1, waiting for transfers between devices: 0.01 us -> 0.46 us  [on_device(): halo = lax.ppermute(rims, 'vox', [(0, 1), (1, 0)])]
  transfers between devices with their start and end apart: 3 -> 6, of which waited for: 2 -> 5; matrix products, arithmetic and copies ran while one was open for 0% -> 2% of each run, Pallas kernels for 12% -> 16%
where the time goes in v7:
time: 41 us; the launch traced here: 40.8 us
  Pallas kernels  15.8 us (39%)
  starting transfers between devices  14.4 us (35%)
  waiting for transfers between devices  7.42 us (18%)
  local copies, waits for them, and re-layouts  1.45 us (4%)
  between operations  1.39 us (3%)
    pallas_call x1, Pallas kernels, on_device(): pl.pallas_call(sweep_kernel, out_shape=(last_layer, last_layer, last_laye...  8.76 us
    ppermute x4, starting transfers between devices, gather_by_exchange(): x = jnp.concatenate([x, lax.ppermute(x, axis, partner)], axis=0)  6.11 us
    all_to_all x1, starting transfers between devices, on_device(): lax.all_to_all(packet, ('vox', 'macro'), split_axis=0, concat_axis=0, til...  5.71 us
    all_to_all x1, waiting for transfers between devices, on_device(): lax.all_to_all(packet, ('vox', 'macro'), split_axis=0, concat_axis=0, til...  4.39 us
    pallas_call x1, Pallas kernels, on_device(): pl.pallas_call(stress_kernel, out_shape=jax.ShapeDtypeStruct((6, planes *...  2.74 us
    ppermute x1, starting transfers between devices, on_device(): halo = lax.ppermute(rims, 'vox', [(0, 1), (1, 0)])  2.58 us
    ppermute x4, waiting for transfers between devices, gather_by_exchange(): x = jnp.concatenate([x, lax.ppermute(x, axis, partner)], axis=0)  2.58 us
    pallas_call x1, Pallas kernels, on_device(): pl.pallas_call(prepare_kernel, out_shape=jax.ShapeDtypeStruct((packed, 12...  1.92 us
  transfers between devices with their start and end apart: 6, of which 5 were waited for; matrix products, arithmetic and copies ran while one was open for 2% of the time, Pallas kernels for 16%

profile of v7, /device:TPU:0, one launch (start us, length us, event | category | flops | bytes accessed | tf_op | source)
XLA Modules:
  0.0 40.8 jit_solution(5218087435731987165)
XLA Ops:
  0.6 0.0 copy-start.1
  0.6 0.0 copy-start
  0.7 0.0 copy-start.5
  0.7 0.0 copy-start.4
  0.7 0.0 copy-start.2
  0.7 0.8 %copy.15 = f32[1,3]{0,1:T(4,128)S(1)} copy(f32[1,3]{1,0:T(1,128)} %param.7) | data formatting | bytes 24 | tf_op args[0]
  1.5 0.5 %collective-permute-start = (f32[1,3]{0,1:T(4,128)S(1)}, f32[1,3]{0,1:T(4,128)S(1)}, u32[]{:S(2)}, u32[]{:S(2)}) collective-permute-start(f32[1,3]{0,1:T(4,128)S(1)} %copy.15), channel_id=1, source_target_pairs={{0,2},{2,0},{4,6},{6,4},{8,10},{10,8},{12,14},{14,12},{16,18},{18,... | collective-permute-start | bytes 44 | tf_op jit(solution)/shard_map/ppermute | solution.py:536
  2.0 1.9 %prepare.1 = f32[384,128]{1,0:T(8,128)} custom-call(f32[1024,128]{1,0:T(8,128)} %bitcast.26, s32[1024,128]{1,0:T(8,128)} %bitcast.28), custom_call_target="tpu_custom_call" | custom-call | flops 1310720000 | bytes 131072 | tf_op jit(solution)/shard_map/prepare/pallas_call | solution.py:582
  3.9 0.0 copy-start.3
  3.9 2.6 %collective-permute-start.3 = (f32[384,128]{1,0:T(8,128)}, f32[384,128]{1,0:T(8,128)S(1)}, u32[]{:S(2)}, u32[]{:S(2)}) collective-permute-start(f32[384,128]{1,0:T(8,128)} %prepare.1), channel_id=1, source_target_pairs={{0,1},{1,0},{2,3},{3,2},{4,5},{5,4},{6,7},{7,6},{8,9},{9,8},{10,11... | collective-permute-start | bytes 589832 | tf_op jit(solution)/shard_map/ppermute | solution.py:598
  6.5 0.0 copy-done.5
  6.5 0.0 collective-permute-done
  6.5 0.1 pad_maximum_fusion
  6.6 1.5 %collective-permute-start.1 = (f32[2,3]{0,1:T(4,128)S(1)}, f32[2,3]{0,1:T(4,128)S(1)}, u32[]{:S(2)}, u32[]{:S(2)}) collective-permute-start(f32[2,3]{0,1:T(4,128)S(1)} %pad_maximum_fusion), channel_id=1, source_target_pairs={{0,4},{2,6},{4,0},{6,2},{8,12},{10,14},{12,8},{14,10},{16,20},{18,... | collective-permute-start | bytes 80 | tf_op jit(solution)/shard_map/ppermute | solution.py:536
  8.1 2.1 %collective-permute-done.1 = f32[2,3]{0,1:T(4,128)S(1)} collective-permute-done((f32[2,3]{0,1:T(4,128)S(1)}, f32[2,3]{0,1:T(4,128)S(1)}, u32[]{:S(2)}, u32[]{:S(2)}) %collective-permute-start.1) | collective-permute-done | bytes 56 | tf_op jit(solution)/shard_map/ppermute | solution.py:536
  10.2 0.1 pad_maximum_fusion.1
  10.2 1.6 %collective-permute-start.2 = (f32[4,3]{0,1:T(4,128)S(1)}, f32[4,3]{0,1:T(4,128)S(1)}, u32[]{:S(2)}, u32[]{:S(2)}) collective-permute-start(f32[4,3]{0,1:T(4,128)S(1)} %pad_maximum_fusion.1), channel_id=1, source_target_pairs={{0,8},{2,10},{4,12},{6,14},{8,0},{10,2},{12,4},{14,6},{16,24},{18,... | collective-permute-start | bytes 152 | tf_op jit(solution)/shard_map/ppermute | solution.py:536
  11.8 0.5 %collective-permute-done.3.halo_ref = f32[384,128]{1,0:T(8,128)S(1)} collective-permute-done((f32[384,128]{1,0:T(8,128)}, f32[384,128]{1,0:T(8,128)S(1)}, u32[]{:S(2)}, u32[]{:S(2)}) %collective-permute-start.3) | collective-permute-done | bytes 196640 | tf_op jit(solution)/shard_map/ppermute | solution.py:598
  12.3 0.5 %slice.4 = f32[1,1]{1,0:T(1,128)} slice(f32[384,128]{1,0:T(8,128)S(1)} %collective-permute-done.3.halo_ref), slice={[0:1], [0:1]} | slice | bytes 8 | tf_op jit(solution)/shard_map/slice | solution.py:535
  13.4 0.4 collective-permute-done.2
  13.8 0.1 maximum_add_fusion
  13.9 2.6 %collective-permute-start.4 = (f32[8,3]{0,1:T(4,128)S(1)}, f32[8,3]{0,1:T(4,128)S(1)}, u32[]{:S(2)}, u32[]{:S(2)}) collective-permute-start(f32[8,3]{0,1:T(4,128)S(1)} %maximum_add_fusion), channel_id=1, source_target_pairs={{0,16},{2,18},{4,20},{6,22},{8,24},{10,26},{12,28},{14,30},{16,0},... | collective-permute-start | bytes 296 | tf_op jit(solution)/shard_map/ppermute | solution.py:536
  16.5 0.0 copy-done.1
  16.5 0.0 copy-done
  16.5 0.0 copy-done.4
  16.5 0.0 copy-done.2
  16.5 1.8 %material.1 = (f32[22,32,256]{2,1,0:T(8,128)S(1)}, f32[22,32,256]{2,1,0:T(8,128)S(1)}, f32[8,128]{1,0:T(8,128)S(1)}) custom-call(f32[3,8]{1,0:T(4,128)S(1)} %bitcast.24, s32[16]{0:T(128)S(1)} %copy-done.4, s32[2,8,8]{2,1,0:T(8,128)S(1)} %copy-done.2, f32[1024,128]{1,0:T(8,128)S(1)} %bitcast.27, s32[1024,128]{1,0:T(8,128)S(1)} %bitcast.29, ...), custom_call_target="tpu_custom_call" | custom-call | flops 1310720000 | bytes 131072 | tf_op jit(solution)/shard_map/material/pallas_call | solution.py:612
  18.3 0.1 collective-permute-done.4
  18.4 0.1 pad_maximum_fusion.2
  18.5 0.1 copy.16.gathered
  18.5 0.0 copy-done.3
  18.5 8.8 %sweeps.1 = (f32[17,32,256]{2,1,0:T(8,128)S(1)}, f32[17,32,256]{2,1,0:T(8,128)S(1)}, f32[17,32,256]{2,1,0:T(8,128)S(1)}, f32[1,6]{1,0:T(1,128)}, f32[48,128]{1,0:T(8,128)S(1)}, /*index=5*/f32[32,128]{1,0:T(8,128)}) custom-call(f32[3,8]{1,0:T(4,128)S(1)} %bitcast.25, s32[16]{0:T(128)S(1)} %copy-done.4, s32[2,8]{1,0:T(2,128)S(1)} %copy-done.3, ...), custom_call_target="tpu_custom_call" | custom-call | flops 2621440000 | bytes 131072 | tf_op jit(solution)/shard_map/sweeps/pallas_call | solution.py:629
  27.3 5.7 %all-to-all-start = ((f32[32,1,128]{2,1,0:T(1,128)}), f32[32,1,128]{2,1,0:T(1,128)S(1)}, u32[]{:S(2)}, u32[]{:S(2)}) async-start(f32[32,1,128]{2,1,0:T(1,128)} %bitcast.15), calls=%async_computation | async-start | bytes 32768 | tf_op jit(solution)/shard_map/all_to_all | solution.py:647
  33.0 2.7 %stress.1 = f32[6,1024,128]{2,1,0:T(8,128)} custom-call(f32[48,128]{1,0:T(8,128)S(1)} %get-tuple-element.20.strain_in, f32[22,32,256]{2,1,0:T(8,128)S(1)} %get-tuple-element.17.lame_ref, f32[22,32,256]{2,1,0:T(8,128)S(1)} %get-tuple-element.18.shear_ref, f32[17,32,256]{2,1,0:T(8,128)S(1)} %get-tuple-element.21.w30_ref, ...), custom_call_target="tpu_custom_call" | custom-call | flops 1310720000 | bytes 131072 | tf_op jit(solution)/shard_map/stress/pallas_call | solution.py:651
  35.8 4.4 %all-to-all-done = f32[32,1,128]{2,1,0:T(1,128)S(1)} async-done(((f32[32,1,128]{2,1,0:T(1,128)}), f32[32,1,128]{2,1,0:T(1,128)S(1)}, u32[]{:S(2)}, u32[]{:S(2)}) %all-to-all-start) | async-done | bytes 16416 | tf_op jit(solution)/shard_map/all_to_all | solution.py:647
  40.2 0.6 %nodes.1 = (f32[1,6]{1,0:T(1,128)}, f32[1,3]{1,0:T(1,128)}, f32[1,108]{1,0:T(1,128)}) custom-call(f32[32,128]{1,0:T(8,128)S(1)} %bitcast.23), custom_call_target="tpu_custom_call" | custom-call | tf_op jit(solution)/shard_map/nodes/pallas_call | solution.py:672
  (1 shorter events, 0.0 us)
Async XLA Ops:
  0.6 15.9 %copy-start.1 = (s32[1,32,4096]{2,1,0:T(8,128)S(1)}, s32[1,32,4096]{2,1,0:T(8,128)}, u32[]{:S(2)}) copy-start(s32[1,32,4096]{2,1,0:T(8,128)} %param.13) | copy-start | bytes 1572868
  0.6 15.8 %copy-start = (f32[1,32,4096]{2,1,0:T(8,128)S(1)}, f32[1,32,4096]{2,1,0:T(8,128)}, u32[]{:S(2)}) copy-start(f32[1,32,4096]{2,1,0:T(8,128)} %param.12) | copy-start | bytes 1572868
  0.7 5.8 %copy-start.5 = (f32[1,3,8]{2,0,1:T(1,128)S(1)}, f32[1,3,8]{2,0,1:T(1,128)}, u32[]{:S(2)}) copy-start(f32[1,3,8]{2,0,1:T(1,128)} %param.8) | copy-start | bytes 292
  0.7 15.8 %copy-start.4 = (s32[16]{0:T(128)S(1)}, s32[16]{0:T(128)}, u32[]{:S(2)}) copy-start(s32[16]{0:T(128)} %rve_element.1) | copy-start | bytes 196
  0.7 15.8 %copy-start.2 = (s32[2,8,8]{2,1,0:T(8,128)S(1)}, s32[2,8,8]{2,1,0:T(8,128)}, u32[]{:S(2)}) copy-start(s32[2,8,8]{2,1,0:T(8,128)} %slot_hbm.1) | copy-start | bytes 1540
  1.5 5.0 %collective-permute-start = (f32[1,3]{0,1:T(4,128)S(1)}, f32[1,3]{0,1:T(4,128)S(1)}, u32[]{:S(2)}, u32[]{:S(2)}) collective-permute-start(f32[1,3]{0,1:T(4,128)S(1)} %copy.15), channel_id=1, source_target_pairs={{0,2},{2,0},{4,6},{6,4},{8,10},{10,8},{12,14},{14,12},{16,18},{18,... | collective-permute-start | bytes 44 | tf_op jit(solution)/shard_map/ppermute | solution.py:536
  3.9 14.7 %copy-start.3 = (s32[2,8]{1,0:T(2,128)S(1)}, s32[2,8]{1,0:T(2,128)}, u32[]{:S(2)}) copy-start(s32[2,8]{1,0:T(2,128)} %connectivity.1) | copy-start | bytes 196
  3.9 8.4 %collective-permute-start.3 = (f32[384,128]{1,0:T(8,128)}, f32[384,128]{1,0:T(8,128)S(1)}, u32[]{:S(2)}, u32[]{:S(2)}) collective-permute-start(f32[384,128]{1,0:T(8,128)} %prepare.1), channel_id=1, source_target_pairs={{0,1},{1,0},{2,3},{3,2},{4,5},{5,4},{6,7},{7,6},{8,9},{9,8},{10,11... | collective-permute-start | bytes 589832 | tf_op jit(solution)/shard_map/ppermute | solution.py:598
  6.6 3.6 %collective-permute-start.1 = (f32[2,3]{0,1:T(4,128)S(1)}, f32[2,3]{0,1:T(4,128)S(1)}, u32[]{:S(2)}, u32[]{:S(2)}) collective-permute-start(f32[2,3]{0,1:T(4,128)S(1)} %pad_maximum_fusion), channel_id=1, source_target_pairs={{0,4},{2,6},{4,0},{6,2},{8,12},{10,14},{12,8},{14,10},{16,20},{18,... | collective-permute-start | bytes 80 | tf_op jit(solution)/shard_map/ppermute | solution.py:536
  10.2 3.6 %collective-permute-start.2 = (f32[4,3]{0,1:T(4,128)S(1)}, f32[4,3]{0,1:T(4,128)S(1)}, u32[]{:S(2)}, u32[]{:S(2)}) collective-permute-start(f32[4,3]{0,1:T(4,128)S(1)} %pad_maximum_fusion.1), channel_id=1, source_target_pairs={{0,8},{2,10},{4,12},{6,14},{8,0},{10,2},{12,4},{14,6},{16,24},{18,... | collective-permute-start | bytes 152 | tf_op jit(solution)/shard_map/ppermute | solution.py:536
  13.9 4.5 %collective-permute-start.4 = (f32[8,3]{0,1:T(4,128)S(1)}, f32[8,3]{0,1:T(4,128)S(1)}, u32[]{:S(2)}, u32[]{:S(2)}) collective-permute-start(f32[8,3]{0,1:T(4,128)S(1)} %maximum_add_fusion), channel_id=1, source_target_pairs={{0,16},{2,18},{4,20},{6,22},{8,24},{10,26},{12,28},{14,30},{16,0},... | collective-permute-start | bytes 296 | tf_op jit(solution)/shard_map/ppermute | solution.py:536
  27.3 12.9 %all-to-all-start = ((f32[32,1,128]{2,1,0:T(1,128)}), f32[32,1,128]{2,1,0:T(1,128)S(1)}, u32[]{:S(2)}, u32[]{:S(2)}) async-start(f32[32,1,128]{2,1,0:T(1,128)} %bitcast.15), calls=%async_computation | async-start | bytes 32768 | tf_op jit(solution)/shard_map/all_to_all | solution.py:647

commit v8 on v6

--- a/solution.py
+++ b/solution.py
@@ -79,13 +79,14 @@
     return pltpu.roll(x, 2, 1)
 
 
-def differences(ref, at, jj):
+def differences(ref, lane_ref, at, jj, known):
     here = load(ref, at, jj)
-    return (
-        here - load(ref, at - 1, jj),
-        here - prev_row(ref, at, jj),
-        here - prev_lane(here),
-    )
+    if known:
+        along = load(lane_ref, at, jj)
+    else:
+        along = here - prev_lane(here)
+        lane_ref[spot(at, jj)] = along
+    return here - load(ref, at - 1, jj), here - prev_row(ref, at, jj), along
 
 
 def plane_stress(w_refs, at, lame_ref, shear_ref, lame_at, strain):
@@ -326,6 +327,8 @@
     w20_v,
     w21_v,
     w22_v,
+    dlame_v,
+    dshear_v,
     carry2_v,
     carry3_v,
 ):
@@ -363,8 +366,8 @@
 
     def sweep1(at):
         for jj in range(8):
-            l0, l1, l2 = differences(lame_ref, at, jj)
-            m0, m1, m2 = differences(shear_ref, at, jj)
+            l0, l1, l2 = differences(lame_ref, dlame_v, at, jj, False)
+            m0, m1, m2 = differences(shear_ref, dshear_v, at, jj, False)
             w1_v[0][spot(at, jj)] = (
                 trace1 * l0 + twice1[0] * m0 + (strain1[5] * m1 + strain1[4] * m2)
             )
@@ -391,8 +394,8 @@
         bulk, a0, a1, a2, a3, a4, a5 = (jnp.zeros((8, 128), jnp.float32),) * 7
         for jj in range(8):
             w0, w1, w2 = load3(w3_v, at - HALO, jj)
-            l0, l1, l2 = differences(lame_ref, at, jj)
-            m0, m1, m2 = differences(shear_ref, at, jj)
+            l0, l1, l2 = differences(lame_ref, dlame_v, at, jj, True)
+            m0, m1, m2 = differences(shear_ref, dshear_v, at, jj, True)
             bulk = bulk + (l0 * w0 + l1 * w1 + l2 * w2)
             a0 = a0 + m0 * w0
             a1 = a1 + m1 * w1
@@ -631,7 +634,7 @@
         ),
         in_specs=[smem] * 4 + [vmem] * 3,
         out_specs=(vmem, vmem, vmem, smem, vmem, vmem),
-        scratch_shapes=[beyond] * 3 + [field] * 3 + [carry] * 2,
+        scratch_shapes=[beyond] * 3 + [field] * 5 + [carry] * 2,
         compiler_params=pltpu.CompilerParams(vmem_limit_bytes=12 * mib),
         cost_estimate=cost(2 * 10**4, 1),
         name="sweeps",

time: 37.4 us -> 36.6 us (0.979)
  Pallas kernels: 15.9 us -> 15.1 us
    pallas_call x1, Pallas kernels: 8.76 us -> 7.97 us  [on_device(): pl.pallas_call(sweep_kernel, out_shape=(last_layer, last_layer, last_laye...]
where the time goes in v8:
time: 36.6 us; the launch traced here: 36.4 us
  Pallas kernels  15.1 us (41%)
  starting transfers between devices  11.5 us (31%)
  waiting for transfers between devices  8.94 us (24%)
  between operations  0.79 us (2%)
    pallas_call x1, Pallas kernels, on_device(): pl.pallas_call(sweep_kernel, out_shape=(last_layer, last_layer, last_laye...  7.97 us
    all_to_all x1, starting transfers between devices, on_device(): lax.all_to_all(disp, 'macro', split_axis=0, concat_axis=0, tiled=True)  5.91 us
    all_to_all x1, waiting for transfers between devices, on_device(): lax.all_to_all(disp, 'macro', split_axis=0, concat_axis=0, tiled=True)  4.55 us
    all_to_all x1, waiting for transfers between devices, on_device(): lax.all_to_all(packet, ('vox', 'macro'), split_axis=0, concat_axis=0, til...  4.39 us
    ppermute x1, starting transfers between devices, on_device(): halo = lax.ppermute(rims, 'vox', [(0, 1), (1, 0)])  3.03 us
    pallas_call x1, Pallas kernels, on_device(): pl.pallas_call(stress_kernel, out_shape=jax.ShapeDtypeStruct((6, planes *...  2.74 us
    all_to_all x1, starting transfers between devices, on_device(): lax.all_to_all(packet, ('vox', 'macro'), split_axis=0, concat_axis=0, til...  2.54 us
    pallas_call x1, Pallas kernels, on_device(): pl.pallas_call(prepare_kernel, out_shape=(jax.ShapeDtypeStruct((macro_siz...  2.03 us
  transfers between devices with their start and end apart: 3, of which 2 were waited for; matrix products, arithmetic and copies ran while one was open for 0% of the time, Pallas kernels for 12%

profile of v8, /device:TPU:0, one launch (start us, length us, event | category | flops | bytes accessed | tf_op | source)
XLA Modules:
  0.0 36.4 jit_solution(8847020417251357824)
XLA Ops:
  0.6 0.0 copy-start.1
  0.6 0.0 copy-start
  0.7 0.0 copy-start.5
  0.7 0.0 copy-start.4
  0.7 0.0 copy-start.2
  0.7 2.0 %prepare.1 = (f32[16,3]{1,0:T(8,128)}, f32[384,128]{1,0:T(8,128)}) custom-call(f32[1,3]{1,0:T(1,128)} %disp_hbm.1, f32[1024,128]{1,0:T(8,128)} %bitcast.30, s32[1024,128]{1,0:T(8,128)} %bitcast.32), custom_call_target="tpu_custom_call" | custom-call | flops 1310720000 | bytes 131072 | tf_op jit(solution)/shard_map/prepare/pallas_call | solution.py:574
  2.7 0.0 copy-start.3
  2.7 3.0 %collective-permute-start = (f32[384,128]{1,0:T(8,128)}, f32[384,128]{1,0:T(8,128)S(1)}, u32[]{:S(2)}, u32[]{:S(2)}) collective-permute-start(f32[384,128]{1,0:T(8,128)} %get-tuple-element.20), channel_id=1, source_target_pairs={{0,1},{1,0},{2,3},{3,2},{4,5},{5,4},{6,7},{7,6},{8,9},{9,8},{10,11... | collective-permute-start | bytes 589832 | tf_op jit(solution)/shard_map/ppermute | solution.py:594
  5.8 5.9 %all-to-all-start = ((f32[16,1,3]{2,1,0:T(1,128)}), f32[16,1,3]{2,1,0:T(1,128)S(1)}, u32[]{:S(2)}, u32[]{:S(2)}) async-start(f32[16,1,3]{2,1,0:T(1,128)} %bitcast.35), calls=%async_computation | async-start | bytes 16384 | tf_op jit(solution)/shard_map/all_to_all | solution.py:605
  11.7 0.0 copy-done.5
  11.7 0.0 collective-permute-done.halo_ref
  11.7 0.0 copy-done.1
  11.7 0.0 copy-done
  11.7 0.0 copy-done.4
  11.7 0.0 copy-done.2
  11.8 1.8 %material.1 = (f32[22,32,256]{2,1,0:T(8,128)S(1)}, f32[22,32,256]{2,1,0:T(8,128)S(1)}, f32[8,128]{1,0:T(8,128)S(1)}) custom-call(f32[3,8]{1,0:T(4,128)S(1)} %bitcast.28, s32[16]{0:T(128)S(1)} %copy-done.4, s32[2,8,8]{2,1,0:T(8,128)S(1)} %copy-done.2, f32[1024,128]{1,0:T(8,128)S(1)} %bitcast.31, s32[1024,128]{1,0:T(8,128)S(1)} %bitcast.33, ...), custom_call_target="tpu_custom_call" | custom-call | flops 1310720000 | bytes 131072 | tf_op jit(solution)/shard_map/material/pallas_call | solution.py:608
  13.5 4.5 %all-to-all-done = f32[16,1,3]{2,1,0:T(1,128)S(1)} async-done(((f32[16,1,3]{2,1,0:T(1,128)}), f32[16,1,3]{2,1,0:T(1,128)S(1)}, u32[]{:S(2)}, u32[]{:S(2)}) %all-to-all-start) | async-done | bytes 224 | tf_op jit(solution)/shard_map/all_to_all | solution.py:605
  18.1 0.0 copy-done.3
  18.1 8.0 %sweeps.1 = (f32[17,32,256]{2,1,0:T(8,128)S(1)}, f32[17,32,256]{2,1,0:T(8,128)S(1)}, f32[17,32,256]{2,1,0:T(8,128)S(1)}, f32[1,6]{1,0:T(1,128)}, f32[48,128]{1,0:T(8,128)S(1)}, /*index=5*/f32[32,128]{1,0:T(8,128)}) custom-call(f32[3,8]{1,0:T(4,128)S(1)} %bitcast.29, s32[16]{0:T(128)S(1)} %copy-done.4, s32[2,8]{1,0:T(2,128)S(1)} %copy-done.3, ...), custom_call_target="tpu_custom_call" | custom-call | flops 2621440000 | bytes 131072 | tf_op jit(solution)/shard_map/sweeps/pallas_call | solution.py:625
  26.1 2.5 %all-to-all-start.1 = ((f32[32,1,128]{2,1,0:T(1,128)}), f32[32,1,128]{2,1,0:T(1,128)S(1)}, u32[]{:S(2)}, u32[]{:S(2)}) async-start(f32[32,1,128]{2,1,0:T(1,128)} %bitcast.16), calls=%async_computation.1 | async-start | bytes 32768 | tf_op jit(solution)/shard_map/all_to_all | solution.py:643
  28.6 2.7 %stress.1 = f32[6,1024,128]{2,1,0:T(8,128)} custom-call(f32[48,128]{1,0:T(8,128)S(1)} %get-tuple-element.24.strain_in, f32[22,32,256]{2,1,0:T(8,128)S(1)} %get-tuple-element.21.lame_ref, f32[22,32,256]{2,1,0:T(8,128)S(1)} %get-tuple-element.22.shear_ref, f32[17,32,256]{2,1,0:T(8,128)S(1)} %get-tuple-element.25.w30_ref, ...), custom_call_target="tpu_custom_call" | custom-call | flops 1310720000 | bytes 131072 | tf_op jit(solution)/shard_map/stress/pallas_call | solution.py:647
  31.4 4.4 %all-to-all-done.1 = f32[32,1,128]{2,1,0:T(1,128)S(1)} async-done(((f32[32,1,128]{2,1,0:T(1,128)}), f32[32,1,128]{2,1,0:T(1,128)S(1)}, u32[]{:S(2)}, u32[]{:S(2)}) %all-to-all-start.1) | async-done | bytes 16416 | tf_op jit(solution)/shard_map/all_to_all | solution.py:643
  35.8 0.6 %nodes.1 = (f32[1,6]{1,0:T(1,128)}, f32[1,3]{1,0:T(1,128)}, f32[1,108]{1,0:T(1,128)}) custom-call(f32[32,128]{1,0:T(8,128)S(1)} %bitcast.26), custom_call_target="tpu_custom_call" | custom-call | tf_op jit(solution)/shard_map/nodes/pallas_call | solution.py:668
  (1 shorter events, 0.0 us)
Async XLA Ops:
  0.6 11.1 %copy-start.1 = (s32[1,32,4096]{2,1,0:T(8,128)S(1)}, s32[1,32,4096]{2,1,0:T(8,128)}, u32[]{:S(2)}) copy-start(s32[1,32,4096]{2,1,0:T(8,128)} %param.13) | copy-start | bytes 1572868
  0.6 11.1 %copy-start = (f32[1,32,4096]{2,1,0:T(8,128)S(1)}, f32[1,32,4096]{2,1,0:T(8,128)}, u32[]{:S(2)}) copy-start(f32[1,32,4096]{2,1,0:T(8,128)} %param.12) | copy-start | bytes 1572868
  0.7 11.0 %copy-start.5 = (f32[1,3,8]{2,0,1:T(1,128)S(1)}, f32[1,3,8]{2,0,1:T(1,128)}, u32[]{:S(2)}) copy-start(f32[1,3,8]{2,0,1:T(1,128)} %param.8) | copy-start | bytes 292
  0.7 11.1 %copy-start.4 = (s32[16]{0:T(128)S(1)}, s32[16]{0:T(128)}, u32[]{:S(2)}) copy-start(s32[16]{0:T(128)} %rve_element.1) | copy-start | bytes 196
  0.7 11.1 %copy-start.2 = (s32[2,8,8]{2,1,0:T(8,128)S(1)}, s32[2,8,8]{2,1,0:T(8,128)}, u32[]{:S(2)}) copy-start(s32[2,8,8]{2,1,0:T(8,128)} %slot_hbm.1) | copy-start | bytes 1540
  2.7 15.4 %copy-start.3 = (s32[2,8]{1,0:T(2,128)S(1)}, s32[2,8]{1,0:T(2,128)}, u32[]{:S(2)}) copy-start(s32[2,8]{1,0:T(2,128)} %connectivity.1) | copy-start | bytes 196
  2.7 9.0 %collective-permute-start = (f32[384,128]{1,0:T(8,128)}, f32[384,128]{1,0:T(8,128)S(1)}, u32[]{:S(2)}, u32[]{:S(2)}) collective-permute-start(f32[384,128]{1,0:T(8,128)} %get-tuple-element.20), channel_id=1, source_target_pairs={{0,1},{1,0},{2,3},{3,2},{4,5},{5,4},{6,7},{7,6},{8,9},{9,8},{10,11... | collective-permute-start | bytes 589832 | tf_op jit(solution)/shard_map/ppermute | solution.py:594
  5.8 12.3 %all-to-all-start = ((f32[16,1,3]{2,1,0:T(1,128)}), f32[16,1,3]{2,1,0:T(1,128)S(1)}, u32[]{:S(2)}, u32[]{:S(2)}) async-start(f32[16,1,3]{2,1,0:T(1,128)} %bitcast.35), calls=%async_computation | async-start | bytes 16384 | tf_op jit(solution)/shard_map/all_to_all | solution.py:605
  26.1 9.7 %all-to-all-start.1 = ((f32[32,1,128]{2,1,0:T(1,128)}), f32[32,1,128]{2,1,0:T(1,128)S(1)}, u32[]{:S(2)}, u32[]{:S(2)}) async-start(f32[32,1,128]{2,1,0:T(1,128)} %bitcast.16), calls=%async_computation.1 | async-start | bytes 32768 | tf_op jit(solution)/shard_map/all_to_all | solution.py:643
